TPU v7x, 32 devices: a whole 2x2x4 slice. The times are simulated.
32 devices in a mesh: dp: 16 (over z, y, x), mp: 2 (over core).
Axes of the slice: x: 2, y: 2, z: 4, core: 2. Of those that a mesh axis runs over, the one named last changes fastest.
Arguments:
- preact: float32 [16, 16, 16, 1024], P('dp', None, None, 'mp'), may hold values from -6 to 6
- weights: float32 [512, 9, 1024], P('mp'), may hold values from -0.0625 to 0.0625
- cotangent: float32 [16, 16, 16, 512], P('dp', None, None, 'mp'), may hold values from -24 to 24
Outputs:
- output: float32 [16, 16, 16, 512], P('dp', None, None, 'mp')
- input_grad: float32 [16, 16, 16, 1024], P('dp', None, None, 'mp')
- weight_grad: float32 [512, 9216], P('mp', 'dp')
All inputs are finite; a program needn't handle non-finite values.
Results may differ from a plain program's by a relative error of at most 0.0003.
Values sent between devices are 32-bit elements; how exact they have to be, the bound alone decides.
No kernel may reach another device: no remote copies, remote signals or barrier semaphores. Data moves between devices by JAX's collectives and lax.ppermute only.
A program may use at most 64 MiB of HBM per device.

v0:
```python
import jax
import jax.numpy as jnp
from jax import lax
from jax.sharding import PartitionSpec as P

highest = lax.Precision.HIGHEST
epsilon = 1e-06


def from_partner(x, axis, apart):
    return lax.ppermute(x, axis, [(i, i ^ 1 << apart) for i in range(lax.axis_size(axis))])


def activate(values):
    return 0.5 * values * (1.0 + lax.erf(values * 0.7071067811865476))


def gelu_slope(values):
    return (
        0.5 * (1.0 + lax.erf(values * 0.7071067811865476))
        + values * jnp.exp(-0.5 * values * values) * 0.3989422804014327
    )


def pad_image(values):
    return jnp.pad(values, ((0, 0), (1, 1), (1, 1), (0, 0)))


def convolve_piece(activity, filters):
    extent = activity.shape[1]
    padded = pad_image(activity)
    summed = jnp.zeros(activity.shape[:3] + (filters.shape[0],), jnp.float32)
    for kernel_tap in range(9):
        row_shift, column_shift = divmod(kernel_tap, 3)
        window = padded[:, row_shift : row_shift + extent, column_shift : column_shift + extent, :]
        summed = summed + jnp.einsum(
            "nhwc,oc->nhwo", window, filters[:, kernel_tap, :], precision=highest
        )
    return summed


def weight_piece(activity, upstream):
    extent = activity.shape[1]
    padded = pad_image(activity)
    tap_grads = []
    for kernel_tap in range(9):
        row_shift, column_shift = divmod(kernel_tap, 3)
        window = padded[:, row_shift : row_shift + extent, column_shift : column_shift + extent, :]
        tap_grads.append(jnp.einsum("nhwo,nhwc->oc", upstream, window, precision=highest))
    return jnp.stack(tap_grads, 1)


def input_partial(upstream, filters):
    extent = upstream.shape[1]
    padded = pad_image(upstream)
    summed = jnp.zeros(upstream.shape[:3] + (filters.shape[2],), jnp.float32)
    for kernel_tap in range(9):
        row_shift, column_shift = divmod(kernel_tap, 3)
        window = padded[
            :,
            2 - row_shift : 2 - row_shift + extent,
            2 - column_shift : 2 - column_shift + extent,
            :,
        ]
        summed = summed + jnp.einsum(
            "nhwo,oc->nhwc", window, filters[:, kernel_tap, :], precision=highest
        )
    return summed


def adasum_halving(gradient):
    filter_count = gradient.shape[0]
    groups = lax.axis_size("dp")
    height = groups.bit_length() - 1
    data_index = lax.axis_index("dp")
    breadth = gradient.shape[1] * gradient.shape[2] // groups
    current = gradient.reshape(filter_count, groups, breadth)
    for section in range(height):
        parity = data_index >> section & 1
        paired = current.reshape(filter_count, current.shape[1] // 2, 2, breadth)
        kept_rows = lax.dynamic_slice_in_dim(paired, parity, 1, 2)[:, :, 0]
        sent_rows = lax.dynamic_slice_in_dim(paired, 1 - parity, 1, 2)[:, :, 0]
        partner = from_partner(sent_rows, "dp", section)
        lower = parity == 0
        leading = jnp.where(lower, kept_rows, partner)
        second = jnp.where(lower, partner, kept_rows)
        moments = jnp.stack(
            [jnp.sum(leading * second), jnp.sum(leading * leading), jnp.sum(second * second)]
        )
        for bit_level in range(section + 1):
            moments = moments + from_partner(moments, "dp", bit_level)
        moments = lax.psum(moments, "mp")
        cross = moments[0]
        lead_sq = moments[1]
        second_sq = moments[2]
        current = (1.0 - cross / (2.0 * (lead_sq + epsilon))) * leading + (
            1.0 - cross / (2.0 * (second_sq + epsilon))
        ) * second
    return current.reshape(filter_count, breadth)


def local(preact, weights, cotangent):
    activity = activate(preact)
    positions = preact.shape[0] * preact.shape[1] * preact.shape[2]
    output = convolve_piece(lax.all_gather(activity, "mp", axis=3, tiled=True), weights)
    gradient = weight_piece(lax.all_gather(activity, "mp", axis=3, tiled=True), cotangent)
    partial_sum = input_partial(cotangent, weights)
    input_grad = lax.psum_scatter(partial_sum, "mp", scatter_dimension=3, tiled=True) * gelu_slope(
        preact
    )
    weight_grad = adasum_halving(gradient / float(positions))
    return (output, input_grad, weight_grad)


def solution(mesh):
    in_specs = (P("dp", None, None, "mp"), P("mp", None, None), P("dp", None, None, "mp"))
    out_specs = (P("dp", None, None, "mp"), P("dp", None, None, "mp"), P("mp", "dp"))
    return jax.shard_map(local, mesh=mesh, in_specs=in_specs, out_specs=out_specs, check_vma=False)
```

profile of v0, /device:TPU:0, one launch (start us, length us, event | category | flops | bytes accessed | tf_op | source)
XLA Modules:
  0.0 423.9 jit_solution(16643354898103946618)
XLA Ops:
  7.2 2.4 fusion.37
  9.7 2.5 convolution_add_fusion.7
  12.2 2.8 convolution_add_fusion.6
  15.0 2.3 convolution_add_fusion.5
  23.8 11.2 %reduce-scatter.2.cloned.1.call-done = f32[1,16,16,512]{3,2,1,0:T(8,128)} async-done(((f32[1,16,16,1024]{3,2,1,0:T(8,128)}), f32[1,16,16,512]{3,2,1,0:T(8,128)}) %reduce-scatter.2.cloned.1.call-update) | async-done | bytes 524304 | tf_op jit(solution)/shard_map/reduce_scatter | solution.py:108
  34.9 2.3 fusion.79
  37.2 10.3 %all-gather.2.cloned.1.call-done = f32[1,16,16,1024]{3,2,1,0:T(8,128)} async-done(((f32[1,16,16,512]{3,2,1,0:T(8,128)}), f32[1,16,16,1024]{3,2,1,0:T(8,128)}) %all-gather.2.cloned.1.call-update) | async-done | bytes 1048592 | tf_op jit(solution)/shard_map/all_gather | solution.py:105
  47.6 4.1 fusion.8
  51.7 2.8 fusion.7
  54.5 2.8 fusion.6
  57.3 2.8 fusion.5
  60.1 2.8 fusion.4
  62.9 2.8 fusion.3
  65.7 3.0 fusion.2
  68.8 2.8 fusion.1
  71.6 2.9 fusion
  74.5 4.6 %broadcast_multiply_fusion = f32[256,9,1024]{0,2,1:T(8,128)S(1)} fusion(f32[256,9,1024]{0,2,1:T(8,128)} %fusion), kind=kLoop, calls=%fused_computation.7 | loop fusion | flops 2359296 | bytes 18874368 | tf_op jit(solution)/shard_map/div | solution.py:111
  79.1 3.1 dynamic-slice_bitcast_fusion
  85.8 102.6 %collective-permute-done = f32[256,8,576]{0,2,1:T(8,128)} collective-permute-done((f32[256,8,576]{0,2,1:T(8,128)}, f32[256,8,576]{0,2,1:T(8,128)}, u32[]{:S(2)}, u32[]{:S(2)}) %collective-permute-start) | collective-permute-done | bytes 4718624 | tf_op jit(solution)/shard_map/ppermute | solution.py:11
  188.4 7.3 %multiply_reduce_fusion.2 = (f32[]{:T(128)}, f32[]{:T(128)}, f32[]{:T(128)}, f32[256,8,576]{0,2,1:T(8,128)}, f32[256,8,576]{0,2,1:T(8,128)}) fusion(f32[256,8,576]{0,2,1:T(8,128)} %collective-permute-done, f32[256,8,2,576]{0,3,2,1:T(8,128)} %bitcast.259, s32[]{:T(128)S(6)} %select_n.76, pred[]{:T(512)S(6)} %eq.15), kind=kLoop, calls=%fused_computation.5 | loop fusion | flops 9437181 | bytes 18874384 | tf_op jit(solution)/shard_map/reduce_sum | solution.py:88
  203.2 2.4 psum.28
  209.0 4.4 %multiply_add_fusion = f32[256,8,576]{0,2,1:T(8,128)S(1)} fusion(f32[256,8,576]{0,2,1:T(8,128)} %get-tuple-element.22, f32[256,8,576]{0,2,1:T(8,128)} %get-tuple-element.21, f32[]{:T(128)} %bitcast.72, f32[]{:T(128)} %bitcast.71), kind=kLoop, calls=%fused_computation.2 | loop fusion | flops 3538944 | bytes 14155784 | tf_op jit(solution)/shard_map/add | solution.py:96
  213.4 2.1 copy-done.4
  217.5 51.7 %collective-permute-done.2 = f32[256,4,576]{0,2,1:T(8,128)} collective-permute-done((f32[256,4,576]{0,2,1:T(8,128)S(1)}, f32[256,4,576]{0,2,1:T(8,128)}, u32[]{:S(2)}, u32[]{:S(2)}) %collective-permute-start.2) | collective-permute-done | bytes 2359328 | tf_op jit(solution)/shard_map/ppermute | solution.py:11
  269.1 5.8 %multiply_reduce_fusion.5 = (f32[]{:T(128)}, f32[]{:T(128)}, f32[]{:T(128)}, f32[256,4,576]{0,2,1:T(8,128)}, f32[256,4,576]{0,2,1:T(8,128)}) fusion(f32[256,4,576]{0,2,1:T(8,128)} %collective-permute-done.2, f32[256,4,2,576]{0,3,2,1:T(8,128)} %bitcast.261, s32[]{:T(128)S(6)} %select_n.80, pred[]{:T(512)S(6)} %eq.14), kind=kLoop, calls=%fused_computation.21 | loop fusion | flops 4718589 | bytes 9437201 | tf_op jit(solution)/shard_map/reduce_sum | solution.py:88
  288.0 2.7 psum.29
  294.1 2.7 multiply_add_fusion.1
  299.6 2.3 fusion.39
  301.9 2.3 convolution_add_fusion.15
  304.2 2.3 convolution_add_fusion.14
  306.5 2.3 convolution_add_fusion.13
  308.8 17.5 %collective-permute-done.5 = f32[256,2,576]{0,2,1:T(8,128)} collective-permute-done((f32[256,2,576]{0,2,1:T(8,128)}, f32[256,2,576]{0,2,1:T(8,128)}, u32[]{:S(2)}, u32[]{:S(2)}) %collective-permute-start.5) | collective-permute-done | bytes 1179680 | tf_op jit(solution)/shard_map/ppermute | solution.py:11
  326.2 3.6 multiply_reduce_fusion.8
  346.3 2.3 convolution_add_fusion.12
  348.5 2.5 psum.30
  355.9 2.7 collective-permute-start.9
  358.6 2.3 convolution_add_fusion.11
  360.9 2.3 convolution_add_fusion.10
  363.2 2.3 convolution_add_fusion.9
  365.5 19.4 %collective-permute-done.9 = f32[256,1,576]{0,2,1:T(8,128)S(1)} collective-permute-done((f32[256,1,576]{0,2,1:T(8,128)S(1)}, f32[256,1,576]{0,2,1:T(8,128)S(1)}, u32[]{:S(2)}, u32[]{:S(2)}) %collective-permute-start.9) | collective-permute-done | bytes 589856 | tf_op jit(solution)/shard_map/ppermute | solution.py:11
  385.8 2.1 pad_maximum_fusion.3
  391.4 2.1 fusion.134
  397.0 2.1 fusion.138
  399.8 2.8 collective-permute-done.12
  402.6 2.1 collective-permute-start.13
  404.7 2.4 collective-permute-done.13
  407.1 3.0 fusion.10
  410.1 2.4 psum.31
  (61 shorter events, 65.9 us)
Async XLA Ops:
  7.2 5.0 %copy-start.3 = (f32[1,16,16,256]{3,2,1,0:T(8,128)S(1)}, f32[1,16,16,256]{3,2,1,0:T(8,128)}, u32[]{:S(2)}) copy-start(f32[1,16,16,256]{3,2,1,0:T(8,128)} %param.5) | copy-start | bytes 786436
  7.2 27.8 %reduce-scatter.2.cloned.1.call-start = ((), (), s32[]{:S(2)}) async-start(), calls=%async_computation.2 | async-start | bytes 1572864 | tf_op jit(solution)/shard_map/reduce_scatter | solution.py:108
  9.7 7.7 %copy-start.1 = (f32[256,9,1024]{2,0,1:T(8,128)S(1)}, f32[256,9,1024]{2,0,1:T(8,128)}, u32[]{:S(2)}) copy-start(f32[256,9,1024]{2,0,1:T(8,128)} %param.4) | copy-start | bytes 28311556
  20.4 14.5 %copy-start.5 = (f32[1,16,16,512]{3,2,1,0:T(8,128)S(1)}, f32[1,16,16,512]{3,2,1,0:T(8,128)}, u32[]{:S(2)}) copy-start(f32[1,16,16,512]{3,2,1,0:T(8,128)} %param.3) | copy-start | bytes 1572868
  23.5 24.0 %all-gather.2.cloned.1.call-start = ((), (), s32[]{:S(2)}) async-start(), calls=%async_computation.1 | async-start | bytes 1572864 | tf_op jit(solution)/shard_map/all_gather | solution.py:105
  47.6 4.1 copy-start
  79.1 5.0 %copy-start.2 = (f32[256,9,1024]{0,2,1:T(8,128)}, f32[256,9,1024]{0,2,1:T(8,128)S(1)}, u32[]{:S(2)}) copy-start(f32[256,9,1024]{0,2,1:T(8,128)S(1)} %broadcast_multiply_fusion) | copy-start | bytes 28311556
  84.1 104.3 %collective-permute-start = (f32[256,8,576]{0,2,1:T(8,128)}, f32[256,8,576]{0,2,1:T(8,128)}, u32[]{:S(2)}, u32[]{:S(2)}) collective-permute-start(f32[256,8,576]{0,2,1:T(8,128)} %dynamic-slice_bitcast_fusion), channel_id=1, source_target_pairs={{0,2},{2,0},{4,6},{6,4},{8,10},{10,8},{12,14},{14,12},{16,18},{18,... | collective-permute-start | bytes 14155784 | tf_op jit(solution)/shard_map/ppermute | solution.py:11
  197.7 3.5 collective-permute-start.1
  213.4 2.1 copy-start.4
  215.7 53.5 %collective-permute-start.2 = (f32[256,4,576]{0,2,1:T(8,128)S(1)}, f32[256,4,576]{0,2,1:T(8,128)}, u32[]{:S(2)}, u32[]{:S(2)}) collective-permute-start(f32[256,4,576]{0,2,1:T(8,128)S(1)} %dynamic-slice_bitcast_fusion.1), channel_id=1, source_target_pairs={{0,4},{2,6},{4,0},{6,2},{8,12},{10,14},{12,8},{14,10},{16,20},{18,... | collective-permute-start | bytes 7077896 | tf_op jit(solution)/shard_map/ppermute | solution.py:11
  277.0 3.5 collective-permute-start.3
  282.5 3.5 collective-permute-start.4
  297.9 28.4 %collective-permute-start.5 = (f32[256,2,576]{0,2,1:T(8,128)}, f32[256,2,576]{0,2,1:T(8,128)}, u32[]{:S(2)}, u32[]{:S(2)}) collective-permute-start(f32[256,2,576]{0,2,1:T(8,128)} %dynamic-slice_bitcast_fusion.2), channel_id=1, source_target_pairs={{0,8},{2,10},{4,12},{6,14},{8,0},{10,2},{12,4},{14,6},{16,24},{18,... | collective-permute-start | bytes 3538952 | tf_op jit(solution)/shard_map/ppermute | solution.py:11
  331.8 3.5 collective-permute-start.6
  337.2 3.5 collective-permute-start.7
  342.7 3.5 collective-permute-start.8
  355.9 29.0 %collective-permute-start.9 = (f32[256,1,576]{0,2,1:T(8,128)S(1)}, f32[256,1,576]{0,2,1:T(8,128)S(1)}, u32[]{:S(2)}, u32[]{:S(2)}) collective-permute-start(f32[256,1,576]{0,2,1:T(8,128)S(1)} %constant_dynamic-slice_fusion), channel_id=1, source_target_pairs={{0,16},{2,18},{4,20},{6,22},{8,24},{10,26},{12,28},{14,30},{16,0},... | collective-permute-start | bytes 1769480 | tf_op jit(solution)/shard_map/ppermute | solution.py:11
  387.9 3.5 collective-permute-start.10
  393.5 3.5 collective-permute-start.11
  399.1 3.5 collective-permute-start.12
  402.6 4.4 %collective-permute-start.13 = (f32[3]{0:T(128)S(1)}, f32[3]{0:T(128)S(1)}, u32[]{:S(2)}, u32[]{:S(2)}) collective-permute-start(f32[3]{0:T(128)S(1)} %add.236), channel_id=1, source_target_pairs={{0,16},{2,18},{4,20},{6,22},{8,24},{10,26},{12,28},{14,30},{16,0},... | collective-permute-start | bytes 44 | tf_op jit(solution)/shard_map/ppermute | solution.py:11
Sparse Core Ops, SparseCore 0:
  23.7 11.2 reduce-scatter.1
  37.3 10.1 all-gather.1
where the time goes:
time: 432 us; the launch traced here: 424 us
  waiting for transfers between devices  232 us (54%)
  matrix products  64.3 us (15%)
  other arithmetic  56.1 us (13%)
  between operations  25.1 us (6%)
  starting transfers between devices  25 us (6%)
  local copies, waits for them, and re-layouts  11.1 us (3%)
  blocking collectives  10.1 us (2%)
    ppermute x14, waiting for transfers between devices, from_partner(): lax.ppermute(x, axis, [(i, i ^ 1 << apart) for i in range(lax.axis_size(a...  211 us
    dot_general x9, matrix products, weight_piece(): jnp.einsum('nhwo,nhwc->oc', upstream, window, precision=highest)  26.9 us
    ppermute x14, starting transfers between devices, from_partner(): lax.ppermute(x, axis, [(i, i ^ 1 << apart) for i in range(lax.axis_size(a...  24.7 us
    dot_general x9, matrix products, convolve_piece(): jnp.einsum('nhwc,oc->nhwo', window, filters[:, kernel_tap, :], precision=...  21.2 us
    reduce_sum x4, other arithmetic, adasum_halving(): jnp.sum(leading * second)  17.7 us
    dot_general x9, matrix products, input_partial(): jnp.einsum('nhwo,oc->nhwc', window, filters[:, kernel_tap, :], precision=...  16.2 us
    add x10, other arithmetic, adasum_halving(): moments = moments + from_partner(moments, 'dp', bit_level)  13.9 us
    reduce_scatter x1, waiting for transfers between devices, local(): lax.psum_scatter(partial_sum, 'mp', scatter_dimension=3, tiled=True)  11.2 us
  transfers between devices with their start and end apart: 16, of which 16 were waited for; matrix products, arithmetic and copies ran while one was open for 4% of the time, Pallas kernels for 0%

commit v1 on v0

--- a/solution.py
+++ b/solution.py
@@ -1,10 +1,15 @@
+import functools
+
 import jax
 import jax.numpy as jnp
 from jax import lax
+from jax.experimental import pallas as pl
+from jax.experimental.pallas import tpu as pltpu
 from jax.sharding import PartitionSpec as P
 
 highest = lax.Precision.HIGHEST
 epsilon = 1e-06
+MIB = 1 << 20
 
 
 def from_partner(x, axis, apart):
@@ -99,7 +104,7 @@
     return current.reshape(filter_count, breadth)
 
 
-def local(preact, weights, cotangent):
+def local_any(preact, weights, cotangent):
     activity = activate(preact)
     positions = preact.shape[0] * preact.shape[1] * preact.shape[2]
     output = convolve_piece(lax.all_gather(activity, "mp", axis=3, tiled=True), weights)
@@ -112,6 +117,428 @@
     return (output, input_grad, weight_grad)
 
 
+VMEM = pl.BlockSpec(memory_space=pltpu.VMEM)
+SMEM = pl.BlockSpec(memory_space=pltpu.SMEM)
+
+
+def params(limit):
+    return pltpu.CompilerParams(vmem_limit_bytes=limit * MIB)
+
+
+def split(values):
+    high = values.astype(jnp.bfloat16)
+    low = (values - high.astype(jnp.float32)).astype(jnp.bfloat16)
+    return high, low
+
+
+def dot(left, right, contract):
+    return lax.dot_general(
+        left, right, (contract, ((), ())), preferred_element_type=jnp.float32
+    )
+
+
+def dot3(left, right, contract):
+    lh, ll = left
+    rh, rl = right
+    return dot(lh, rh, contract) + (dot(lh, rl, contract) + dot(ll, rh, contract))
+
+
+def shifted(values, offset, extent):
+    if offset == 0:
+        return values
+    rows = values.shape[0]
+    column = lax.rem(lax.broadcasted_iota(jnp.int32, values.shape, 0), extent)
+    if offset == 1:
+        moved = jnp.concatenate([values[rows - 1 :], values[: rows - 1]], 0)
+        return jnp.where(column >= 1, moved, 0.0)
+    moved = jnp.concatenate([values[1:], values[:1]], 0)
+    return jnp.where(column < extent - 1, moved, 0.0)
+
+
+def aligned(index, size):
+    return pl.ds(pl.multiple_of(index * size, size), size)
+
+
+def prepare_kernel(where_ref, preact_ref, up_ref, act_ref, *message_refs):
+    act_ref[...] = activate(preact_ref[...])
+    member = where_ref[0]
+    channels = message_refs[0].shape[2]
+    for other, message in enumerate(message_refs):
+        target = member ^ other
+        message[0] = act_ref[:, aligned(target >> 1, channels)]
+        message[1] = up_ref[:, aligned(target & 1, channels)]
+
+
+def image_kernel(extent, where_ref, mine_ref, theirs_ref, up_ref, weight_ref,
+                 out_ref, keep_ref, send_ref,
+                 act_high, act_low, up_high, up_low, total, back):
+    step = pl.program_id(0)
+    pixels, channels = mine_ref.shape
+    core = where_ref[1]
+
+    @pl.when(step == 0)
+    def _():
+        for ref in (act_high, act_low):
+            ref[...] = jnp.zeros_like(ref)
+        for part, place in ((mine_ref, core), (theirs_ref, 1 - core)):
+            high, low = split(part[...])
+            act_high[extent : extent + pixels, aligned(place, channels)] = high
+            act_low[extent : extent + pixels, aligned(place, channels)] = low
+        for ref in (up_high, up_low):
+            ref[...] = jnp.zeros_like(ref)
+        for column in range(3):
+            high, low = split(shifted(up_ref[...], column - 1, extent))
+            up_high[column, extent : extent + pixels] = high
+            up_low[column, extent : extent + pixels] = low
+        total[...] = jnp.zeros_like(total)
+        back[...] = jnp.zeros_like(back)
+
+    row, column = step // 3, lax.rem(step, 3)
+    weight = split(weight_ref[0])
+    window = pl.ds(pl.multiple_of(row * extent, extent), pixels)
+    total[column] += dot3((act_high[window, :], act_low[window, :]), weight, ((1,), (1,)))
+    window = pl.ds(pl.multiple_of((2 - row) * extent, extent), pixels)
+    back[...] += dot3((up_high[column, window], up_low[column, window]), weight, ((1,), (0,)))
+
+    @pl.when(step == pl.num_programs(0) - 1)
+    def _():
+        out_ref[...] = (
+            shifted(total[0], 1, extent) + total[1] + shifted(total[2], -1, extent)
+        )
+        keep_ref[...] = back[:, aligned(core, channels)]
+        send_ref[...] = back[:, aligned(1 - core, channels)]
+
+
+def pairs(count):
+    return [(i, j) for i in range(count) for j in range(i, count)]
+
+
+def leaf_kernel(extent, images, where_ref, *refs):
+    messages, swapped = refs[:images], refs[images : 2 * images]
+    leaf_out, gram_ref = refs[2 * images : 2 * images + 2]
+    left, right, leaf, sems = refs[2 * images + 2 :]
+    pixels, filters = messages[0].shape[1:]
+    member, core = where_ref[0], where_ref[1]
+    scale = 1.0 / pixels
+    channels = filters
+
+    for other in range(images):
+        for part, place in ((messages[other][0], core), (swapped[other][...], 1 - core)):
+            high, low = split(part.T)
+            rows = aligned(place, channels)
+            left[other, rows, 0:pixels] = high
+            left[other, rows, pixels : 2 * pixels] = high
+            left[other, rows, 2 * pixels : 3 * pixels] = low
+        for column in range(3):
+            moved = shifted(messages[other][1] * scale, column - 1, extent)
+            for row in range(3):
+                tap = 3 * row + column
+                gap = jnp.zeros((extent, filters), jnp.float32)
+                if row == 0:
+                    placed = jnp.concatenate([moved[extent:], gap], 0)
+                elif row == 2:
+                    placed = jnp.concatenate([gap, moved[: pixels - extent]], 0)
+                else:
+                    placed = moved
+                high, low = split(placed)
+                lanes = slice(tap * filters, (tap + 1) * filters)
+                right[other, 0:pixels, lanes] = high
+                right[other, pixels : 2 * pixels, lanes] = low
+                right[other, 2 * pixels : 3 * pixels, lanes] = high
+
+    def one(other, carry):
+        image = member ^ other
+        product = dot(left[other], right[other], ((1,), (0,)))
+        depth = 2 * channels
+        for tap in range(9):
+            leaf[image, tap * depth : (tap + 1) * depth, :] = product[
+                :, tap * filters : (tap + 1) * filters
+            ]
+        pltpu.make_async_copy(leaf.at[image], leaf_out.at[image], sems.at[other]).start()
+        return carry
+
+    lax.fori_loop(0, images, one, 0)
+
+    def add(chunk, sums):
+        rows = pl.ds(pl.multiple_of(chunk * 8, 8), 8)
+        blocks = [leaf[i, rows, :] for i in range(images)]
+        return tuple(s + blocks[i] * blocks[j] for s, (i, j) in zip(sums, pairs(images)))
+
+    zero = jnp.zeros((8, filters), jnp.float32)
+    sums = lax.fori_loop(0, leaf.shape[1] // 8, add, tuple(zero for _ in pairs(images)))
+    gram_ref[...] = jnp.zeros_like(gram_ref)
+    for at, block in enumerate(sums):
+        gram_ref[at : at + 1, :] = jnp.sum(block, 0, keepdims=True)
+    for other in range(images):
+        pltpu.make_async_copy(
+            leaf.at[member ^ other], leaf_out.at[member ^ other], sems.at[other]
+        ).wait()
+
+
+def factors(cross, lead_sq, second_sq):
+    return (
+        1.0 - cross / (2.0 * (lead_sq + epsilon)),
+        1.0 - cross / (2.0 * (second_sq + epsilon)),
+    )
+
+
+def tree_factors(gram, images):
+    inner = {pair: gram[at : at + 1, :] for at, pair in enumerate(pairs(images))}
+    held = [1.0] * images
+    count, width = images, 1
+    while count > 1:
+        scaled = []
+        for node in range(0, count, 2):
+            scaled += factors(
+                inner[node, node + 1],
+                jnp.maximum(inner[node, node], 0.0),
+                jnp.maximum(inner[node + 1, node + 1], 0.0),
+            )
+        held = [value * scaled[at // width] for at, value in enumerate(held)]
+        merged = {}
+        for i, j in pairs(count // 2):
+            terms = [
+                scaled[2 * i + u] * scaled[2 * j + v] * inner[min(2 * i + u, 2 * j + v), max(2 * i + u, 2 * j + v)]
+                for u in range(2)
+                for v in range(2)
+            ]
+            merged[i, j] = (terms[0] + terms[1]) + (terms[2] + terms[3])
+        inner, count, width = merged, count // 2, 2 * width
+    return held
+
+
+def combine_kernel(images, where_ref, gram_ref, leaf_ref, out_ref):
+    gram = jnp.sum(gram_ref[...], 1, keepdims=True)
+    held = tree_factors(gram, images)
+    total = held[0] * leaf_ref[0]
+    for image in range(1, images):
+        total = total + held[image] * leaf_ref[image]
+    out_ref[...] = total
+
+
+def first_unit(target, part):
+    low = 2 * part
+    return jnp.where(low >= target, 2 * target, jnp.where(low + 1 >= target, 2 * target + 1, 2 * target + 2))
+
+
+def pack(member, source_ref, message_refs, unit, start):
+    for other, message in enumerate(message_refs):
+        target = member ^ other
+        first = first_unit(target, member >> 1)
+        rows = message.shape[0] - start
+        message[start:, :] = source_ref[pl.ds(pl.multiple_of(first * unit, unit), rows), :]
+
+
+def pack_kernel(unit, where_ref, own_ref, *message_refs):
+    pack(where_ref[0], own_ref, message_refs, unit, 0)
+
+
+def moments_kernel(unit, where_ref, own_ref, far_ref, *message_refs):
+    pack(where_ref[0], far_ref, message_refs, unit, 8)
+    lower = where_ref[2] == 0
+    own, far = own_ref[...], far_ref[...]
+    cross = jnp.sum(own * far, 0, keepdims=True)
+    own_sq = jnp.sum(own * own, 0, keepdims=True)
+    far_sq = jnp.sum(far * far, 0, keepdims=True)
+    lead_sq = jnp.where(lower, own_sq, far_sq)
+    second_sq = jnp.where(lower, far_sq, own_sq)
+    rest = jnp.zeros((5, own.shape[1]), jnp.float32)
+    block = jnp.concatenate([cross, lead_sq, second_sq, rest], 0)
+    for message in message_refs:
+        message[0:8, :] = block
+
+
+def finish_kernel(unit, images, where_ref, moments_ref, *refs):
+    own, far = refs[:images], refs[images : 2 * images]
+    out_ref, placed, turned = refs[2 * images :]
+    member, lower = where_ref[0], where_ref[2] == 0
+    moments = jnp.sum(moments_ref[...], 1, keepdims=True)
+    lead, second = factors(moments[0:1], moments[1:2], moments[2:3])
+    own_factor = jnp.where(lower, lead, second)
+    far_factor = jnp.where(lower, second, lead)
+    filters = own[0].shape[1]
+    for other in range(images):
+        rows = own[other].shape[0]
+        placed[member ^ other, 0:rows, :] = own_factor * own[other][...] + far_factor * far[other][8:, :]
+    for place in range(images + 1):
+        kind = (member + place) & (images - 1)
+        part = kind >> 1
+        at = jnp.where(
+            part == member >> 1, 0 if place == 0 else 2 if place == images else 1, kind & 1
+        )
+        rows = pl.ds(pl.multiple_of(at * unit, unit), unit)
+        for half in range(2):
+            turned[place * unit : (place + 1) * unit, half * filters : (half + 1) * filters] = placed[
+                2 * part + half, rows, :
+            ]
+    out_ref[...] = turned[...].T
+
+
+def exchange(x, other):
+    size = lax.axis_size("dp")
+    return lax.ppermute(x, "dp", [(i, i ^ other) for i in range(size)])
+
+
+def swap_cores(x):
+    return lax.ppermute(x, "mp", [(0, 1), (1, 0)])
+
+
+def f32(*shape):
+    return jax.ShapeDtypeStruct(shape, jnp.float32)
+
+
+def local_cube(preact, weights, cotangent):
+    extent, own_channels = preact.shape[2], preact.shape[3]
+    pixels = preact.shape[1] * preact.shape[2]
+    filters, taps, channels = weights.shape
+    images = taps - 1
+    lanes = own_channels // 4
+    unit = channels // lax.axis_size("dp")
+    depth = 2 * lanes * taps
+    half = depth // 2
+    data_index = lax.axis_index("dp")
+    where = jnp.stack([data_index & (images - 1), lax.axis_index("mp"), data_index // images]).astype(jnp.int32)
+
+    before = preact.reshape(pixels, own_channels)
+    upstream = cotangent.reshape(pixels, filters)
+    activity, *sent = pl.pallas_call(
+        prepare_kernel,
+        in_specs=[SMEM, VMEM, VMEM],
+        out_specs=[VMEM] * (1 + images),
+        out_shape=[f32(pixels, own_channels)] + [f32(2, pixels, lanes)] * images,
+        compiler_params=params(32),
+        name="prepare",
+    )(where, before, upstream)
+    messages = [sent[0]] + [exchange(sent[other], other) for other in range(1, images)]
+
+    theirs = swap_cores(activity)
+    tap_weights = weights.transpose(1, 0, 2)
+    output, kept, given = pl.pallas_call(
+        functools.partial(image_kernel, extent),
+        grid=(taps,),
+        in_specs=[SMEM, VMEM, VMEM, VMEM, pl.BlockSpec((1, filters, channels), lambda t: (t, 0, 0))],
+        out_specs=[VMEM] * 3,
+        out_shape=[f32(pixels, filters), f32(pixels, own_channels), f32(pixels, own_channels)],
+        scratch_shapes=[
+            pltpu.VMEM((pixels + 2 * extent, channels), jnp.bfloat16),
+            pltpu.VMEM((pixels + 2 * extent, channels), jnp.bfloat16),
+            pltpu.VMEM((3, pixels + 2 * extent, filters), jnp.bfloat16),
+            pltpu.VMEM((3, pixels + 2 * extent, filters), jnp.bfloat16),
+            pltpu.VMEM((3, pixels, filters), jnp.float32),
+            pltpu.VMEM((pixels, channels), jnp.float32),
+        ],
+        compiler_params=params(40),
+        cost_estimate=pl.CostEstimate(
+            flops=12 * pixels * filters * taps * channels,
+            bytes_accessed=4 * filters * taps * channels,
+            transcendentals=0,
+        ),
+        name="image",
+    )(where, activity, theirs, upstream, tap_weights)
+    input_grad = (kept + swap_cores(given)) * gelu_slope(before)
+
+    swapped = swap_cores(jnp.stack([message[0] for message in messages]))
+    inner_count = len(pairs(images))
+    inner_rows = -(-inner_count // 8) * 8
+    leaves, gram = pl.pallas_call(
+        functools.partial(leaf_kernel, extent, images),
+        in_specs=[SMEM] + [VMEM] * (2 * images),
+        out_specs=[pl.BlockSpec(memory_space=pl.ANY), VMEM],
+        out_shape=[f32(images, depth, lanes), f32(inner_rows, lanes)],
+        scratch_shapes=[
+            pltpu.VMEM((images, 2 * lanes, 3 * pixels), jnp.bfloat16),
+            pltpu.VMEM((images, 3 * pixels, taps * lanes), jnp.bfloat16),
+            pltpu.VMEM((images, depth, lanes), jnp.float32),
+            pltpu.SemaphoreType.DMA((images,)),
+        ],
+        compiler_params=params(48),
+        name="leaf",
+    )(where, *messages, *[swapped[i] for i in range(images)])
+    for bit in range(3):
+        gram = gram + from_partner(gram, "dp", bit)
+    gram = gram + swap_cores(gram)
+
+    def combined(which):
+        step = half // 9
+        return pl.pallas_call(
+            functools.partial(combine_kernel, images),
+            grid_spec=pltpu.PrefetchScalarGridSpec(
+                num_scalar_prefetch=1,
+                grid=(half // step,),
+                in_specs=[
+                    pl.BlockSpec((inner_rows, lanes), lambda i, at: (0, 0)),
+                    pl.BlockSpec(
+                        (images, step, lanes), lambda i, at: (0, at[0] * (half // step) + i, 0)
+                    ),
+                ],
+                out_specs=pl.BlockSpec((step, lanes), lambda i, at: (i, 0)),
+            ),
+            out_shape=f32(half, lanes),
+            compiler_params=params(32),
+            name="combine",
+        )(which.reshape(1), gram, leaves)
+
+    side = where[2]
+    far = exchange(combined(1 - side), images)
+    own = combined(side)
+    counts = [3 if other < 2 else 2 for other in range(images)]
+    own_sent = pl.pallas_call(
+        functools.partial(pack_kernel, unit),
+        in_specs=[SMEM, VMEM],
+        out_specs=[VMEM] * images,
+        out_shape=[f32(count * unit, lanes) for count in counts],
+        compiler_params=params(32),
+        name="pack",
+    )(where, own)
+    own_messages = [own_sent[0]] + [exchange(own_sent[other], other) for other in range(1, images)]
+    far_sent = pl.pallas_call(
+        functools.partial(moments_kernel, unit),
+        in_specs=[SMEM, VMEM, VMEM],
+        out_specs=[VMEM] * images,
+        out_shape=[f32(8 + count * unit, lanes) for count in counts],
+        compiler_params=params(32),
+        name="moments",
+    )(where, own, far)
+    far_messages = [far_sent[0]] + [exchange(far_sent[other], other) for other in range(1, images)]
+    moments = functools.reduce(jnp.add, [message[0:8] for message in far_messages])
+    moments = moments + swap_cores(moments)
+    moments = moments + exchange(moments, images)
+    weight_grad = pl.pallas_call(
+        functools.partial(finish_kernel, unit, images),
+        in_specs=[SMEM] + [VMEM] * (1 + 2 * images),
+        out_specs=VMEM,
+        out_shape=f32(filters, taps * unit),
+        scratch_shapes=[
+            pltpu.VMEM((images, 3 * unit, lanes), jnp.float32),
+            pltpu.VMEM((taps * unit, filters), jnp.float32),
+        ],
+        compiler_params=params(32),
+        name="finish",
+    )(where, moments, *own_messages, *far_messages)
+    return (
+        output.reshape(cotangent.shape),
+        input_grad.reshape(preact.shape),
+        weight_grad,
+    )
+
+
+def local(preact, weights, cotangent):
+    count, rows, extent, channels = preact.shape
+    filters, taps = weights.shape[:2]
+    fits = (
+        count == 1
+        and taps == 9
+        and extent % 16 == 0
+        and lax.axis_size("mp") == 2
+        and lax.axis_size("dp") == 2 * (taps - 1)
+        and channels == 4 * 128
+        and filters == 2 * 128
+    )
+    if fits:
+        return local_cube(preact, weights, cotangent)
+    return local_any(preact, weights, cotangent)
+
+
 def solution(mesh):
     in_specs = (P("dp", None, None, "mp"), P("mp", None, None), P("dp", None, None, "mp"))
     out_specs = (P("dp", None, None, "mp"), P("dp", None, None, "mp"), P("mp", "dp"))

time: 432 us -> 133 us (0.31); the launches traced: 424 us -> 133 us
  waiting for transfers between devices: 232 us -> 44.4 us
  matrix products: 64.3 us -> 0 us
  other arithmetic: 56.1 us -> 1.13 us
  Pallas kernels: 0 us -> 34.6 us
  between operations: 25.1 us -> 0.85 us
  starting transfers between devices: 25 us -> 41.7 us
  blocking collectives: 10.1 us -> 0 us
    ppermute x14 -> x3, waiting for transfers between devices: 211 us -> 8.19 us  [from_partner(): lax.ppermute(x, axis, [(i, i ^ 1 << apart) for i in range(lax.axis_size(a...]
    dot_general x27 -> x0, matrix products: 64.3 us -> none  [the longest x9 26.9 us: weight_piece(): jnp.einsum('nhwo,nhwc->oc', upstream, window, precision=highest)]
    ppermute x0 -> x28, starting transfers between devices: none -> 38.4 us  [the longest x23 37.8 us: exchange(): return lax.ppermute(x, 'dp', [(i, i ^ other) for i in range(size)])]
    ppermute x0 -> x28, waiting for transfers between devices: none -> 36.2 us  [the longest x23 31.7 us: exchange(): return lax.ppermute(x, 'dp', [(i, i ^ other) for i in range(size)])]
    pallas_call x0 -> x8, Pallas kernels: none -> 34.6 us  [the longest x1 15.2 us: local_cube(): pl.pallas_call(functools.partial(leaf_kernel, extent, images), in_specs=[...]
    add x13 -> x7, other arithmetic: 22.7 us -> 0.03 us  [the longest x3 0.01 us: local_cube(): gram = gram + from_partner(gram, 'dp', bit)]
    ppermute x14 -> x3, starting transfers between devices: 24.7 us -> 3.22 us  [from_partner(): lax.ppermute(x, axis, [(i, i ^ 1 << apart) for i in range(lax.axis_size(a...]
    reduce_sum x4 -> x0, other arithmetic: 17.7 us -> none  [adasum_halving(): jnp.sum(leading * second)]
  transfers between devices with their start and end apart: 16 -> 31, of which waited for: 16 -> 16; matrix products, arithmetic and copies ran while one was open for 4% -> 1% of each run, Pallas kernels for 0% -> 25%
where the time goes in v1:
time: 133 us
  waiting for transfers between devices  44.4 us (33%)
  starting transfers between devices  41.7 us (31%)
  Pallas kernels  34.6 us (26%)
  local copies, waits for them, and re-layouts  10.6 us (8%)
    ppermute x23, starting transfers between devices, exchange(): return lax.ppermute(x, 'dp', [(i, i ^ other) for i in range(size)])  37.8 us
    ppermute x23, waiting for transfers between devices, exchange(): return lax.ppermute(x, 'dp', [(i, i ^ other) for i in range(size)])  31.7 us
    pallas_call x1, Pallas kernels, local_cube(): pl.pallas_call(functools.partial(leaf_kernel, extent, images), in_specs=[...  15.2 us
    pallas_call x1, Pallas kernels, local_cube(): pl.pallas_call(functools.partial(image_kernel, extent), grid=(taps,), in_...  11.5 us
    unnamed x26, local copies, waits for them, and re-layouts  10.5 us
    ppermute x3, waiting for transfers between devices, from_partner(): lax.ppermute(x, axis, [(i, i ^ 1 << apart) for i in range(lax.axis_size(a...  8.19 us
    pallas_call x2, Pallas kernels, combined(): pl.pallas_call(functools.partial(combine_kernel, images), grid_spec=pltpu...  4.67 us
    ppermute x5, waiting for transfers between devices, swap_cores(): return lax.ppermute(x, 'mp', [(0, 1), (1, 0)])  4.49 us
  transfers between devices with their start and end apart: 31, of which 16 were waited for; matrix products, arithmetic and copies ran while one was open for 1% of the time, Pallas kernels for 25%

profile of v1, /device:TPU:0, one launch (start us, length us, event | category | flops | bytes accessed | tf_op | source)
XLA Modules:
  0.0 133.2 jit_solution(17755197258216505530)
XLA Ops:
  0.7 1.0 copy-done.1
  1.8 0.9 copy-done.3
  2.7 0.9 prepare.1
  3.6 3.0 %collective-permute-start.2 = (f32[2,256,128]{2,1,0:T(8,128)S(1)}, f32[2,256,128]{2,1,0:T(8,128)S(1)}, u32[]{:S(2)}, u32[]{:S(2)}) collective-permute-start(f32[2,256,128]{2,1,0:T(8,128)S(1)} %get-tuple-element.38), channel_id=1, source_target_pairs={{0,2},{2,0},{4,6},{6,4},{8,10},{10,8},{12,14},{14,12},{16,18},{18,... | collective-permute-start | bytes 786440 | tf_op jit(solution)/shard_map/ppermute | solution.py:379
  6.6 1.5 %collective-permute-start.3 = (f32[2,256,128]{2,1,0:T(8,128)S(1)}, f32[2,256,128]{2,1,0:T(8,128)S(1)}, u32[]{:S(2)}, u32[]{:S(2)}) collective-permute-start(f32[2,256,128]{2,1,0:T(8,128)S(1)} %get-tuple-element.39), channel_id=1, source_target_pairs={{0,4},{2,6},{4,0},{6,2},{8,12},{10,14},{12,8},{14,10},{16,20},{18,... | collective-permute-start | bytes 786440 | tf_op jit(solution)/shard_map/ppermute | solution.py:379
  8.1 2.0 %collective-permute-start.5 = (f32[2,256,128]{2,1,0:T(8,128)S(1)}, f32[2,256,128]{2,1,0:T(8,128)S(1)}, u32[]{:S(2)}, u32[]{:S(2)}) collective-permute-start(f32[2,256,128]{2,1,0:T(8,128)S(1)} %get-tuple-element.41), channel_id=1, source_target_pairs={{0,8},{2,10},{4,12},{6,14},{8,0},{10,2},{12,4},{14,6},{16,24},{18,... | collective-permute-start | bytes 786440 | tf_op jit(solution)/shard_map/ppermute | solution.py:379
  10.2 1.4 %collective-permute-start.6 = (f32[2,256,128]{2,1,0:T(8,128)S(1)}, f32[2,256,128]{2,1,0:T(8,128)S(1)}, u32[]{:S(2)}, u32[]{:S(2)}) collective-permute-start(f32[2,256,128]{2,1,0:T(8,128)S(1)} %get-tuple-element.42), channel_id=1, source_target_pairs={{0,10},{2,8},{4,14},{6,12},{8,2},{10,0},{12,6},{14,4},{16,26},{18,... | collective-permute-start | bytes 786440 | tf_op jit(solution)/shard_map/ppermute | solution.py:379
  11.5 2.2 %collective-permute-done.2.refs_1_ = f32[2,256,128]{2,1,0:T(8,128)S(1)} collective-permute-done((f32[2,256,128]{2,1,0:T(8,128)S(1)}, f32[2,256,128]{2,1,0:T(8,128)S(1)}, u32[]{:S(2)}, u32[]{:S(2)}) %collective-permute-start.2) | collective-permute-done | bytes 262176 | tf_op jit(solution)/shard_map/ppermute | solution.py:379
  13.7 3.1 %collective-permute-start.7 = (f32[2,256,128]{2,1,0:T(8,128)S(1)}, f32[2,256,128]{2,1,0:T(8,128)S(1)}, u32[]{:S(2)}, u32[]{:S(2)}) collective-permute-start(f32[2,256,128]{2,1,0:T(8,128)S(1)} %get-tuple-element.43), channel_id=1, source_target_pairs={{0,12},{2,14},{4,8},{6,10},{8,4},{10,6},{12,0},{14,2},{16,28},{18,... | collective-permute-start | bytes 786440 | tf_op jit(solution)/shard_map/ppermute | solution.py:379
  16.8 1.8 %collective-permute-start.8 = (f32[2,256,128]{2,1,0:T(8,128)S(1)}, f32[2,256,128]{2,1,0:T(8,128)S(1)}, u32[]{:S(2)}, u32[]{:S(2)}) collective-permute-start(f32[2,256,128]{2,1,0:T(8,128)S(1)} %get-tuple-element.44), channel_id=1, source_target_pairs={{0,14},{2,12},{4,10},{6,8},{8,6},{10,4},{12,2},{14,0},{16,30},{18,... | collective-permute-start | bytes 786440 | tf_op jit(solution)/shard_map/ppermute | solution.py:379
  18.7 7.0 %collective-permute-done.4.refs_3_ = f32[2,256,128]{2,1,0:T(8,128)S(1)} collective-permute-done((f32[2,256,128]{2,1,0:T(8,128)S(1)}, f32[2,256,128]{2,1,0:T(8,128)S(1)}, u32[]{:S(2)}, u32[]{:S(2)}) %collective-permute-start.4) | collective-permute-done | bytes 262176 | tf_op jit(solution)/shard_map/ppermute | solution.py:379
  25.8 4.5 %collective-permute-done.7.refs_6_ = f32[2,256,128]{2,1,0:T(8,128)S(1)} collective-permute-done((f32[2,256,128]{2,1,0:T(8,128)S(1)}, f32[2,256,128]{2,1,0:T(8,128)S(1)}, u32[]{:S(2)}, u32[]{:S(2)}) %collective-permute-start.7) | collective-permute-done | bytes 262176 | tf_op jit(solution)/shard_map/ppermute | solution.py:379
  30.3 4.8 %collective-permute-done.8.refs_7_ = f32[2,256,128]{2,1,0:T(8,128)S(1)} collective-permute-done((f32[2,256,128]{2,1,0:T(8,128)S(1)}, f32[2,256,128]{2,1,0:T(8,128)S(1)}, u32[]{:S(2)}, u32[]{:S(2)}) %collective-permute-start.8) | collective-permute-done | bytes 262176 | tf_op jit(solution)/shard_map/ppermute | solution.py:379
  35.7 2.1 %collective-permute-done.9 = f32[8,256,128]{2,1,0:T(8,128)S(1)} collective-permute-done((f32[8,256,128]{2,1,0:T(8,128)S(1)}, f32[8,256,128]{2,1,0:T(8,128)S(1)}, u32[]{:S(2)}, u32[]{:S(2)}) %collective-permute-start.9) | collective-permute-done | bytes 1048608 | tf_op jit(solution)/shard_map/ppermute | solution.py:383
  37.9 15.2 %leaf.1 = (f32[8,2304,128]{2,1,0:T(8,128)}, f32[40,128]{1,0:T(8,128)S(1)}) custom-call(s32[3]{0:T(128)S(1)} %pad_add_fusion.where_ref, f32[2,256,128]{2,1,0:T(8,128)S(1)} %get-tuple-element.37.refs_0_, f32[2,256,128]{2,1,0:T(8,128)S(1)} %collective-permute-done.2.refs_1_, f32[2,256,128]{2,1,0:T(8,128)S(1)} %collective-permute-done.3.refs_2_, ...), custom_call_target="tpu_custom_call" | custom-call | tf_op jit(solution)/shard_map/leaf/pallas_call | solution.py:443
  53.1 1.0 collective-permute-start.10
  54.1 2.9 %collective-permute-done.10 = f32[40,128]{1,0:T(8,128)S(1)} collective-permute-done((f32[40,128]{1,0:T(8,128)S(1)}, f32[40,128]{1,0:T(8,128)S(1)}, u32[]{:S(2)}, u32[]{:S(2)}) %collective-permute-start.10) | collective-permute-done | bytes 20512 | tf_op jit(solution)/shard_map/ppermute | solution.py:16
  57.6 3.1 %collective-permute-done.11 = f32[40,128]{1,0:T(8,128)S(1)} collective-permute-done((f32[40,128]{1,0:T(8,128)S(1)}, f32[40,128]{1,0:T(8,128)S(1)}, u32[]{:S(2)}, u32[]{:S(2)}) %collective-permute-start.11) | collective-permute-done | bytes 20512 | tf_op jit(solution)/shard_map/ppermute | solution.py:16
  60.8 1.6 %collective-permute-start.12 = (f32[40,128]{1,0:T(8,128)S(1)}, f32[40,128]{1,0:T(8,128)S(1)}, u32[]{:S(2)}, u32[]{:S(2)}) collective-permute-start(f32[40,128]{1,0:T(8,128)S(1)} %add.57), channel_id=1, source_target_pairs={{0,8},{2,10},{4,12},{6,14},{8,0},{10,2},{12,4},{14,6},{16,24},{18,... | collective-permute-start | bytes 61448 | tf_op jit(solution)/shard_map/ppermute | solution.py:16
  62.3 2.2 %collective-permute-done.12 = f32[40,128]{1,0:T(8,128)S(1)} collective-permute-done((f32[40,128]{1,0:T(8,128)S(1)}, f32[40,128]{1,0:T(8,128)S(1)}, u32[]{:S(2)}, u32[]{:S(2)}) %collective-permute-start.12) | collective-permute-done | bytes 20512 | tf_op jit(solution)/shard_map/ppermute | solution.py:16
  64.5 1.2 collective-permute-done.13
  65.7 3.7 %copy-done = f32[8,2304,128]{2,1,0:T(8,128)S(1)} copy-done((f32[8,2304,128]{2,1,0:T(8,128)S(1)}, f32[8,2304,128]{2,1,0:T(8,128)}, u32[]{:S(2)}) %copy-start) | copy-done | bytes 9437208
  69.4 2.3 %combine.3 = f32[1152,128]{1,0:T(8,128)S(1)} custom-call(s32[1]{0:T(128)} %bitcast.16.where_ref, f32[40,128]{1,0:T(8,128)S(1)} %add.59.gram_ref, f32[8,2304,128]{2,1,0:T(8,128)S(1)} %copy-done), custom_call_target="tpu_custom_call" | custom-call | tf_op jit(solution)/shard_map/combine/pallas_call | solution.py:463
  71.8 2.7 %collective-permute-start.14 = (f32[1152,128]{1,0:T(8,128)S(1)}, f32[1152,128]{1,0:T(8,128)S(1)}, u32[]{:S(2)}, u32[]{:S(2)}) collective-permute-start(f32[1152,128]{1,0:T(8,128)S(1)} %combine.3), channel_id=1, source_target_pairs={{0,16},{2,18},{4,20},{6,22},{8,24},{10,26},{12,28},{14,30},{16,0},... | collective-permute-start | bytes 1769480 | tf_op jit(solution)/shard_map/ppermute | solution.py:379
  74.4 3.7 %copy-done.5 = f32[256,9,1024]{2,0,1:T(8,128)S(1)} copy-done((f32[256,9,1024]{2,0,1:T(8,128)S(1)}, f32[256,9,1024]{2,0,1:T(8,128)}, u32[]{:S(2)}) %copy-start.5) | copy-done | bytes 9437208
  78.1 11.5 %image.1 = (f32[256,256]{1,0:T(8,128)}, f32[256,512]{1,0:T(8,128)S(1)}, f32[256,512]{1,0:T(8,128)S(1)}) custom-call(s32[3]{0:T(128)S(1)} %pad_add_fusion.where_ref, f32[256,512]{1,0:T(8,128)S(1)} %get-tuple-element.33.mine_ref, f32[256,512]{1,0:T(8,128)S(1)} %collective-permute-done.theirs_ref, f32[256,256]{1,0:T(8,128)S(1)} %bitcast.30, ...), custom_call_target="tpu_custom_call" | custom-call | flops 7247757312 | bytes 9437184 | tf_op jit(solution)/shard_map/image/pallas_call | solution.py:416
  89.6 2.3 %combine.2.own_ref = f32[1152,128]{1,0:T(8,128)S(1)} custom-call(s32[1]{0:T(128)} %bitcast.2.where_ref, f32[40,128]{1,0:T(8,128)S(1)} %add.59.gram_ref, f32[8,2304,128]{2,1,0:T(8,128)S(1)} %bitcast.27), custom_call_target="tpu_custom_call" | custom-call | tf_op jit(solution)/shard_map/combine/pallas_call | solution.py:463
  92.0 8.8 %collective-permute-done.14.far_ref = f32[1152,128]{1,0:T(8,128)S(1)} collective-permute-done((f32[1152,128]{1,0:T(8,128)S(1)}, f32[1152,128]{1,0:T(8,128)S(1)}, u32[]{:S(2)}, u32[]{:S(2)}) %collective-permute-start.14) | collective-permute-done | bytes 589856 | tf_op jit(solution)/shard_map/ppermute | solution.py:379
  100.8 0.8 moments.1
  101.5 0.7 collective-permute-start.16
  102.3 1.7 %collective-permute-start.17 = (f32[136,128]{1,0:T(8,128)S(1)}, f32[136,128]{1,0:T(8,128)S(1)}, u32[]{:S(2)}, u32[]{:S(2)}) collective-permute-start(f32[136,128]{1,0:T(8,128)S(1)} %get-tuple-element.50), channel_id=1, source_target_pairs={{0,6},{2,4},{4,2},{6,0},{8,14},{10,12},{12,10},{14,8},{16,22},{18,... | collective-permute-start | bytes 208904 | tf_op jit(solution)/shard_map/ppermute | solution.py:379
  104.7 1.1 collective-permute-start.15
  106.3 1.6 %collective-permute-start.19 = (f32[136,128]{1,0:T(8,128)S(1)}, f32[136,128]{1,0:T(8,128)S(1)}, u32[]{:S(2)}, u32[]{:S(2)}) collective-permute-start(f32[136,128]{1,0:T(8,128)S(1)} %get-tuple-element.52), channel_id=1, source_target_pairs={{0,10},{2,8},{4,14},{6,12},{8,2},{10,0},{12,6},{14,4},{16,26},{18,... | collective-permute-start | bytes 208904 | tf_op jit(solution)/shard_map/ppermute | solution.py:379
  108.2 1.5 %collective-permute-start.20 = (f32[136,128]{1,0:T(8,128)S(1)}, f32[136,128]{1,0:T(8,128)S(1)}, u32[]{:S(2)}, u32[]{:S(2)}) collective-permute-start(f32[136,128]{1,0:T(8,128)S(1)} %get-tuple-element.53), channel_id=1, source_target_pairs={{0,12},{2,14},{4,8},{6,10},{8,4},{10,6},{12,0},{14,2},{16,28},{18,... | collective-permute-start | bytes 208904 | tf_op jit(solution)/shard_map/ppermute | solution.py:379
  109.7 2.1 %collective-permute-start.21 = (f32[136,128]{1,0:T(8,128)S(1)}, f32[136,128]{1,0:T(8,128)S(1)}, u32[]{:S(2)}, u32[]{:S(2)}) collective-permute-start(f32[136,128]{1,0:T(8,128)S(1)} %get-tuple-element.54), channel_id=1, source_target_pairs={{0,14},{2,12},{4,10},{6,8},{8,6},{10,4},{12,2},{14,0},{16,30},{18,... | collective-permute-start | bytes 208904 | tf_op jit(solution)/shard_map/ppermute | solution.py:379
  112.4 1.1 collective-permute-start.25
  113.6 1.7 %collective-permute-start.26 = (f32[128,128]{1,0:T(8,128)S(1)}, f32[128,128]{1,0:T(8,128)S(1)}, u32[]{:S(2)}, u32[]{:S(2)}) collective-permute-start(f32[128,128]{1,0:T(8,128)S(1)} %get-tuple-element.58), channel_id=1, source_target_pairs={{0,6},{2,4},{4,2},{6,0},{8,14},{10,12},{12,10},{14,8},{16,22},{18,... | collective-permute-start | bytes 196616 | tf_op jit(solution)/shard_map/ppermute | solution.py:379
  115.9 1.2 collective-permute-done.22
  117.1 3.3 %collective-permute-start.23 = (f32[8,128]{1,0:T(8,128)S(1)}, f32[8,128]{1,0:T(8,128)S(1)}, u32[]{:S(2)}, u32[]{:S(2)}) collective-permute-start(f32[8,128]{1,0:T(8,128)S(1)} %add.67), channel_id=1, source_target_pairs={{0,16},{2,18},{4,20},{6,22},{8,24},{10,26},{12,28},{14,30},{16,0},... | collective-permute-start | bytes 12296 | tf_op jit(solution)/shard_map/ppermute | solution.py:379
  120.4 0.9 collective-permute-start.24
  121.6 2.3 %collective-permute-start.28 = (f32[128,128]{1,0:T(8,128)S(1)}, f32[128,128]{1,0:T(8,128)S(1)}, u32[]{:S(2)}, u32[]{:S(2)}) collective-permute-start(f32[128,128]{1,0:T(8,128)S(1)} %get-tuple-element.60), channel_id=1, source_target_pairs={{0,10},{2,8},{4,14},{6,12},{8,2},{10,0},{12,6},{14,4},{16,26},{18,... | collective-permute-start | bytes 196616 | tf_op jit(solution)/shard_map/ppermute | solution.py:379
  123.9 1.2 collective-permute-start.29
  125.0 2.1 %collective-permute-start.30 = (f32[128,128]{1,0:T(8,128)S(1)}, f32[128,128]{1,0:T(8,128)S(1)}, u32[]{:S(2)}, u32[]{:S(2)}) collective-permute-start(f32[128,128]{1,0:T(8,128)S(1)} %get-tuple-element.62), channel_id=1, source_target_pairs={{0,14},{2,12},{4,10},{6,8},{8,6},{10,4},{12,2},{14,0},{16,30},{18,... | collective-permute-start | bytes 196616 | tf_op jit(solution)/shard_map/ppermute | solution.py:379
  127.2 1.0 fusion.4
  128.2 1.4 %collective-permute-done.29.refs_6_ = f32[128,128]{1,0:T(8,128)S(1)} collective-permute-done((f32[128,128]{1,0:T(8,128)S(1)}, f32[128,128]{1,0:T(8,128)S(1)}, u32[]{:S(2)}, u32[]{:S(2)}) %collective-permute-start.29) | collective-permute-done | bytes 65568 | tf_op jit(solution)/shard_map/ppermute | solution.py:379
  129.6 1.5 %collective-permute-done.30.refs_7_ = f32[128,128]{1,0:T(8,128)S(1)} collective-permute-done((f32[128,128]{1,0:T(8,128)S(1)}, f32[128,128]{1,0:T(8,128)S(1)}, u32[]{:S(2)}, u32[]{:S(2)}) %collective-permute-start.30) | collective-permute-done | bytes 65568 | tf_op jit(solution)/shard_map/ppermute | solution.py:379
  131.1 1.0 finish.1
  132.1 1.0 copy.6
  (60 shorter events, 4.7 us)
Async XLA Ops:
  0.7 1.0 copy-start.1
  1.8 0.9 copy-start.3
  2.7 71.7 %copy-start.4 = (f32[1,16,16,256]{3,2,1,0:T(8,128)S(1)}, f32[1,16,16,256]{3,2,1,0:T(8,128)}, u32[]{:S(2)}) copy-start(f32[1,16,16,256]{3,2,1,0:T(8,128)} %param.5) | copy-start | bytes 786436
  3.6 10.1 %collective-permute-start.2 = (f32[2,256,128]{2,1,0:T(8,128)S(1)}, f32[2,256,128]{2,1,0:T(8,128)S(1)}, u32[]{:S(2)}, u32[]{:S(2)}) collective-permute-start(f32[2,256,128]{2,1,0:T(8,128)S(1)} %get-tuple-element.38), channel_id=1, source_target_pairs={{0,2},{2,0},{4,6},{6,4},{8,10},{10,8},{12,14},{14,12},{16,18},{18,... | collective-permute-start | bytes 786440 | tf_op jit(solution)/shard_map/ppermute | solution.py:379
  6.6 10.2 %collective-permute-start.3 = (f32[2,256,128]{2,1,0:T(8,128)S(1)}, f32[2,256,128]{2,1,0:T(8,128)S(1)}, u32[]{:S(2)}, u32[]{:S(2)}) collective-permute-start(f32[2,256,128]{2,1,0:T(8,128)S(1)} %get-tuple-element.39), channel_id=1, source_target_pairs={{0,4},{2,6},{4,0},{6,2},{8,12},{10,14},{12,8},{14,10},{16,20},{18,... | collective-permute-start | bytes 786440 | tf_op jit(solution)/shard_map/ppermute | solution.py:379
  8.1 17.6 %collective-permute-start.4 = (f32[2,256,128]{2,1,0:T(8,128)S(1)}, f32[2,256,128]{2,1,0:T(8,128)S(1)}, u32[]{:S(2)}, u32[]{:S(2)}) collective-permute-start(f32[2,256,128]{2,1,0:T(8,128)S(1)} %get-tuple-element.40), channel_id=1, source_target_pairs={{0,6},{2,4},{4,2},{6,0},{8,14},{10,12},{12,10},{14,8},{16,22},{18,... | collective-permute-start | bytes 786440 | tf_op jit(solution)/shard_map/ppermute | solution.py:379
  8.1 17.6 %collective-permute-start.5 = (f32[2,256,128]{2,1,0:T(8,128)S(1)}, f32[2,256,128]{2,1,0:T(8,128)S(1)}, u32[]{:S(2)}, u32[]{:S(2)}) collective-permute-start(f32[2,256,128]{2,1,0:T(8,128)S(1)} %get-tuple-element.41), channel_id=1, source_target_pairs={{0,8},{2,10},{4,12},{6,14},{8,0},{10,2},{12,4},{14,6},{16,24},{18,... | collective-permute-start | bytes 786440 | tf_op jit(solution)/shard_map/ppermute | solution.py:379
  10.2 15.6 %collective-permute-start.6 = (f32[2,256,128]{2,1,0:T(8,128)S(1)}, f32[2,256,128]{2,1,0:T(8,128)S(1)}, u32[]{:S(2)}, u32[]{:S(2)}) collective-permute-start(f32[2,256,128]{2,1,0:T(8,128)S(1)} %get-tuple-element.42), channel_id=1, source_target_pairs={{0,10},{2,8},{4,14},{6,12},{8,2},{10,0},{12,6},{14,4},{16,26},{18,... | collective-permute-start | bytes 786440 | tf_op jit(solution)/shard_map/ppermute | solution.py:379
  13.7 16.6 %collective-permute-start.7 = (f32[2,256,128]{2,1,0:T(8,128)S(1)}, f32[2,256,128]{2,1,0:T(8,128)S(1)}, u32[]{:S(2)}, u32[]{:S(2)}) collective-permute-start(f32[2,256,128]{2,1,0:T(8,128)S(1)} %get-tuple-element.43), channel_id=1, source_target_pairs={{0,12},{2,14},{4,8},{6,10},{8,4},{10,6},{12,0},{14,2},{16,28},{18,... | collective-permute-start | bytes 786440 | tf_op jit(solution)/shard_map/ppermute | solution.py:379
  16.8 18.3 %collective-permute-start.8 = (f32[2,256,128]{2,1,0:T(8,128)S(1)}, f32[2,256,128]{2,1,0:T(8,128)S(1)}, u32[]{:S(2)}, u32[]{:S(2)}) collective-permute-start(f32[2,256,128]{2,1,0:T(8,128)S(1)} %get-tuple-element.44), channel_id=1, source_target_pairs={{0,14},{2,12},{4,10},{6,8},{8,6},{10,4},{12,2},{14,0},{16,30},{18,... | collective-permute-start | bytes 786440 | tf_op jit(solution)/shard_map/ppermute | solution.py:379
  35.1 2.7 %collective-permute-start.9 = (f32[8,256,128]{2,1,0:T(8,128)S(1)}, f32[8,256,128]{2,1,0:T(8,128)S(1)}, u32[]{:S(2)}, u32[]{:S(2)}) collective-permute-start(f32[8,256,128]{2,1,0:T(8,128)S(1)} %slice_dynamic-update-slice_fusion), channel_id=1, source_target_pairs={{0,1},{1,0},{2,3},{3,2},{4,5},{5,4},{6,7},{7,6},{8,9},{9,8},{10,11... | collective-permute-start | bytes 3145736 | tf_op jit(solution)/shard_map/ppermute | solution.py:383
  35.2 39.2 %collective-permute-start = (f32[256,512]{1,0:T(8,128)S(1)}, f32[256,512]{1,0:T(8,128)S(1)}, u32[]{:S(2)}, u32[]{:S(2)}) collective-permute-start(f32[256,512]{1,0:T(8,128)S(1)} %get-tuple-element.33.mine_ref), channel_id=1, source_target_pairs={{0,1},{1,0},{2,3},{3,2},{4,5},{5,4},{6,7},{7,6},{8,9},{9,8},{10,11... | collective-permute-start | bytes 1572872 | tf_op jit(solution)/shard_map/ppermute | solution.py:383
  53.1 3.8 %collective-permute-start.10 = (f32[40,128]{1,0:T(8,128)S(1)}, f32[40,128]{1,0:T(8,128)S(1)}, u32[]{:S(2)}, u32[]{:S(2)}) collective-permute-start(f32[40,128]{1,0:T(8,128)S(1)} %get-tuple-element.45), channel_id=1, source_target_pairs={{0,2},{2,0},{4,6},{6,4},{8,10},{10,8},{12,14},{14,12},{16,18},{18,... | collective-permute-start | bytes 61448 | tf_op jit(solution)/shard_map/ppermute | solution.py:16
  57.0 3.8 %collective-permute-start.11 = (f32[40,128]{1,0:T(8,128)S(1)}, f32[40,128]{1,0:T(8,128)S(1)}, u32[]{:S(2)}, u32[]{:S(2)}) collective-permute-start(f32[40,128]{1,0:T(8,128)S(1)} %add.56), channel_id=1, source_target_pairs={{0,4},{2,6},{4,0},{6,2},{8,12},{10,14},{12,8},{14,10},{16,20},{18,... | collective-permute-start | bytes 61448 | tf_op jit(solution)/shard_map/ppermute | solution.py:16
  60.8 3.8 %collective-permute-start.12 = (f32[40,128]{1,0:T(8,128)S(1)}, f32[40,128]{1,0:T(8,128)S(1)}, u32[]{:S(2)}, u32[]{:S(2)}) collective-permute-start(f32[40,128]{1,0:T(8,128)S(1)} %add.57), channel_id=1, source_target_pairs={{0,8},{2,10},{4,12},{6,14},{8,0},{10,2},{12,4},{14,6},{16,24},{18,... | collective-permute-start | bytes 61448 | tf_op jit(solution)/shard_map/ppermute | solution.py:16
  64.5 1.2 collective-permute-start.13
  65.7 3.7 %copy-start = (f32[8,2304,128]{2,1,0:T(8,128)S(1)}, f32[8,2304,128]{2,1,0:T(8,128)}, u32[]{:S(2)}) copy-start(f32[8,2304,128]{2,1,0:T(8,128)} %get-tuple-element.46.leaf_ref) | copy-start | bytes 28311556
  69.4 20.2 %slice-start = ((s8[9437184]{0:T(1024)(128)(4,1)}), s8[4194304]{0:T(1024)(128)(4,1)S(1)}, s32[]{:S(2)}) async-start(s8[9437184]{0:T(1024)(128)(4,1)} %bitcast.26), calls=%async_computation | async-start | bytes 8388608
  71.8 29.0 %collective-permute-start.14 = (f32[1152,128]{1,0:T(8,128)S(1)}, f32[1152,128]{1,0:T(8,128)S(1)}, u32[]{:S(2)}, u32[]{:S(2)}) collective-permute-start(f32[1152,128]{1,0:T(8,128)S(1)} %combine.3), channel_id=1, source_target_pairs={{0,16},{2,18},{4,20},{6,22},{8,24},{10,26},{12,28},{14,30},{16,0},... | collective-permute-start | bytes 1769480 | tf_op jit(solution)/shard_map/ppermute | solution.py:379
  74.4 3.7 %copy-start.5 = (f32[256,9,1024]{2,0,1:T(8,128)S(1)}, f32[256,9,1024]{2,0,1:T(8,128)}, u32[]{:S(2)}) copy-start(f32[256,9,1024]{2,0,1:T(8,128)} %param.4) | copy-start | bytes 28311556
  78.1 11.5 %slice-start.1 = ((s8[9437184]{0:T(1024)(128)(4,1)}), s8[4194304]{0:T(1024)(128)(4,1)S(1)}, s32[]{:S(2)}) async-start(s8[9437184]{0:T(1024)(128)(4,1)} %bitcast.26), calls=%async_computation.1 | async-start | bytes 8388608
  78.1 11.5 %slice-start.2 = ((s8[9437184]{0:T(1024)(128)(4,1)}), s8[1048576]{0:T(1024)(128)(4,1)S(1)}, s32[]{:S(2)}) async-start(s8[9437184]{0:T(1024)(128)(4,1)} %bitcast.26), calls=%async_computation.2 | async-start | bytes 2097152
  89.6 37.6 %copy-start.2 = (f32[1,16,16,512]{3,2,1,0:T(8,128)S(1)}, f32[1,16,16,512]{3,2,1,0:T(8,128)}, u32[]{:S(2)}) copy-start(f32[1,16,16,512]{3,2,1,0:T(8,128)} %param.3) | copy-start | bytes 1572868
  89.6 31.7 %collective-permute-start.1 = (f32[256,512]{1,0:T(8,128)S(1)}, f32[256,512]{1,0:T(8,128)S(1)}, u32[]{:S(2)}, u32[]{:S(2)}) collective-permute-start(f32[256,512]{1,0:T(8,128)S(1)} %get-tuple-element.36), channel_id=1, source_target_pairs={{0,1},{1,0},{2,3},{3,2},{4,5},{5,4},{6,7},{7,6},{8,9},{9,8},{10,11... | collective-permute-start | bytes 1572872 | tf_op jit(solution)/shard_map/ppermute | solution.py:383
  101.5 4.8 %collective-permute-start.16 = (f32[136,128]{1,0:T(8,128)S(1)}, f32[136,128]{1,0:T(8,128)S(1)}, u32[]{:S(2)}, u32[]{:S(2)}) collective-permute-start(f32[136,128]{1,0:T(8,128)S(1)} %get-tuple-element.49), channel_id=1, source_target_pairs={{0,4},{2,6},{4,0},{6,2},{8,12},{10,14},{12,8},{14,10},{16,20},{18,... | collective-permute-start | bytes 208904 | tf_op jit(solution)/shard_map/ppermute | solution.py:379
  102.3 6.0 %collective-permute-start.17 = (f32[136,128]{1,0:T(8,128)S(1)}, f32[136,128]{1,0:T(8,128)S(1)}, u32[]{:S(2)}, u32[]{:S(2)}) collective-permute-start(f32[136,128]{1,0:T(8,128)S(1)} %get-tuple-element.50), channel_id=1, source_target_pairs={{0,6},{2,4},{4,2},{6,0},{8,14},{10,12},{12,10},{14,8},{16,22},{18,... | collective-permute-start | bytes 208904 | tf_op jit(solution)/shard_map/ppermute | solution.py:379
  104.0 5.7 %collective-permute-start.18 = (f32[136,128]{1,0:T(8,128)S(1)}, f32[136,128]{1,0:T(8,128)S(1)}, u32[]{:S(2)}, u32[]{:S(2)}) collective-permute-start(f32[136,128]{1,0:T(8,128)S(1)} %get-tuple-element.51), channel_id=1, source_target_pairs={{0,8},{2,10},{4,12},{6,14},{8,0},{10,2},{12,4},{14,6},{16,24},{18,... | collective-permute-start | bytes 208904 | tf_op jit(solution)/shard_map/ppermute | solution.py:379
  104.7 11.1 %collective-permute-start.15 = (f32[200,128]{1,0:T(8,128)S(1)}, f32[200,128]{1,0:T(8,128)S(1)}, u32[]{:S(2)}, u32[]{:S(2)}) collective-permute-start(f32[200,128]{1,0:T(8,128)S(1)} %get-tuple-element.48), channel_id=1, source_target_pairs={{0,2},{2,0},{4,6},{6,4},{8,10},{10,8},{12,14},{14,12},{16,18},{18,... | collective-permute-start | bytes 307208 | tf_op jit(solution)/shard_map/ppermute | solution.py:379
  106.3 6.1 %collective-permute-start.19 = (f32[136,128]{1,0:T(8,128)S(1)}, f32[136,128]{1,0:T(8,128)S(1)}, u32[]{:S(2)}, u32[]{:S(2)}) collective-permute-start(f32[136,128]{1,0:T(8,128)S(1)} %get-tuple-element.52), channel_id=1, source_target_pairs={{0,10},{2,8},{4,14},{6,12},{8,2},{10,0},{12,6},{14,4},{16,26},{18,... | collective-permute-start | bytes 208904 | tf_op jit(solution)/shard_map/ppermute | solution.py:379
  108.2 5.3 %collective-permute-start.20 = (f32[136,128]{1,0:T(8,128)S(1)}, f32[136,128]{1,0:T(8,128)S(1)}, u32[]{:S(2)}, u32[]{:S(2)}) collective-permute-start(f32[136,128]{1,0:T(8,128)S(1)} %get-tuple-element.53), channel_id=1, source_target_pairs={{0,12},{2,14},{4,8},{6,10},{8,4},{10,6},{12,0},{14,2},{16,28},{18,... | collective-permute-start | bytes 208904 | tf_op jit(solution)/shard_map/ppermute | solution.py:379
  109.7 6.1 %collective-permute-start.21 = (f32[136,128]{1,0:T(8,128)S(1)}, f32[136,128]{1,0:T(8,128)S(1)}, u32[]{:S(2)}, u32[]{:S(2)}) collective-permute-start(f32[136,128]{1,0:T(8,128)S(1)} %get-tuple-element.54), channel_id=1, source_target_pairs={{0,14},{2,12},{4,10},{6,8},{8,6},{10,4},{12,2},{14,0},{16,30},{18,... | collective-permute-start | bytes 208904 | tf_op jit(solution)/shard_map/ppermute | solution.py:379
  112.4 9.2 %collective-permute-start.25 = (f32[128,128]{1,0:T(8,128)S(1)}, f32[128,128]{1,0:T(8,128)S(1)}, u32[]{:S(2)}, u32[]{:S(2)}) collective-permute-start(f32[128,128]{1,0:T(8,128)S(1)} %get-tuple-element.57), channel_id=1, source_target_pairs={{0,4},{2,6},{4,0},{6,2},{8,12},{10,14},{12,8},{14,10},{16,20},{18,... | collective-permute-start | bytes 196616 | tf_op jit(solution)/shard_map/ppermute | solution.py:379
  113.6 10.3 %collective-permute-start.26 = (f32[128,128]{1,0:T(8,128)S(1)}, f32[128,128]{1,0:T(8,128)S(1)}, u32[]{:S(2)}, u32[]{:S(2)}) collective-permute-start(f32[128,128]{1,0:T(8,128)S(1)} %get-tuple-element.58), channel_id=1, source_target_pairs={{0,6},{2,4},{4,2},{6,0},{8,14},{10,12},{12,10},{14,8},{16,22},{18,... | collective-permute-start | bytes 196616 | tf_op jit(solution)/shard_map/ppermute | solution.py:379
  115.8 1.2 collective-permute-start.22
  117.1 8.0 %collective-permute-start.23 = (f32[8,128]{1,0:T(8,128)S(1)}, f32[8,128]{1,0:T(8,128)S(1)}, u32[]{:S(2)}, u32[]{:S(2)}) collective-permute-start(f32[8,128]{1,0:T(8,128)S(1)} %add.67), channel_id=1, source_target_pairs={{0,16},{2,18},{4,20},{6,22},{8,24},{10,26},{12,28},{14,30},{16,0},... | collective-permute-start | bytes 12296 | tf_op jit(solution)/shard_map/ppermute | solution.py:379
  120.4 10.8 %collective-permute-start.24 = (f32[192,128]{1,0:T(8,128)S(1)}, f32[192,128]{1,0:T(8,128)S(1)}, u32[]{:S(2)}, u32[]{:S(2)}) collective-permute-start(f32[192,128]{1,0:T(8,128)S(1)} %get-tuple-element.56), channel_id=1, source_target_pairs={{0,2},{2,0},{4,6},{6,4},{8,10},{10,8},{12,14},{14,12},{16,18},{18,... | collective-permute-start | bytes 294920 | tf_op jit(solution)/shard_map/ppermute | solution.py:379
  121.3 6.9 %collective-permute-start.27 = (f32[128,128]{1,0:T(8,128)S(1)}, f32[128,128]{1,0:T(8,128)S(1)}, u32[]{:S(2)}, u32[]{:S(2)}) collective-permute-start(f32[128,128]{1,0:T(8,128)S(1)} %get-tuple-element.59), channel_id=1, source_target_pairs={{0,8},{2,10},{4,12},{6,14},{8,0},{10,2},{12,4},{14,6},{16,24},{18,... | collective-permute-start | bytes 196616 | tf_op jit(solution)/shard_map/ppermute | solution.py:379
  121.6 6.6 %collective-permute-start.28 = (f32[128,128]{1,0:T(8,128)S(1)}, f32[128,128]{1,0:T(8,128)S(1)}, u32[]{:S(2)}, u32[]{:S(2)}) collective-permute-start(f32[128,128]{1,0:T(8,128)S(1)} %get-tuple-element.60), channel_id=1, source_target_pairs={{0,10},{2,8},{4,14},{6,12},{8,2},{10,0},{12,6},{14,4},{16,26},{18,... | collective-permute-start | bytes 196616 | tf_op jit(solution)/shard_map/ppermute | solution.py:379
  123.9 5.8 %collective-permute-start.29 = (f32[128,128]{1,0:T(8,128)S(1)}, f32[128,128]{1,0:T(8,128)S(1)}, u32[]{:S(2)}, u32[]{:S(2)}) collective-permute-start(f32[128,128]{1,0:T(8,128)S(1)} %get-tuple-element.61), channel_id=1, source_target_pairs={{0,12},{2,14},{4,8},{6,10},{8,4},{10,6},{12,0},{14,2},{16,28},{18,... | collective-permute-start | bytes 196616 | tf_op jit(solution)/shard_map/ppermute | solution.py:379
  125.0 6.1 %collective-permute-start.30 = (f32[128,128]{1,0:T(8,128)S(1)}, f32[128,128]{1,0:T(8,128)S(1)}, u32[]{:S(2)}, u32[]{:S(2)}) collective-permute-start(f32[128,128]{1,0:T(8,128)S(1)} %get-tuple-element.62), channel_id=1, source_target_pairs={{0,14},{2,12},{4,10},{6,8},{8,6},{10,4},{12,2},{14,0},{16,30},{18,... | collective-permute-start | bytes 196616 | tf_op jit(solution)/shard_map/ppermute | solution.py:379

commit v2 on v1

--- a/solution.py
+++ b/solution.py
@@ -118,7 +118,6 @@
 
 
 VMEM = pl.BlockSpec(memory_space=pltpu.VMEM)
-SMEM = pl.BlockSpec(memory_space=pltpu.SMEM)
 
 
 def params(limit):
@@ -159,9 +158,14 @@
     return pl.ds(pl.multiple_of(index * size, size), size)
 
 
-def prepare_kernel(where_ref, preact_ref, up_ref, act_ref, *message_refs):
+def place():
+    index = lax.axis_index("dp")
+    return index & 7, index >> 3, lax.axis_index("mp")
+
+
+def prepare_kernel(preact_ref, up_ref, act_ref, *message_refs):
     act_ref[...] = activate(preact_ref[...])
-    member = where_ref[0]
+    member = place()[0]
     channels = message_refs[0].shape[2]
     for other, message in enumerate(message_refs):
         target = member ^ other
@@ -169,21 +173,21 @@
         message[1] = up_ref[:, aligned(target & 1, channels)]
 
 
-def image_kernel(extent, where_ref, mine_ref, theirs_ref, up_ref, weight_ref,
+def image_kernel(extent, mine_ref, theirs_ref, up_ref, weight_ref,
                  out_ref, keep_ref, send_ref,
                  act_high, act_low, up_high, up_low, total, back):
     step = pl.program_id(0)
     pixels, channels = mine_ref.shape
-    core = where_ref[1]
+    core = place()[2]
 
     @pl.when(step == 0)
     def _():
         for ref in (act_high, act_low):
             ref[...] = jnp.zeros_like(ref)
-        for part, place in ((mine_ref, core), (theirs_ref, 1 - core)):
+        for part, at in ((mine_ref, core), (theirs_ref, 1 - core)):
             high, low = split(part[...])
-            act_high[extent : extent + pixels, aligned(place, channels)] = high
-            act_low[extent : extent + pixels, aligned(place, channels)] = low
+            act_high[extent : extent + pixels, aligned(at, channels)] = high
+            act_low[extent : extent + pixels, aligned(at, channels)] = low
         for ref in (up_high, up_low):
             ref[...] = jnp.zeros_like(ref)
         for column in range(3):
@@ -213,27 +217,31 @@
     return [(i, j) for i in range(count) for j in range(i, count)]
 
 
-def leaf_kernel(extent, images, where_ref, *refs):
-    messages, swapped = refs[:images], refs[images : 2 * images]
-    leaf_out, gram_ref = refs[2 * images : 2 * images + 2]
-    left, right, leaf, sems = refs[2 * images + 2 :]
+def leaf_kernel(extent, images, known, others, *refs):
+    count = len(others)
+    messages, swapped = refs[:count], refs[count : 2 * count]
+    refs = refs[2 * count :]
+    if known:
+        products_in, _ = refs[:2]
+        refs = refs[2:]
+    leaf, products_ref, left, right = refs[:4]
     pixels, filters = messages[0].shape[1:]
-    member, core = where_ref[0], where_ref[1]
+    member, _, core = place()
     scale = 1.0 / pixels
     channels = filters
-
-    for other in range(images):
-        for part, place in ((messages[other][0], core), (swapped[other][...], 1 - core)):
+    depth = 2 * channels
+
+    for at, other in enumerate(others):
+        for part, where in ((messages[at][0], core), (swapped[at][...], 1 - core)):
             high, low = split(part.T)
-            rows = aligned(place, channels)
-            left[other, rows, 0:pixels] = high
-            left[other, rows, pixels : 2 * pixels] = high
-            left[other, rows, 2 * pixels : 3 * pixels] = low
+            rows = aligned(where, channels)
+            left[at, rows, 0:pixels] = high
+            left[at, rows, pixels : 2 * pixels] = high
+            left[at, rows, 2 * pixels : 3 * pixels] = low
         for column in range(3):
-            moved = shifted(messages[other][1] * scale, column - 1, extent)
+            moved = shifted(messages[at][1] * scale, column - 1, extent)
+            gap = jnp.zeros((extent, filters), jnp.float32)
             for row in range(3):
-                tap = 3 * row + column
-                gap = jnp.zeros((extent, filters), jnp.float32)
                 if row == 0:
                     placed = jnp.concatenate([moved[extent:], gap], 0)
                 elif row == 2:
@@ -241,38 +249,41 @@
                 else:
                     placed = moved
                 high, low = split(placed)
+                tap = 3 * row + column
                 lanes = slice(tap * filters, (tap + 1) * filters)
-                right[other, 0:pixels, lanes] = high
-                right[other, pixels : 2 * pixels, lanes] = low
-                right[other, 2 * pixels : 3 * pixels, lanes] = high
-
-    def one(other, carry):
+                right[at, 0:pixels, lanes] = high
+                right[at, pixels : 2 * pixels, lanes] = low
+                right[at, 2 * pixels : 3 * pixels, lanes] = high
+        product = dot(left[at], right[at], ((1,), (0,)))
         image = member ^ other
-        product = dot(left[other], right[other], ((1,), (0,)))
-        depth = 2 * channels
         for tap in range(9):
             leaf[image, tap * depth : (tap + 1) * depth, :] = product[
                 :, tap * filters : (tap + 1) * filters
             ]
-        pltpu.make_async_copy(leaf.at[image], leaf_out.at[image], sems.at[other]).start()
-        return carry
-
-    lax.fori_loop(0, images, one, 0)
+
+    fresh = [(i, j) for at, i in enumerate(others) for j in list(known) + list(others[: at + 1])]
+    held = list(known) + list(others)
 
     def add(chunk, sums):
         rows = pl.ds(pl.multiple_of(chunk * 8, 8), 8)
-        blocks = [leaf[i, rows, :] for i in range(images)]
-        return tuple(s + blocks[i] * blocks[j] for s, (i, j) in zip(sums, pairs(images)))
+        blocks = {i: leaf[member ^ i, rows, :] for i in held}
+        return tuple(s + blocks[i] * blocks[j] for s, (i, j) in zip(sums, fresh))
 
     zero = jnp.zeros((8, filters), jnp.float32)
-    sums = lax.fori_loop(0, leaf.shape[1] // 8, add, tuple(zero for _ in pairs(images)))
-    gram_ref[...] = jnp.zeros_like(gram_ref)
-    for at, block in enumerate(sums):
-        gram_ref[at : at + 1, :] = jnp.sum(block, 0, keepdims=True)
-    for other in range(images):
-        pltpu.make_async_copy(
-            leaf.at[member ^ other], leaf_out.at[member ^ other], sems.at[other]
-        ).wait()
+    sums = lax.fori_loop(0, leaf.shape[1] // 8, add, tuple(zero for _ in fresh), unroll=4)
+    table = products_ref if len(held) < images else refs[4]
+    if known:
+        table[...] = products_in[...]
+    else:
+        table[...] = jnp.zeros_like(table)
+    for block, (i, j) in zip(sums, fresh):
+        line = jnp.sum(block, 0, keepdims=True)
+        table[i * images + j : i * images + j + 1, :] = line
+        table[j * images + i : j * images + i + 1, :] = line
+    if len(held) == images:
+        products_ref[...] = jnp.zeros_like(products_ref)
+        for at, (i, j) in enumerate(pairs(images)):
+            products_ref[at : at + 1, :] = table[pl.ds((member ^ i) * images + (member ^ j), 1), :]
 
 
 def factors(cross, lead_sq, second_sq):
@@ -307,13 +318,33 @@
     return held
 
 
-def combine_kernel(images, where_ref, gram_ref, leaf_ref, out_ref):
-    gram = jnp.sum(gram_ref[...], 1, keepdims=True)
-    held = tree_factors(gram, images)
-    total = held[0] * leaf_ref[0]
-    for image in range(1, images):
-        total = total + held[image] * leaf_ref[image]
-    out_ref[...] = total
+def combine(held, leaf_ref, start, out_ref):
+    size = 64
+
+    def some(chunk, carry):
+        at = pl.multiple_of(start + chunk * size, size)
+        total = held[0] * leaf_ref[0, pl.ds(at, size), :]
+        for image in range(1, len(held)):
+            total = total + held[image] * leaf_ref[image, pl.ds(at, size), :]
+        out_ref[pl.ds(pl.multiple_of(chunk * size, size), size), :] = total
+        return carry
+
+    lax.fori_loop(0, out_ref.shape[0] // size, some, 0)
+
+
+def far_kernel(gram_ref, leaf_ref, out_ref):
+    images = leaf_ref.shape[0]
+    held = tree_factors(jnp.sum(gram_ref[...], 1, keepdims=True), images)
+    combine(held, leaf_ref, (1 - place()[1]) * out_ref.shape[0], out_ref)
+
+
+def own_kernel(unit, gram_ref, leaf_ref, out_ref, *message_refs):
+    images = leaf_ref.shape[0]
+    member, cube, _ = place()
+    held = tree_factors(jnp.sum(gram_ref[...], 1, keepdims=True), images)
+    combine(held, leaf_ref, cube * out_ref.shape[0], out_ref)
+    for other, message in zip(EARLY, message_refs):
+        pack(member, out_ref, message, other, unit, 0)
 
 
 def first_unit(target, part):
@@ -321,21 +352,19 @@
     return jnp.where(low >= target, 2 * target, jnp.where(low + 1 >= target, 2 * target + 1, 2 * target + 2))
 
 
-def pack(member, source_ref, message_refs, unit, start):
-    for other, message in enumerate(message_refs):
-        target = member ^ other
-        first = first_unit(target, member >> 1)
-        rows = message.shape[0] - start
-        message[start:, :] = source_ref[pl.ds(pl.multiple_of(first * unit, unit), rows), :]
-
-
-def pack_kernel(unit, where_ref, own_ref, *message_refs):
-    pack(where_ref[0], own_ref, message_refs, unit, 0)
-
-
-def moments_kernel(unit, where_ref, own_ref, far_ref, *message_refs):
-    pack(where_ref[0], far_ref, message_refs, unit, 8)
-    lower = where_ref[2] == 0
+def units(other):
+    return 3 if other < 2 else 2
+
+
+def pack(member, source_ref, message, other, unit, start):
+    first = first_unit(member ^ other, member >> 1)
+    rows = units(other) * unit
+    message[start : start + rows, :] = source_ref[pl.ds(pl.multiple_of(first * unit, unit), rows), :]
+
+
+def moments_kernel(unit, own_ref, far_ref, *message_refs):
+    member, cube, _ = place()
+    lower = cube == 0
     own, far = own_ref[...], far_ref[...]
     cross = jnp.sum(own * far, 0, keepdims=True)
     own_sq = jnp.sum(own * own, 0, keepdims=True)
@@ -344,34 +373,38 @@
     second_sq = jnp.where(lower, far_sq, own_sq)
     rest = jnp.zeros((5, own.shape[1]), jnp.float32)
     block = jnp.concatenate([cross, lead_sq, second_sq, rest], 0)
-    for message in message_refs:
+    for other, message in enumerate(message_refs):
         message[0:8, :] = block
-
-
-def finish_kernel(unit, images, where_ref, moments_ref, *refs):
-    own, far = refs[:images], refs[images : 2 * images]
-    out_ref, placed, turned = refs[2 * images :]
-    member, lower = where_ref[0], where_ref[2] == 0
+        pack(member, far_ref, message, other, unit, 8)
+        if other not in EARLY:
+            pack(member, own_ref, message, other, unit, 8 + units(other) * unit)
+
+
+def finish_kernel(unit, images, moments_ref, *refs):
+    far, own = refs[:images], refs[images:-2]
+    out_ref, placed = refs[-2:]
+    member, cube, _ = place()
+    lower = cube == 0
     moments = jnp.sum(moments_ref[...], 1, keepdims=True)
     lead, second = factors(moments[0:1], moments[1:2], moments[2:3])
     own_factor = jnp.where(lower, lead, second)
     far_factor = jnp.where(lower, second, lead)
-    filters = own[0].shape[1]
+    filters = placed.shape[2]
     for other in range(images):
-        rows = own[other].shape[0]
-        placed[member ^ other, 0:rows, :] = own_factor * own[other][...] + far_factor * far[other][8:, :]
-    for place in range(images + 1):
-        kind = (member + place) & (images - 1)
+        rows = units(other) * unit
+        own_rows = own[EARLY.index(other)][...] if other in EARLY else far[other][8 + rows :, :]
+        placed[member ^ other, 0:rows, :] = own_factor * own_rows + far_factor * far[other][8 : 8 + rows, :]
+    for slot in range(images + 1):
+        kind = (member + slot) & (images - 1)
         part = kind >> 1
         at = jnp.where(
-            part == member >> 1, 0 if place == 0 else 2 if place == images else 1, kind & 1
+            part == member >> 1, 0 if slot == 0 else 2 if slot == images else 1, kind & 1
         )
         rows = pl.ds(pl.multiple_of(at * unit, unit), unit)
         for half in range(2):
-            turned[place * unit : (place + 1) * unit, half * filters : (half + 1) * filters] = placed[
+            out_ref[slot * unit : (slot + 1) * unit, half * filters : (half + 1) * filters] = placed[
                 2 * part + half, rows, :
             ]
-    out_ref[...] = turned[...].T
 
 
 def exchange(x, other):
@@ -385,6 +418,19 @@
 
 def f32(*shape):
     return jax.ShapeDtypeStruct(shape, jnp.float32)
+
+
+ORDER = (1, 6, 2, 5, 4, 3, 7)
+EARLY = (1, 6, 2, 5)
+COST = 10**10
+BATCHES = ((0, 1, 6), (2, 5, 4, 3), (7,))
+
+
+def spread(messages):
+    received = {0: messages[0]}
+    for other in ORDER:
+        received[other] = exchange(messages[other], other)
+    return received
 
 
 def local_cube(preact, weights, cotangent):
@@ -396,27 +442,88 @@
     unit = channels // lax.axis_size("dp")
     depth = 2 * lanes * taps
     half = depth // 2
-    data_index = lax.axis_index("dp")
-    where = jnp.stack([data_index & (images - 1), lax.axis_index("mp"), data_index // images]).astype(jnp.int32)
+
+    small = pl.CostEstimate(flops=1, bytes_accessed=1, transcendentals=0)
 
     before = preact.reshape(pixels, own_channels)
     upstream = cotangent.reshape(pixels, filters)
     activity, *sent = pl.pallas_call(
         prepare_kernel,
-        in_specs=[SMEM, VMEM, VMEM],
+        in_specs=[VMEM, VMEM],
         out_specs=[VMEM] * (1 + images),
         out_shape=[f32(pixels, own_channels)] + [f32(2, pixels, lanes)] * images,
         compiler_params=params(32),
+        cost_estimate=small,
         name="prepare",
-    )(where, before, upstream)
-    messages = [sent[0]] + [exchange(sent[other], other) for other in range(1, images)]
-
-    theirs = swap_cores(activity)
-    tap_weights = weights.transpose(1, 0, 2)
+    )(before, upstream)
+    messages = spread(sent)
+
+    leaves, products = None, None
+    known = ()
+    for batch in BATCHES:
+        last = len(known) + len(batch) == images
+        size = len(batch)
+        if known:
+            arrived, leaves = lax.optimization_barrier(([messages[i] for i in batch], leaves))
+            messages.update(zip(batch, arrived))
+        operands = [messages[i] for i in batch] + [swap_cores(messages[i][0]) for i in batch]
+        aliases = {}
+        if known:
+            aliases = {len(operands) + 1: 0}
+            operands += [products, leaves]
+        scratch = [
+            pltpu.VMEM((size, 2 * lanes, 3 * pixels), jnp.bfloat16),
+            pltpu.VMEM((size, 3 * pixels, taps * lanes), jnp.bfloat16),
+        ]
+        if last:
+            scratch.append(pltpu.VMEM((images * images, lanes), jnp.float32))
+        leaves, products = pl.pallas_call(
+            functools.partial(leaf_kernel, extent, images, known, batch),
+            in_specs=[VMEM] * len(operands),
+            out_specs=[VMEM, VMEM],
+            out_shape=[
+                f32(images, depth, lanes),
+                f32(-(-len(pairs(images)) // 8) * 8 if last else images * images, lanes),
+            ],
+            scratch_shapes=scratch,
+            input_output_aliases=aliases,
+            compiler_params=params(24),
+            cost_estimate=small,
+        name="leaf",
+        )(*operands)
+        known += batch
+    gram = products
+    for bit in range(3):
+        gram = gram + from_partner(gram, "dp", bit)
+    gram = gram + swap_cores(gram)
+
+    piece = pl.pallas_call(
+        far_kernel,
+        in_specs=[VMEM, VMEM],
+        out_specs=VMEM,
+        out_shape=f32(half, lanes),
+        compiler_params=params(24),
+        cost_estimate=small,
+        name="far",
+    )(gram, leaves)
+    far = exchange(piece, images)
+
+    own, *own_sent = pl.pallas_call(
+        functools.partial(own_kernel, unit),
+        in_specs=[VMEM, VMEM],
+        out_specs=[VMEM] * (1 + len(EARLY)),
+        out_shape=[f32(half, lanes)] + [f32(units(other) * unit, lanes) for other in EARLY],
+        compiler_params=params(24),
+        cost_estimate=small,
+        name="own",
+    )(gram, leaves)
+    own_messages = [exchange(message, other) for message, other in zip(own_sent, EARLY)]
+
+    activity, piece = lax.optimization_barrier((activity, piece))
     output, kept, given = pl.pallas_call(
         functools.partial(image_kernel, extent),
         grid=(taps,),
-        in_specs=[SMEM, VMEM, VMEM, VMEM, pl.BlockSpec((1, filters, channels), lambda t: (t, 0, 0))],
+        in_specs=[VMEM, VMEM, VMEM, pl.BlockSpec((1, filters, channels), lambda t: (t, 0, 0))],
         out_specs=[VMEM] * 3,
         out_shape=[f32(pixels, filters), f32(pixels, own_channels), f32(pixels, own_channels)],
         scratch_shapes=[
@@ -427,98 +534,42 @@
             pltpu.VMEM((3, pixels, filters), jnp.float32),
             pltpu.VMEM((pixels, channels), jnp.float32),
         ],
-        compiler_params=params(40),
-        cost_estimate=pl.CostEstimate(
-            flops=12 * pixels * filters * taps * channels,
-            bytes_accessed=4 * filters * taps * channels,
-            transcendentals=0,
-        ),
+        compiler_params=params(44),
+        cost_estimate=pl.CostEstimate(flops=COST, bytes_accessed=1, transcendentals=0),
         name="image",
-    )(where, activity, theirs, upstream, tap_weights)
+    )(activity, swap_cores(activity), upstream, weights.transpose(1, 0, 2))
     input_grad = (kept + swap_cores(given)) * gelu_slope(before)
 
-    swapped = swap_cores(jnp.stack([message[0] for message in messages]))
-    inner_count = len(pairs(images))
-    inner_rows = -(-inner_count // 8) * 8
-    leaves, gram = pl.pallas_call(
-        functools.partial(leaf_kernel, extent, images),
-        in_specs=[SMEM] + [VMEM] * (2 * images),
-        out_specs=[pl.BlockSpec(memory_space=pl.ANY), VMEM],
-        out_shape=[f32(images, depth, lanes), f32(inner_rows, lanes)],
-        scratch_shapes=[
-            pltpu.VMEM((images, 2 * lanes, 3 * pixels), jnp.bfloat16),
-            pltpu.VMEM((images, 3 * pixels, taps * lanes), jnp.bfloat16),
-            pltpu.VMEM((images, depth, lanes), jnp.float32),
-            pltpu.SemaphoreType.DMA((images,)),
-        ],
-        compiler_params=params(48),
-        name="leaf",
-    )(where, *messages, *[swapped[i] for i in range(images)])
-    for bit in range(3):
-        gram = gram + from_partner(gram, "dp", bit)
-    gram = gram + swap_cores(gram)
-
-    def combined(which):
-        step = half // 9
-        return pl.pallas_call(
-            functools.partial(combine_kernel, images),
-            grid_spec=pltpu.PrefetchScalarGridSpec(
-                num_scalar_prefetch=1,
-                grid=(half // step,),
-                in_specs=[
-                    pl.BlockSpec((inner_rows, lanes), lambda i, at: (0, 0)),
-                    pl.BlockSpec(
-                        (images, step, lanes), lambda i, at: (0, at[0] * (half // step) + i, 0)
-                    ),
-                ],
-                out_specs=pl.BlockSpec((step, lanes), lambda i, at: (i, 0)),
-            ),
-            out_shape=f32(half, lanes),
-            compiler_params=params(32),
-            name="combine",
-        )(which.reshape(1), gram, leaves)
-
-    side = where[2]
-    far = exchange(combined(1 - side), images)
-    own = combined(side)
-    counts = [3 if other < 2 else 2 for other in range(images)]
-    own_sent = pl.pallas_call(
-        functools.partial(pack_kernel, unit),
-        in_specs=[SMEM, VMEM],
-        out_specs=[VMEM] * images,
-        out_shape=[f32(count * unit, lanes) for count in counts],
-        compiler_params=params(32),
-        name="pack",
-    )(where, own)
-    own_messages = [own_sent[0]] + [exchange(own_sent[other], other) for other in range(1, images)]
+    far, own_messages = lax.optimization_barrier((far, own_messages))
     far_sent = pl.pallas_call(
         functools.partial(moments_kernel, unit),
-        in_specs=[SMEM, VMEM, VMEM],
+        in_specs=[VMEM, VMEM],
         out_specs=[VMEM] * images,
-        out_shape=[f32(8 + count * unit, lanes) for count in counts],
-        compiler_params=params(32),
+        out_shape=[
+            f32(8 + (1 if other in EARLY else 2) * units(other) * unit, lanes) for other in range(images)
+        ],
+        compiler_params=params(24),
+        cost_estimate=small,
         name="moments",
-    )(where, own, far)
-    far_messages = [far_sent[0]] + [exchange(far_sent[other], other) for other in range(1, images)]
-    moments = functools.reduce(jnp.add, [message[0:8] for message in far_messages])
+    )(own, far)
+    far_messages = spread(far_sent)
+    moments = functools.reduce(jnp.add, [far_messages[i][0:8] for i in range(images)])
     moments = moments + swap_cores(moments)
     moments = moments + exchange(moments, images)
     weight_grad = pl.pallas_call(
         functools.partial(finish_kernel, unit, images),
-        in_specs=[SMEM] + [VMEM] * (1 + 2 * images),
+        in_specs=[VMEM] * (1 + images + len(EARLY)),
         out_specs=VMEM,
-        out_shape=f32(filters, taps * unit),
-        scratch_shapes=[
-            pltpu.VMEM((images, 3 * unit, lanes), jnp.float32),
-            pltpu.VMEM((taps * unit, filters), jnp.float32),
-        ],
-        compiler_params=params(32),
+        out_shape=f32(taps * unit, filters),
+        scratch_shapes=[pltpu.VMEM((images, 3 * unit, lanes), jnp.float32)],
+        compiler_params=params(24),
+        cost_estimate=small,
         name="finish",
-    )(where, moments, *own_messages, *far_messages)
+    )(moments, *[far_messages[i] for i in range(images)], *own_messages)
     return (
         output.reshape(cotangent.shape),
         input_grad.reshape(preact.shape),
-        weight_grad,
+        weight_grad.T,
     )
 
 

time: 133 us -> 109 us (0.82)
  local copies, waits for them, and re-layouts: 10.6 us -> 2.07 us
  Pallas kernels: 34.6 us -> 27.2 us
  waiting for transfers between devices: 44.4 us -> 39.1 us
  starting transfers between devices: 41.7 us -> 38 us
    pallas_call x6 -> x7, Pallas kernels: 22.1 us -> 13.5 us  [the longest x3 10.7 us: local_cube(): pl.pallas_call(functools.partial(leaf_kernel, extent, images, known, batc...]
    unnamed x26 -> x8, local copies, waits for them, and re-layouts: 10.5 us -> 1.99 us
    ppermute x23 -> x20, waiting for transfers between devices: 31.7 us -> 25 us  [exchange(): return lax.ppermute(x, 'dp', [(i, i ^ other) for i in range(size)])]
    ppermute x23 -> x20, starting transfers between devices: 37.8 us -> 31.7 us  [exchange(): return lax.ppermute(x, 'dp', [(i, i ^ other) for i in range(size)])]
    ppermute x5 -> x12, waiting for transfers between devices: 4.49 us -> 6.92 us  [swap_cores(): return lax.ppermute(x, 'mp', [(0, 1), (1, 0)])]
    ppermute x5 -> x12, starting transfers between devices: 0.64 us -> 2 us  [swap_cores(): return lax.ppermute(x, 'mp', [(0, 1), (1, 0)])]
  transfers between devices with their start and end apart: 31 -> 35, of which waited for: 16 -> 19; matrix products, arithmetic and copies ran while one was open for 1% -> 0% of each run, Pallas kernels for 25% -> 22%
where the time goes in v2:
time: 109 us; the launch traced here: 108 us
  waiting for transfers between devices  39.1 us (36%)
  starting transfers between devices  38 us (35%)
  Pallas kernels  27.2 us (25%)
  local copies, waits for them, and re-layouts  2.07 us (2%)
    ppermute x20, starting transfers between devices, exchange(): return lax.ppermute(x, 'dp', [(i, i ^ other) for i in range(size)])  31.7 us
    ppermute x20, waiting for transfers between devices, exchange(): return lax.ppermute(x, 'dp', [(i, i ^ other) for i in range(size)])  25 us
    pallas_call x1, Pallas kernels, local_cube(): pl.pallas_call(functools.partial(image_kernel, extent), grid=(taps,), in_...  12.6 us
    pallas_call x3, Pallas kernels, local_cube(): pl.pallas_call(functools.partial(leaf_kernel, extent, images, known, batc...  10.7 us
    ppermute x3, waiting for transfers between devices, from_partner(): lax.ppermute(x, axis, [(i, i ^ 1 << apart) for i in range(lax.axis_size(a...  7.18 us
    ppermute x12, waiting for transfers between devices, swap_cores(): return lax.ppermute(x, 'mp', [(0, 1), (1, 0)])  6.92 us
    ppermute x3, starting transfers between devices, from_partner(): lax.ppermute(x, axis, [(i, i ^ 1 << apart) for i in range(lax.axis_size(a...  4.24 us
  transfers between devices with their start and end apart: 35, of which 19 were waited for; matrix products, arithmetic and copies ran while one was open for 0% of the time, Pallas kernels for 22%

profile of v2, /device:TPU:0, one launch (start us, length us, event | category | flops | bytes accessed | tf_op | source)
XLA Modules:
  0.0 108.2 jit_solution(4358003694480458722)
XLA Ops:
  0.6 1.0 copy-done
  1.7 0.9 copy-done.2
  3.0 3.0 %collective-permute-start.5 = (f32[2,256,128]{2,1,0:T(8,128)S(1)}, f32[2,256,128]{2,1,0:T(8,128)S(1)}, u32[]{:S(2)}, u32[]{:S(2)}) collective-permute-start(f32[2,256,128]{2,1,0:T(8,128)S(1)} %get-tuple-element.54), channel_id=1, source_target_pairs={{0,2},{2,0},{4,6},{6,4},{8,10},{10,8},{12,14},{14,12},{16,18},{18,... | collective-permute-start | bytes 786440 | tf_op jit(solution)/shard_map/ppermute | solution.py:412
  6.0 2.5 %collective-permute-start.6 = (f32[2,256,128]{2,1,0:T(8,128)S(1)}, f32[2,256,128]{2,1,0:T(8,128)S(1)}, u32[]{:S(2)}, u32[]{:S(2)}) collective-permute-start(f32[2,256,128]{2,1,0:T(8,128)S(1)} %get-tuple-element.55), channel_id=1, source_target_pairs={{0,12},{2,14},{4,8},{6,10},{8,4},{10,6},{12,0},{14,2},{16,28},{18,... | collective-permute-start | bytes 786440 | tf_op jit(solution)/shard_map/ppermute | solution.py:412
  8.6 0.6 collective-permute-start.1
  9.2 3.1 %collective-permute-done.5.refs_1_ = f32[2,256,128]{2,1,0:T(8,128)S(1)} collective-permute-done((f32[2,256,128]{2,1,0:T(8,128)S(1)}, f32[2,256,128]{2,1,0:T(8,128)S(1)}, u32[]{:S(2)}, u32[]{:S(2)}) %collective-permute-start.5) | collective-permute-done | bytes 262176 | tf_op jit(solution)/shard_map/ppermute | solution.py:412
  12.3 1.8 %collective-permute-start.3 = (f32[2,256,128]{2,1,0:T(8,128)S(1)}, f32[2,256,128]{2,1,0:T(8,128)S(1)}, u32[]{:S(2)}, u32[]{:S(2)}) collective-permute-start(f32[2,256,128]{2,1,0:T(8,128)S(1)} %get-tuple-element.51), channel_id=1, source_target_pairs={{0,8},{2,10},{4,12},{6,14},{8,0},{10,2},{12,4},{14,6},{16,24},{18,... | collective-permute-start | bytes 786440 | tf_op jit(solution)/shard_map/ppermute | solution.py:412
  14.1 2.8 %collective-permute-start.4 = (f32[2,256,128]{2,1,0:T(8,128)S(1)}, f32[2,256,128]{2,1,0:T(8,128)S(1)}, u32[]{:S(2)}, u32[]{:S(2)}) collective-permute-start(f32[2,256,128]{2,1,0:T(8,128)S(1)} %get-tuple-element.52), channel_id=1, source_target_pairs={{0,6},{2,4},{4,2},{6,0},{8,14},{10,12},{12,10},{14,8},{16,22},{18,... | collective-permute-start | bytes 786440 | tf_op jit(solution)/shard_map/ppermute | solution.py:412
  17.0 1.3 %collective-permute-done.8.refs_4_ = f32[256,128]{1,0:T(8,128)S(1)} collective-permute-done((f32[256,128]{1,0:T(8,128)S(1)}, f32[256,128]{1,0:T(8,128)S(1)}, u32[]{:S(2)}, u32[]{:S(2)}) %collective-permute-start.8) | collective-permute-done | bytes 131104 | tf_op jit(solution)/shard_map/ppermute | solution.py:416
  18.4 1.2 %collective-permute-done.9.refs_5_ = f32[256,128]{1,0:T(8,128)S(1)} collective-permute-done((f32[256,128]{1,0:T(8,128)S(1)}, f32[256,128]{1,0:T(8,128)S(1)}, u32[]{:S(2)}, u32[]{:S(2)}) %collective-permute-start.9) | collective-permute-done | bytes 131104 | tf_op jit(solution)/shard_map/ppermute | solution.py:416
  19.6 1.7 %collective-permute-start = (f32[2,256,128]{2,1,0:T(8,128)S(1)}, f32[2,256,128]{2,1,0:T(8,128)S(1)}, u32[]{:S(2)}, u32[]{:S(2)}) collective-permute-start(f32[2,256,128]{2,1,0:T(8,128)S(1)} %get-tuple-element.48), channel_id=1, source_target_pairs={{0,14},{2,12},{4,10},{6,8},{8,6},{10,4},{12,2},{14,0},{16,30},{18,... | collective-permute-start | bytes 786440 | tf_op jit(solution)/shard_map/ppermute | solution.py:412
  21.4 3.1 %leaf.3 = (f32[8,2304,128]{2,1,0:T(8,128)S(1)}, f32[64,128]{1,0:T(8,128)S(1)}) custom-call(f32[2,256,128]{2,1,0:T(8,128)S(1)} %get-tuple-element.53.refs_0_, f32[2,256,128]{2,1,0:T(8,128)S(1)} %collective-permute-done.5.refs_1_, f32[2,256,128]{2,1,0:T(8,128)S(1)} %collective-permute-done.6.refs_2_, f32[256,128]{1,0:T(8,128)S(1)} %collective-permute-done.7.refs_3_, ...), custom_call_target="tpu_custom_call" | custom-call | flops 1 | bytes 1 | tf_op jit(solution)/shard_map/leaf/pallas_call | solution.py:480
  24.4 3.1 %collective-permute-done.3.refs_2_ = f32[2,256,128]{2,1,0:T(8,128)S(1)} collective-permute-done((f32[2,256,128]{2,1,0:T(8,128)S(1)}, f32[2,256,128]{2,1,0:T(8,128)S(1)}, u32[]{:S(2)}, u32[]{:S(2)}) %collective-permute-start.3) | collective-permute-done | bytes 262176 | tf_op jit(solution)/shard_map/ppermute | solution.py:412
  27.6 0.5 collective-permute-start.12
  28.2 0.4 collective-permute-start.10
  29.7 5.4 %leaf.4 = (f32[8,2304,128]{2,1,0:T(8,128)S(1)}, f32[64,128]{1,0:T(8,128)S(1)}) custom-call(f32[2,256,128]{2,1,0:T(8,128)S(1)} %collective-permute-done.1.refs_0_, f32[2,256,128]{2,1,0:T(8,128)S(1)} %collective-permute-done.2.refs_1_, f32[2,256,128]{2,1,0:T(8,128)S(1)} %collective-permute-done.3.refs_2_, ...), custom_call_target="tpu_custom_call", output_to_operand_aliasing={{0}: (9, {})} | custom-call | flops 1 | bytes 1 | tf_op jit(solution)/shard_map/leaf/pallas_call | solution.py:480
  35.1 0.4 collective-permute-start.14
  35.5 1.0 collective-permute-done.14.refs_1_
  36.5 2.2 %leaf.5 = (f32[8,2304,128]{2,1,0:T(8,128)S(1)}, f32[40,128]{1,0:T(8,128)S(1)}) custom-call(f32[2,256,128]{2,1,0:T(8,128)S(1)} %collective-permute-done.refs_0_, f32[256,128]{1,0:T(8,128)S(1)} %collective-permute-done.14.refs_1_, f32[64,128]{1,0:T(8,128)S(1)} %get-tuple-element.65.refs_2_, ...), custom_call_target="tpu_custom_call", output_to_operand_aliasing={{0}: (3, {})} | custom-call | flops 1 | bytes 1 | tf_op jit(solution)/shard_map/leaf/pallas_call | solution.py:480
  38.8 1.3 %collective-permute-start.15 = (f32[40,128]{1,0:T(8,128)S(1)}, f32[40,128]{1,0:T(8,128)S(1)}, u32[]{:S(2)}, u32[]{:S(2)}) collective-permute-start(f32[40,128]{1,0:T(8,128)S(1)} %get-tuple-element.67), channel_id=1, source_target_pairs={{0,2},{2,0},{4,6},{6,4},{8,10},{10,8},{12,14},{14,12},{16,18},{18,... | collective-permute-start | bytes 61448 | tf_op jit(solution)/shard_map/ppermute | solution.py:16
  40.1 2.5 %collective-permute-done.15 = f32[40,128]{1,0:T(8,128)S(1)} collective-permute-done((f32[40,128]{1,0:T(8,128)S(1)}, f32[40,128]{1,0:T(8,128)S(1)}, u32[]{:S(2)}, u32[]{:S(2)}) %collective-permute-start.15) | collective-permute-done | bytes 20512 | tf_op jit(solution)/shard_map/ppermute | solution.py:16
  42.6 1.3 %collective-permute-start.16 = (f32[40,128]{1,0:T(8,128)S(1)}, f32[40,128]{1,0:T(8,128)S(1)}, u32[]{:S(2)}, u32[]{:S(2)}) collective-permute-start(f32[40,128]{1,0:T(8,128)S(1)} %add.51), channel_id=1, source_target_pairs={{0,4},{2,6},{4,0},{6,2},{8,12},{10,14},{12,8},{14,10},{16,20},{18,... | collective-permute-start | bytes 61448 | tf_op jit(solution)/shard_map/ppermute | solution.py:16
  43.9 2.4 %collective-permute-done.16 = f32[40,128]{1,0:T(8,128)S(1)} collective-permute-done((f32[40,128]{1,0:T(8,128)S(1)}, f32[40,128]{1,0:T(8,128)S(1)}, u32[]{:S(2)}, u32[]{:S(2)}) %collective-permute-start.16) | collective-permute-done | bytes 20512 | tf_op jit(solution)/shard_map/ppermute | solution.py:16
  46.4 1.6 %collective-permute-start.17 = (f32[40,128]{1,0:T(8,128)S(1)}, f32[40,128]{1,0:T(8,128)S(1)}, u32[]{:S(2)}, u32[]{:S(2)}) collective-permute-start(f32[40,128]{1,0:T(8,128)S(1)} %add.52), channel_id=1, source_target_pairs={{0,8},{2,10},{4,12},{6,14},{8,0},{10,2},{12,4},{14,6},{16,24},{18,... | collective-permute-start | bytes 61448 | tf_op jit(solution)/shard_map/ppermute | solution.py:16
  48.0 2.2 %collective-permute-done.17 = f32[40,128]{1,0:T(8,128)S(1)} collective-permute-done((f32[40,128]{1,0:T(8,128)S(1)}, f32[40,128]{1,0:T(8,128)S(1)}, u32[]{:S(2)}, u32[]{:S(2)}) %collective-permute-start.17) | collective-permute-done | bytes 20512 | tf_op jit(solution)/shard_map/ppermute | solution.py:16
  50.2 1.2 %collective-permute-done.18 = f32[40,128]{1,0:T(8,128)S(1)} collective-permute-done((f32[40,128]{1,0:T(8,128)S(1)}, f32[40,128]{1,0:T(8,128)S(1)}, u32[]{:S(2)}, u32[]{:S(2)}) %collective-permute-start.18) | collective-permute-done | bytes 20512 | tf_op jit(solution)/shard_map/ppermute | solution.py:416
  51.4 1.1 %far.1 = f32[1152,128]{1,0:T(8,128)S(1)} custom-call(f32[40,128]{1,0:T(8,128)S(1)} %add.54.gram_ref, f32[8,2304,128]{2,1,0:T(8,128)S(1)} %get-tuple-element.68.leaf_ref), custom_call_target="tpu_custom_call" | custom-call | flops 1 | bytes 1 | tf_op jit(solution)/shard_map/far/pallas_call | solution.py:500
  52.7 1.1 %own.1 = (f32[1152,128]{1,0:T(8,128)S(1)}, f32[192,128]{1,0:T(8,128)S(1)}, f32[128,128]{1,0:T(8,128)S(1)}, f32[128,128]{1,0:T(8,128)S(1)}, f32[128,128]{1,0:T(8,128)S(1)}) custom-call(f32[40,128]{1,0:T(8,128)S(1)} %add.54.gram_ref, f32[8,2304,128]{2,1,0:T(8,128)S(1)} %get-tuple-element.68.leaf_ref), custom_call_target="tpu_custom_call" | custom-call | flops 1 | bytes 1 | tf_op jit(solution)/shard_map/own/pallas_call | solution.py:511
  53.9 2.7 %collective-permute-start.21 = (f32[1152,128]{1,0:T(8,128)S(1)}, f32[1152,128]{1,0:T(8,128)S(1)}, u32[]{:S(2)}, u32[]{:S(2)}) collective-permute-start(f32[1152,128]{1,0:T(8,128)S(1)} %far.1), channel_id=1, source_target_pairs={{0,16},{2,18},{4,20},{6,22},{8,24},{10,26},{12,28},{14,30},{16,0},... | collective-permute-start | bytes 1769480 | tf_op jit(solution)/shard_map/ppermute | solution.py:412
  56.5 2.3 %collective-permute-start.23 = (f32[128,128]{1,0:T(8,128)S(1)}, f32[128,128]{1,0:T(8,128)S(1)}, u32[]{:S(2)}, u32[]{:S(2)}) collective-permute-start(f32[128,128]{1,0:T(8,128)S(1)} %get-tuple-element.75), channel_id=1, source_target_pairs={{0,12},{2,14},{4,8},{6,10},{8,4},{10,6},{12,0},{14,2},{16,28},{18,... | collective-permute-start | bytes 196616 | tf_op jit(solution)/shard_map/ppermute | solution.py:412
  58.9 0.6 collective-permute-start.22
  59.5 12.6 %image.1 = (f32[256,256]{1,0:T(8,128)}, f32[256,512]{1,0:T(8,128)S(1)}, f32[256,512]{1,0:T(8,128)S(1)}) custom-call(f32[256,512]{1,0:T(8,128)S(1)} %get-tuple-element.69.mine_ref, f32[256,512]{1,0:T(8,128)S(1)} %collective-permute-done.19.theirs_ref, f32[256,256]{1,0:T(8,128)S(1)} %bitcast.25, f32[9,256,1024]{2,1,0:T(8,128)} %bitcast.28), custom_call_target="tpu_custom_call" | custom-call | flops 10000000000 | bytes 1 | tf_op jit(solution)/shard_map/image/pallas_call | solution.py:523
  72.1 0.6 collective-permute-start.24
  72.7 2.5 %collective-permute-start.25 = (f32[128,128]{1,0:T(8,128)S(1)}, f32[128,128]{1,0:T(8,128)S(1)}, u32[]{:S(2)}, u32[]{:S(2)}) collective-permute-start(f32[128,128]{1,0:T(8,128)S(1)} %get-tuple-element.77), channel_id=1, source_target_pairs={{0,10},{2,8},{4,14},{6,12},{8,2},{10,0},{12,6},{14,4},{16,26},{18,... | collective-permute-start | bytes 196616 | tf_op jit(solution)/shard_map/ppermute | solution.py:412
  75.2 1.4 %collective-permute-done.24.refs_10_ = f32[128,128]{1,0:T(8,128)S(1)} collective-permute-done((f32[128,128]{1,0:T(8,128)S(1)}, f32[128,128]{1,0:T(8,128)S(1)}, u32[]{:S(2)}, u32[]{:S(2)}) %collective-permute-start.24) | collective-permute-done | bytes 65568 | tf_op jit(solution)/shard_map/ppermute | solution.py:412
  76.6 8.5 %collective-permute-done.25.refs_11_ = f32[128,128]{1,0:T(8,128)S(1)} collective-permute-done((f32[128,128]{1,0:T(8,128)S(1)}, f32[128,128]{1,0:T(8,128)S(1)}, u32[]{:S(2)}, u32[]{:S(2)}) %collective-permute-start.25) | collective-permute-done | bytes 65568 | tf_op jit(solution)/shard_map/ppermute | solution.py:412
  85.4 1.6 %collective-permute-start.27 = (f32[136,128]{1,0:T(8,128)S(1)}, f32[136,128]{1,0:T(8,128)S(1)}, u32[]{:S(2)}, u32[]{:S(2)}) collective-permute-start(f32[136,128]{1,0:T(8,128)S(1)} %get-tuple-element.81), channel_id=1, source_target_pairs={{0,4},{2,6},{4,0},{6,2},{8,12},{10,14},{12,8},{14,10},{16,20},{18,... | collective-permute-start | bytes 208904 | tf_op jit(solution)/shard_map/ppermute | solution.py:412
  87.0 2.1 %collective-permute-start.31 = (f32[136,128]{1,0:T(8,128)S(1)}, f32[136,128]{1,0:T(8,128)S(1)}, u32[]{:S(2)}, u32[]{:S(2)}) collective-permute-start(f32[136,128]{1,0:T(8,128)S(1)} %get-tuple-element.85), channel_id=1, source_target_pairs={{0,12},{2,14},{4,8},{6,10},{8,4},{10,6},{12,0},{14,2},{16,28},{18,... | collective-permute-start | bytes 208904 | tf_op jit(solution)/shard_map/ppermute | solution.py:412
  89.1 2.3 %collective-permute-start.28 = (f32[264,128]{1,0:T(8,128)S(1)}, f32[264,128]{1,0:T(8,128)S(1)}, u32[]{:S(2)}, u32[]{:S(2)}) collective-permute-start(f32[264,128]{1,0:T(8,128)S(1)} %get-tuple-element.82), channel_id=1, source_target_pairs={{0,6},{2,4},{4,2},{6,0},{8,14},{10,12},{12,10},{14,8},{16,22},{18,... | collective-permute-start | bytes 405512 | tf_op jit(solution)/shard_map/ppermute | solution.py:412
  91.4 1.2 %collective-permute-done.30.refs_5_ = f32[136,128]{1,0:T(8,128)S(1)} collective-permute-done((f32[136,128]{1,0:T(8,128)S(1)}, f32[136,128]{1,0:T(8,128)S(1)}, u32[]{:S(2)}, u32[]{:S(2)}) %collective-permute-start.30) | collective-permute-done | bytes 69664 | tf_op jit(solution)/shard_map/ppermute | solution.py:412
  92.6 0.9 collective-permute-start.32
  93.5 1.3 %collective-permute-start.26 = (f32[200,128]{1,0:T(8,128)S(1)}, f32[200,128]{1,0:T(8,128)S(1)}, u32[]{:S(2)}, u32[]{:S(2)}) collective-permute-start(f32[200,128]{1,0:T(8,128)S(1)} %get-tuple-element.80), channel_id=1, source_target_pairs={{0,2},{2,0},{4,6},{6,4},{8,10},{10,8},{12,14},{14,12},{16,18},{18,... | collective-permute-start | bytes 307208 | tf_op jit(solution)/shard_map/ppermute | solution.py:412
  94.8 5.5 %collective-permute-done.26.refs_1_ = f32[200,128]{1,0:T(8,128)S(1)} collective-permute-done((f32[200,128]{1,0:T(8,128)S(1)}, f32[200,128]{1,0:T(8,128)S(1)}, u32[]{:S(2)}, u32[]{:S(2)}) %collective-permute-start.26) | collective-permute-done | bytes 102432 | tf_op jit(solution)/shard_map/ppermute | solution.py:412
  100.4 1.2 %collective-permute-done.33 = f32[8,128]{1,0:T(8,128)S(1)} collective-permute-done((f32[8,128]{1,0:T(8,128)S(1)}, f32[8,128]{1,0:T(8,128)S(1)}, u32[]{:S(2)}, u32[]{:S(2)}) %collective-permute-start.33) | collective-permute-done | bytes 4128 | tf_op jit(solution)/shard_map/ppermute | solution.py:416
  101.6 2.3 %collective-permute-start.34 = (f32[8,128]{1,0:T(8,128)S(1)}, f32[8,128]{1,0:T(8,128)S(1)}, u32[]{:S(2)}, u32[]{:S(2)}) collective-permute-start(f32[8,128]{1,0:T(8,128)S(1)} %add.66), channel_id=1, source_target_pairs={{0,16},{2,18},{4,20},{6,22},{8,24},{10,26},{12,28},{14,30},{16,0},... | collective-permute-start | bytes 12296 | tf_op jit(solution)/shard_map/ppermute | solution.py:412
  103.9 2.2 %collective-permute-done.34 = f32[8,128]{1,0:T(8,128)S(1)} collective-permute-done((f32[8,128]{1,0:T(8,128)S(1)}, f32[8,128]{1,0:T(8,128)S(1)}, u32[]{:S(2)}, u32[]{:S(2)}) %collective-permute-start.34) | collective-permute-done | bytes 4128 | tf_op jit(solution)/shard_map/ppermute | solution.py:412
  106.1 1.0 finish.1
  107.2 1.0 fusion.4
  (55 shorter events, 2.5 us)
Async XLA Ops:
  0.6 1.0 copy-start
  1.7 0.9 copy-start.2
  3.0 9.3 %collective-permute-start.5 = (f32[2,256,128]{2,1,0:T(8,128)S(1)}, f32[2,256,128]{2,1,0:T(8,128)S(1)}, u32[]{:S(2)}, u32[]{:S(2)}) collective-permute-start(f32[2,256,128]{2,1,0:T(8,128)S(1)} %get-tuple-element.54), channel_id=1, source_target_pairs={{0,2},{2,0},{4,6},{6,4},{8,10},{10,8},{12,14},{14,12},{16,18},{18,... | collective-permute-start | bytes 786440 | tf_op jit(solution)/shard_map/ppermute | solution.py:412
  6.0 11.0 %collective-permute-start.6 = (f32[2,256,128]{2,1,0:T(8,128)S(1)}, f32[2,256,128]{2,1,0:T(8,128)S(1)}, u32[]{:S(2)}, u32[]{:S(2)}) collective-permute-start(f32[2,256,128]{2,1,0:T(8,128)S(1)} %get-tuple-element.55), channel_id=1, source_target_pairs={{0,12},{2,14},{4,8},{6,10},{8,4},{10,6},{12,0},{14,2},{16,28},{18,... | collective-permute-start | bytes 786440 | tf_op jit(solution)/shard_map/ppermute | solution.py:412
  8.5 5.6 %collective-permute-start.7 = (f32[256,128]{1,0:T(8,128)S(1)}, f32[256,128]{1,0:T(8,128)S(1)}, u32[]{:S(2)}, u32[]{:S(2)}) collective-permute-start(f32[256,128]{1,0:T(8,128)S(1)} %slice_bitcast_fusion.7), channel_id=1, source_target_pairs={{0,1},{1,0},{2,3},{3,2},{4,5},{5,4},{6,7},{7,6},{8,9},{9,8},{10,11... | collective-permute-start | bytes 393224 | tf_op jit(solution)/shard_map/ppermute | solution.py:416
  8.6 15.8 %collective-permute-start.1 = (f32[2,256,128]{2,1,0:T(8,128)S(1)}, f32[2,256,128]{2,1,0:T(8,128)S(1)}, u32[]{:S(2)}, u32[]{:S(2)}) collective-permute-start(f32[2,256,128]{2,1,0:T(8,128)S(1)} %get-tuple-element.49), channel_id=1, source_target_pairs={{0,4},{2,6},{4,0},{6,2},{8,12},{10,14},{12,8},{14,10},{16,20},{18,... | collective-permute-start | bytes 786440 | tf_op jit(solution)/shard_map/ppermute | solution.py:412
  9.2 15.3 %collective-permute-start.2 = (f32[2,256,128]{2,1,0:T(8,128)S(1)}, f32[2,256,128]{2,1,0:T(8,128)S(1)}, u32[]{:S(2)}, u32[]{:S(2)}) collective-permute-start(f32[2,256,128]{2,1,0:T(8,128)S(1)} %get-tuple-element.50), channel_id=1, source_target_pairs={{0,10},{2,8},{4,14},{6,12},{8,2},{10,0},{12,6},{14,4},{16,26},{18,... | collective-permute-start | bytes 786440 | tf_op jit(solution)/shard_map/ppermute | solution.py:412
  12.3 15.2 %collective-permute-start.3 = (f32[2,256,128]{2,1,0:T(8,128)S(1)}, f32[2,256,128]{2,1,0:T(8,128)S(1)}, u32[]{:S(2)}, u32[]{:S(2)}) collective-permute-start(f32[2,256,128]{2,1,0:T(8,128)S(1)} %get-tuple-element.51), channel_id=1, source_target_pairs={{0,8},{2,10},{4,12},{6,14},{8,0},{10,2},{12,4},{14,6},{16,24},{18,... | collective-permute-start | bytes 786440 | tf_op jit(solution)/shard_map/ppermute | solution.py:412
  14.1 13.4 %collective-permute-start.4 = (f32[2,256,128]{2,1,0:T(8,128)S(1)}, f32[2,256,128]{2,1,0:T(8,128)S(1)}, u32[]{:S(2)}, u32[]{:S(2)}) collective-permute-start(f32[2,256,128]{2,1,0:T(8,128)S(1)} %get-tuple-element.52), channel_id=1, source_target_pairs={{0,6},{2,4},{4,2},{6,0},{8,14},{10,12},{12,10},{14,8},{16,22},{18,... | collective-permute-start | bytes 786440 | tf_op jit(solution)/shard_map/ppermute | solution.py:412
  16.9 1.3 %collective-permute-start.8 = (f32[256,128]{1,0:T(8,128)S(1)}, f32[256,128]{1,0:T(8,128)S(1)}, u32[]{:S(2)}, u32[]{:S(2)}) collective-permute-start(f32[256,128]{1,0:T(8,128)S(1)} %slice_bitcast_fusion.1), channel_id=1, source_target_pairs={{0,1},{1,0},{2,3},{3,2},{4,5},{5,4},{6,7},{7,6},{8,9},{9,8},{10,11... | collective-permute-start | bytes 393224 | tf_op jit(solution)/shard_map/ppermute | solution.py:416
  18.3 1.3 %collective-permute-start.9 = (f32[256,128]{1,0:T(8,128)S(1)}, f32[256,128]{1,0:T(8,128)S(1)}, u32[]{:S(2)}, u32[]{:S(2)}) collective-permute-start(f32[256,128]{1,0:T(8,128)S(1)} %slice_bitcast_fusion), channel_id=1, source_target_pairs={{0,1},{1,0},{2,3},{3,2},{4,5},{5,4},{6,7},{7,6},{8,9},{9,8},{10,11... | collective-permute-start | bytes 393224 | tf_op jit(solution)/shard_map/ppermute | solution.py:416
  19.6 15.4 %collective-permute-start = (f32[2,256,128]{2,1,0:T(8,128)S(1)}, f32[2,256,128]{2,1,0:T(8,128)S(1)}, u32[]{:S(2)}, u32[]{:S(2)}) collective-permute-start(f32[2,256,128]{2,1,0:T(8,128)S(1)} %get-tuple-element.48), channel_id=1, source_target_pairs={{0,14},{2,12},{4,10},{6,8},{8,6},{10,4},{12,2},{14,0},{16,30},{18,... | collective-permute-start | bytes 786440 | tf_op jit(solution)/shard_map/ppermute | solution.py:412
  27.6 1.4 %collective-permute-start.13 = (f32[256,128]{1,0:T(8,128)S(1)}, f32[256,128]{1,0:T(8,128)S(1)}, u32[]{:S(2)}, u32[]{:S(2)}) collective-permute-start(f32[256,128]{1,0:T(8,128)S(1)} %slice_bitcast_fusion.3), channel_id=1, source_target_pairs={{0,1},{1,0},{2,3},{3,2},{4,5},{5,4},{6,7},{7,6},{8,9},{9,8},{10,11... | collective-permute-start | bytes 393224 | tf_op jit(solution)/shard_map/ppermute | solution.py:416
  27.6 1.5 %collective-permute-start.12 = (f32[256,128]{1,0:T(8,128)S(1)}, f32[256,128]{1,0:T(8,128)S(1)}, u32[]{:S(2)}, u32[]{:S(2)}) collective-permute-start(f32[256,128]{1,0:T(8,128)S(1)} %slice_bitcast_fusion.4), channel_id=1, source_target_pairs={{0,1},{1,0},{2,3},{3,2},{4,5},{5,4},{6,7},{7,6},{8,9},{9,8},{10,11... | collective-permute-start | bytes 393224 | tf_op jit(solution)/shard_map/ppermute | solution.py:416
  28.1 1.3 %collective-permute-start.11 = (f32[256,128]{1,0:T(8,128)S(1)}, f32[256,128]{1,0:T(8,128)S(1)}, u32[]{:S(2)}, u32[]{:S(2)}) collective-permute-start(f32[256,128]{1,0:T(8,128)S(1)} %slice_bitcast_fusion.5), channel_id=1, source_target_pairs={{0,1},{1,0},{2,3},{3,2},{4,5},{5,4},{6,7},{7,6},{8,9},{9,8},{10,11... | collective-permute-start | bytes 393224 | tf_op jit(solution)/shard_map/ppermute | solution.py:416
  28.2 1.5 %collective-permute-start.10 = (f32[256,128]{1,0:T(8,128)S(1)}, f32[256,128]{1,0:T(8,128)S(1)}, u32[]{:S(2)}, u32[]{:S(2)}) collective-permute-start(f32[256,128]{1,0:T(8,128)S(1)} %slice_bitcast_fusion.6), channel_id=1, source_target_pairs={{0,1},{1,0},{2,3},{3,2},{4,5},{5,4},{6,7},{7,6},{8,9},{9,8},{10,11... | collective-permute-start | bytes 393224 | tf_op jit(solution)/shard_map/ppermute | solution.py:416
  35.1 1.4 %collective-permute-start.14 = (f32[256,128]{1,0:T(8,128)S(1)}, f32[256,128]{1,0:T(8,128)S(1)}, u32[]{:S(2)}, u32[]{:S(2)}) collective-permute-start(f32[256,128]{1,0:T(8,128)S(1)} %slice_bitcast_fusion.2), channel_id=1, source_target_pairs={{0,1},{1,0},{2,3},{3,2},{4,5},{5,4},{6,7},{7,6},{8,9},{9,8},{10,11... | collective-permute-start | bytes 393224 | tf_op jit(solution)/shard_map/ppermute | solution.py:416
  38.8 3.8 %collective-permute-start.15 = (f32[40,128]{1,0:T(8,128)S(1)}, f32[40,128]{1,0:T(8,128)S(1)}, u32[]{:S(2)}, u32[]{:S(2)}) collective-permute-start(f32[40,128]{1,0:T(8,128)S(1)} %get-tuple-element.67), channel_id=1, source_target_pairs={{0,2},{2,0},{4,6},{6,4},{8,10},{10,8},{12,14},{14,12},{16,18},{18,... | collective-permute-start | bytes 61448 | tf_op jit(solution)/shard_map/ppermute | solution.py:16
  42.6 3.8 %collective-permute-start.16 = (f32[40,128]{1,0:T(8,128)S(1)}, f32[40,128]{1,0:T(8,128)S(1)}, u32[]{:S(2)}, u32[]{:S(2)}) collective-permute-start(f32[40,128]{1,0:T(8,128)S(1)} %add.51), channel_id=1, source_target_pairs={{0,4},{2,6},{4,0},{6,2},{8,12},{10,14},{12,8},{14,10},{16,20},{18,... | collective-permute-start | bytes 61448 | tf_op jit(solution)/shard_map/ppermute | solution.py:16
  46.4 3.8 %collective-permute-start.17 = (f32[40,128]{1,0:T(8,128)S(1)}, f32[40,128]{1,0:T(8,128)S(1)}, u32[]{:S(2)}, u32[]{:S(2)}) collective-permute-start(f32[40,128]{1,0:T(8,128)S(1)} %add.52), channel_id=1, source_target_pairs={{0,8},{2,10},{4,12},{6,14},{8,0},{10,2},{12,4},{14,6},{16,24},{18,... | collective-permute-start | bytes 61448 | tf_op jit(solution)/shard_map/ppermute | solution.py:16
  50.2 1.2 %collective-permute-start.18 = (f32[40,128]{1,0:T(8,128)S(1)}, f32[40,128]{1,0:T(8,128)S(1)}, u32[]{:S(2)}, u32[]{:S(2)}) collective-permute-start(f32[40,128]{1,0:T(8,128)S(1)} %add.53), channel_id=1, source_target_pairs={{0,1},{1,0},{2,3},{3,2},{4,5},{5,4},{6,7},{7,6},{8,9},{9,8},{10,11... | collective-permute-start | bytes 61448 | tf_op jit(solution)/shard_map/ppermute | solution.py:416
  51.4 8.1 %copy-start.3 = (f32[1,16,16,256]{3,2,1,0:T(8,128)S(1)}, f32[1,16,16,256]{3,2,1,0:T(8,128)}, u32[]{:S(2)}) copy-start(f32[1,16,16,256]{3,2,1,0:T(8,128)} %param.5) | copy-start | bytes 786436
  52.5 7.0 %collective-permute-start.19 = (f32[256,512]{1,0:T(8,128)S(1)}, f32[256,512]{1,0:T(8,128)S(1)}, u32[]{:S(2)}, u32[]{:S(2)}) collective-permute-start(f32[256,512]{1,0:T(8,128)S(1)} %get-tuple-element.69.mine_ref), channel_id=1, source_target_pairs={{0,1},{1,0},{2,3},{3,2},{4,5},{5,4},{6,7},{7,6},{8,9},{9,8},{10,11... | collective-permute-start | bytes 1572872 | tf_op jit(solution)/shard_map/ppermute | solution.py:416
  53.9 31.3 %collective-permute-start.21 = (f32[1152,128]{1,0:T(8,128)S(1)}, f32[1152,128]{1,0:T(8,128)S(1)}, u32[]{:S(2)}, u32[]{:S(2)}) collective-permute-start(f32[1152,128]{1,0:T(8,128)S(1)} %far.1), channel_id=1, source_target_pairs={{0,16},{2,18},{4,20},{6,22},{8,24},{10,26},{12,28},{14,30},{16,0},... | collective-permute-start | bytes 1769480 | tf_op jit(solution)/shard_map/ppermute | solution.py:412
  56.5 16.2 %collective-permute-start.23 = (f32[128,128]{1,0:T(8,128)S(1)}, f32[128,128]{1,0:T(8,128)S(1)}, u32[]{:S(2)}, u32[]{:S(2)}) collective-permute-start(f32[128,128]{1,0:T(8,128)S(1)} %get-tuple-element.75), channel_id=1, source_target_pairs={{0,12},{2,14},{4,8},{6,10},{8,4},{10,6},{12,0},{14,2},{16,28},{18,... | collective-permute-start | bytes 196616 | tf_op jit(solution)/shard_map/ppermute | solution.py:412
  58.9 26.3 %collective-permute-start.22 = (f32[192,128]{1,0:T(8,128)S(1)}, f32[192,128]{1,0:T(8,128)S(1)}, u32[]{:S(2)}, u32[]{:S(2)}) collective-permute-start(f32[192,128]{1,0:T(8,128)S(1)} %get-tuple-element.74), channel_id=1, source_target_pairs={{0,2},{2,0},{4,6},{6,4},{8,10},{10,8},{12,14},{14,12},{16,18},{18,... | collective-permute-start | bytes 294920 | tf_op jit(solution)/shard_map/ppermute | solution.py:412
  59.5 47.7 %copy-start.1 = (f32[1,16,16,512]{3,2,1,0:T(8,128)S(1)}, f32[1,16,16,512]{3,2,1,0:T(8,128)}, u32[]{:S(2)}) copy-start(f32[1,16,16,512]{3,2,1,0:T(8,128)} %param.3) | copy-start | bytes 1572868
  72.1 35.0 %collective-permute-start.20 = (f32[256,512]{1,0:T(8,128)S(1)}, f32[256,512]{1,0:T(8,128)S(1)}, u32[]{:S(2)}, u32[]{:S(2)}) collective-permute-start(f32[256,512]{1,0:T(8,128)S(1)} %get-tuple-element.72), channel_id=1, source_target_pairs={{0,1},{1,0},{2,3},{3,2},{4,5},{5,4},{6,7},{7,6},{8,9},{9,8},{10,11... | collective-permute-start | bytes 1572872 | tf_op jit(solution)/shard_map/ppermute | solution.py:416
  72.1 4.5 %collective-permute-start.24 = (f32[128,128]{1,0:T(8,128)S(1)}, f32[128,128]{1,0:T(8,128)S(1)}, u32[]{:S(2)}, u32[]{:S(2)}) collective-permute-start(f32[128,128]{1,0:T(8,128)S(1)} %get-tuple-element.76), channel_id=1, source_target_pairs={{0,4},{2,6},{4,0},{6,2},{8,12},{10,14},{12,8},{14,10},{16,20},{18,... | collective-permute-start | bytes 196616 | tf_op jit(solution)/shard_map/ppermute | solution.py:412
  72.7 12.4 %collective-permute-start.25 = (f32[128,128]{1,0:T(8,128)S(1)}, f32[128,128]{1,0:T(8,128)S(1)}, u32[]{:S(2)}, u32[]{:S(2)}) collective-permute-start(f32[128,128]{1,0:T(8,128)S(1)} %get-tuple-element.77), channel_id=1, source_target_pairs={{0,10},{2,8},{4,14},{6,12},{8,2},{10,0},{12,6},{14,4},{16,26},{18,... | collective-permute-start | bytes 196616 | tf_op jit(solution)/shard_map/ppermute | solution.py:412
  85.4 6.0 %collective-permute-start.27 = (f32[136,128]{1,0:T(8,128)S(1)}, f32[136,128]{1,0:T(8,128)S(1)}, u32[]{:S(2)}, u32[]{:S(2)}) collective-permute-start(f32[136,128]{1,0:T(8,128)S(1)} %get-tuple-element.81), channel_id=1, source_target_pairs={{0,4},{2,6},{4,0},{6,2},{8,12},{10,14},{12,8},{14,10},{16,20},{18,... | collective-permute-start | bytes 208904 | tf_op jit(solution)/shard_map/ppermute | solution.py:412
  87.0 5.6 %collective-permute-start.30 = (f32[136,128]{1,0:T(8,128)S(1)}, f32[136,128]{1,0:T(8,128)S(1)}, u32[]{:S(2)}, u32[]{:S(2)}) collective-permute-start(f32[136,128]{1,0:T(8,128)S(1)} %get-tuple-element.84), channel_id=1, source_target_pairs={{0,10},{2,8},{4,14},{6,12},{8,2},{10,0},{12,6},{14,4},{16,26},{18,... | collective-permute-start | bytes 208904 | tf_op jit(solution)/shard_map/ppermute | solution.py:412
  87.0 6.5 %collective-permute-start.31 = (f32[136,128]{1,0:T(8,128)S(1)}, f32[136,128]{1,0:T(8,128)S(1)}, u32[]{:S(2)}, u32[]{:S(2)}) collective-permute-start(f32[136,128]{1,0:T(8,128)S(1)} %get-tuple-element.85), channel_id=1, source_target_pairs={{0,12},{2,14},{4,8},{6,10},{8,4},{10,6},{12,0},{14,2},{16,28},{18,... | collective-permute-start | bytes 208904 | tf_op jit(solution)/shard_map/ppermute | solution.py:412
  89.1 11.2 %collective-permute-start.28 = (f32[264,128]{1,0:T(8,128)S(1)}, f32[264,128]{1,0:T(8,128)S(1)}, u32[]{:S(2)}, u32[]{:S(2)}) collective-permute-start(f32[264,128]{1,0:T(8,128)S(1)} %get-tuple-element.82), channel_id=1, source_target_pairs={{0,6},{2,4},{4,2},{6,0},{8,14},{10,12},{12,10},{14,8},{16,22},{18,... | collective-permute-start | bytes 405512 | tf_op jit(solution)/shard_map/ppermute | solution.py:412
  91.4 8.9 %collective-permute-start.29 = (f32[264,128]{1,0:T(8,128)S(1)}, f32[264,128]{1,0:T(8,128)S(1)}, u32[]{:S(2)}, u32[]{:S(2)}) collective-permute-start(f32[264,128]{1,0:T(8,128)S(1)} %get-tuple-element.83), channel_id=1, source_target_pairs={{0,8},{2,10},{4,12},{6,14},{8,0},{10,2},{12,4},{14,6},{16,24},{18,... | collective-permute-start | bytes 405512 | tf_op jit(solution)/shard_map/ppermute | solution.py:412
  92.6 7.7 %collective-permute-start.32 = (f32[264,128]{1,0:T(8,128)S(1)}, f32[264,128]{1,0:T(8,128)S(1)}, u32[]{:S(2)}, u32[]{:S(2)}) collective-permute-start(f32[264,128]{1,0:T(8,128)S(1)} %get-tuple-element.86), channel_id=1, source_target_pairs={{0,14},{2,12},{4,10},{6,8},{8,6},{10,4},{12,2},{14,0},{16,30},{18,... | collective-permute-start | bytes 405512 | tf_op jit(solution)/shard_map/ppermute | solution.py:412
  93.5 6.8 %collective-permute-start.26 = (f32[200,128]{1,0:T(8,128)S(1)}, f32[200,128]{1,0:T(8,128)S(1)}, u32[]{:S(2)}, u32[]{:S(2)}) collective-permute-start(f32[200,128]{1,0:T(8,128)S(1)} %get-tuple-element.80), channel_id=1, source_target_pairs={{0,2},{2,0},{4,6},{6,4},{8,10},{10,8},{12,14},{14,12},{16,18},{18,... | collective-permute-start | bytes 307208 | tf_op jit(solution)/shard_map/ppermute | solution.py:412
  100.4 1.2 %collective-permute-start.33 = (f32[8,128]{1,0:T(8,128)S(1)}, f32[8,128]{1,0:T(8,128)S(1)}, u32[]{:S(2)}, u32[]{:S(2)}) collective-permute-start(f32[8,128]{1,0:T(8,128)S(1)} %slice_add_fusion), channel_id=1, source_target_pairs={{0,1},{1,0},{2,3},{3,2},{4,5},{5,4},{6,7},{7,6},{8,9},{9,8},{10,11... | collective-permute-start | bytes 12296 | tf_op jit(solution)/shard_map/ppermute | solution.py:416
  101.6 4.5 %collective-permute-start.34 = (f32[8,128]{1,0:T(8,128)S(1)}, f32[8,128]{1,0:T(8,128)S(1)}, u32[]{:S(2)}, u32[]{:S(2)}) collective-permute-start(f32[8,128]{1,0:T(8,128)S(1)} %add.66), channel_id=1, source_target_pairs={{0,16},{2,18},{4,20},{6,22},{8,24},{10,26},{12,28},{14,30},{16,0},... | collective-permute-start | bytes 12296 | tf_op jit(solution)/shard_map/ppermute | solution.py:412

commit v3 on v2

--- a/solution.py
+++ b/solution.py
@@ -332,19 +332,15 @@
     lax.fori_loop(0, out_ref.shape[0] // size, some, 0)
 
 
-def far_kernel(gram_ref, leaf_ref, out_ref):
-    images = leaf_ref.shape[0]
-    held = tree_factors(jnp.sum(gram_ref[...], 1, keepdims=True), images)
-    combine(held, leaf_ref, (1 - place()[1]) * out_ref.shape[0], out_ref)
-
-
-def own_kernel(unit, gram_ref, leaf_ref, out_ref, *message_refs):
+def combine_kernel(unit, gram_ref, leaf_ref, far_ref, own_ref, *message_refs):
     images = leaf_ref.shape[0]
     member, cube, _ = place()
+    half = own_ref.shape[0]
     held = tree_factors(jnp.sum(gram_ref[...], 1, keepdims=True), images)
-    combine(held, leaf_ref, cube * out_ref.shape[0], out_ref)
+    combine(held, leaf_ref, (1 - cube) * half, far_ref)
+    combine(held, leaf_ref, cube * half, own_ref)
     for other, message in zip(EARLY, message_refs):
-        pack(member, out_ref, message, other, unit, 0)
+        pack(member, own_ref, message, other, unit, 0)
 
 
 def first_unit(target, part):
@@ -421,7 +417,8 @@
 
 
 ORDER = (1, 6, 2, 5, 4, 3, 7)
-EARLY = (1, 6, 2, 5)
+EARLY = (1, 3, 5, 7)
+LAST = (6, 1, 2, 5, 4, 3, 7)
 COST = 10**10
 BATCHES = ((0, 1, 6), (2, 5, 4, 3), (7,))
 
@@ -449,10 +446,10 @@
     upstream = cotangent.reshape(pixels, filters)
     activity, *sent = pl.pallas_call(
         prepare_kernel,
-        in_specs=[VMEM, VMEM],
+        in_specs=[VMEM] * 2,
         out_specs=[VMEM] * (1 + images),
         out_shape=[f32(pixels, own_channels)] + [f32(2, pixels, lanes)] * images,
-        compiler_params=params(32),
+        compiler_params=params(24),
         cost_estimate=small,
         name="prepare",
     )(before, upstream)
@@ -497,26 +494,18 @@
         gram = gram + from_partner(gram, "dp", bit)
     gram = gram + swap_cores(gram)
 
-    piece = pl.pallas_call(
-        far_kernel,
+    theirs = swap_cores(activity)
+    gram, theirs = lax.optimization_barrier((gram, theirs))
+    piece, own, *own_sent = pl.pallas_call(
+        functools.partial(combine_kernel, unit),
         in_specs=[VMEM, VMEM],
-        out_specs=VMEM,
-        out_shape=f32(half, lanes),
+        out_specs=[VMEM] * (2 + len(EARLY)),
+        out_shape=[f32(half, lanes)] * 2 + [f32(units(other) * unit, lanes) for other in EARLY],
         compiler_params=params(24),
         cost_estimate=small,
-        name="far",
+        name="combine",
     )(gram, leaves)
     far = exchange(piece, images)
-
-    own, *own_sent = pl.pallas_call(
-        functools.partial(own_kernel, unit),
-        in_specs=[VMEM, VMEM],
-        out_specs=[VMEM] * (1 + len(EARLY)),
-        out_shape=[f32(half, lanes)] + [f32(units(other) * unit, lanes) for other in EARLY],
-        compiler_params=params(24),
-        cost_estimate=small,
-        name="own",
-    )(gram, leaves)
     own_messages = [exchange(message, other) for message, other in zip(own_sent, EARLY)]
 
     activity, piece = lax.optimization_barrier((activity, piece))
@@ -537,10 +526,10 @@
         compiler_params=params(44),
         cost_estimate=pl.CostEstimate(flops=COST, bytes_accessed=1, transcendentals=0),
         name="image",
-    )(activity, swap_cores(activity), upstream, weights.transpose(1, 0, 2))
+    )(activity, theirs, upstream, weights.transpose(1, 0, 2))
     input_grad = (kept + swap_cores(given)) * gelu_slope(before)
 
-    far, own_messages = lax.optimization_barrier((far, own_messages))
+    far, own_messages, output = lax.optimization_barrier((far, own_messages, output))
     far_sent = pl.pallas_call(
         functools.partial(moments_kernel, unit),
         in_specs=[VMEM, VMEM],
@@ -552,10 +541,16 @@
         cost_estimate=small,
         name="moments",
     )(own, far)
-    far_messages = spread(far_sent)
-    moments = functools.reduce(jnp.add, [far_messages[i][0:8] for i in range(images)])
+    far_messages = {0: far_sent[0]}
+    for other in LAST:
+        far_messages[other] = exchange(far_sent[other], other)
+    moments = far_sent[0][0:8]
+    for other in LAST:
+        moments, far_messages[other] = lax.optimization_barrier((moments, far_messages[other]))
+        moments = moments + far_messages[other][0:8]
     moments = moments + swap_cores(moments)
     moments = moments + exchange(moments, images)
+    moments, input_grad = lax.optimization_barrier((moments, input_grad))
     weight_grad = pl.pallas_call(
         functools.partial(finish_kernel, unit, images),
         in_specs=[VMEM] * (1 + images + len(EARLY)),

time: 109 us -> 105 us (0.963)
  waiting for transfers between devices: 39.1 us -> 34.7 us
  starting transfers between devices: 38 us -> 39.4 us
    ppermute x20, waiting for transfers between devices: 25 us -> 20.8 us  [exchange(): return lax.ppermute(x, 'dp', [(i, i ^ other) for i in range(size)])]
    ppermute x20, starting transfers between devices: 31.7 us -> 33.1 us  [exchange(): return lax.ppermute(x, 'dp', [(i, i ^ other) for i in range(size)])]
    pallas_call x3 -> x2, Pallas kernels: 2.58 us -> 1.88 us  [the longest x1 1.53 us: local_cube(): pl.pallas_call(functools.partial(combine_kernel, unit), in_specs=[VMEM, V...]
  transfers between devices with their start and end apart: 35 -> 35, of which waited for: 19 -> 20; matrix products, arithmetic and copies ran while one was open for 0% -> 1% of each run, Pallas kernels for 22% -> 22%
where the time goes in v3:
time: 105 us
  starting transfers between devices  39.4 us (38%)
  waiting for transfers between devices  34.7 us (33%)
  Pallas kernels  26.5 us (25%)
  local copies, waits for them, and re-layouts  2.07 us (2%)
  other arithmetic  1.07 us (1%)
    ppermute x20, starting transfers between devices, exchange(): return lax.ppermute(x, 'dp', [(i, i ^ other) for i in range(size)])  33.1 us
    ppermute x20, waiting for transfers between devices, exchange(): return lax.ppermute(x, 'dp', [(i, i ^ other) for i in range(size)])  20.8 us
    pallas_call x1, Pallas kernels, local_cube(): pl.pallas_call(functools.partial(image_kernel, extent), grid=(taps,), in_...  12.6 us
    pallas_call x3, Pallas kernels, local_cube(): pl.pallas_call(functools.partial(leaf_kernel, extent, images, known, batc...  10.7 us
    ppermute x3, waiting for transfers between devices, from_partner(): lax.ppermute(x, axis, [(i, i ^ 1 << apart) for i in range(lax.axis_size(a...  7.18 us
    ppermute x12, waiting for transfers between devices, swap_cores(): return lax.ppermute(x, 'mp', [(0, 1), (1, 0)])  6.71 us
    ppermute x3, starting transfers between devices, from_partner(): lax.ppermute(x, axis, [(i, i ^ 1 << apart) for i in range(lax.axis_size(a...  4.25 us
  transfers between devices with their start and end apart: 35, of which 20 were waited for; matrix products, arithmetic and copies ran while one was open for 1% of the time, Pallas kernels for 22%

profile of v3, /device:TPU:0, one launch (start us, length us, event | category | flops | bytes accessed | tf_op | source)
XLA Modules:
  0.0 104.5 jit_solution(608076957027945465)
XLA Ops:
  0.6 1.0 copy-done
  1.7 0.9 copy-done.2
  3.0 3.0 %collective-permute-start.5 = (f32[2,256,128]{2,1,0:T(8,128)S(1)}, f32[2,256,128]{2,1,0:T(8,128)S(1)}, u32[]{:S(2)}, u32[]{:S(2)}) collective-permute-start(f32[2,256,128]{2,1,0:T(8,128)S(1)} %get-tuple-element.73), channel_id=1, source_target_pairs={{0,2},{2,0},{4,6},{6,4},{8,10},{10,8},{12,14},{14,12},{16,18},{18,... | collective-permute-start | bytes 786440 | tf_op jit(solution)/shard_map/ppermute | solution.py:408
  6.0 2.5 %collective-permute-start.6 = (f32[2,256,128]{2,1,0:T(8,128)S(1)}, f32[2,256,128]{2,1,0:T(8,128)S(1)}, u32[]{:S(2)}, u32[]{:S(2)}) collective-permute-start(f32[2,256,128]{2,1,0:T(8,128)S(1)} %get-tuple-element.74), channel_id=1, source_target_pairs={{0,12},{2,14},{4,8},{6,10},{8,4},{10,6},{12,0},{14,2},{16,28},{18,... | collective-permute-start | bytes 786440 | tf_op jit(solution)/shard_map/ppermute | solution.py:408
  8.6 0.6 collective-permute-start.1
  9.2 3.1 %collective-permute-done.5.refs_1_ = f32[2,256,128]{2,1,0:T(8,128)S(1)} collective-permute-done((f32[2,256,128]{2,1,0:T(8,128)S(1)}, f32[2,256,128]{2,1,0:T(8,128)S(1)}, u32[]{:S(2)}, u32[]{:S(2)}) %collective-permute-start.5) | collective-permute-done | bytes 262176 | tf_op jit(solution)/shard_map/ppermute | solution.py:408
  12.3 1.8 %collective-permute-start.3 = (f32[2,256,128]{2,1,0:T(8,128)S(1)}, f32[2,256,128]{2,1,0:T(8,128)S(1)}, u32[]{:S(2)}, u32[]{:S(2)}) collective-permute-start(f32[2,256,128]{2,1,0:T(8,128)S(1)} %get-tuple-element.70), channel_id=1, source_target_pairs={{0,8},{2,10},{4,12},{6,14},{8,0},{10,2},{12,4},{14,6},{16,24},{18,... | collective-permute-start | bytes 786440 | tf_op jit(solution)/shard_map/ppermute | solution.py:408
  14.1 2.8 %collective-permute-start.4 = (f32[2,256,128]{2,1,0:T(8,128)S(1)}, f32[2,256,128]{2,1,0:T(8,128)S(1)}, u32[]{:S(2)}, u32[]{:S(2)}) collective-permute-start(f32[2,256,128]{2,1,0:T(8,128)S(1)} %get-tuple-element.71), channel_id=1, source_target_pairs={{0,6},{2,4},{4,2},{6,0},{8,14},{10,12},{12,10},{14,8},{16,22},{18,... | collective-permute-start | bytes 786440 | tf_op jit(solution)/shard_map/ppermute | solution.py:408
  17.0 1.3 %collective-permute-done.8.refs_4_ = f32[256,128]{1,0:T(8,128)S(1)} collective-permute-done((f32[256,128]{1,0:T(8,128)S(1)}, f32[256,128]{1,0:T(8,128)S(1)}, u32[]{:S(2)}, u32[]{:S(2)}) %collective-permute-start.8) | collective-permute-done | bytes 131104 | tf_op jit(solution)/shard_map/ppermute | solution.py:412
  18.4 1.2 %collective-permute-done.9.refs_5_ = f32[256,128]{1,0:T(8,128)S(1)} collective-permute-done((f32[256,128]{1,0:T(8,128)S(1)}, f32[256,128]{1,0:T(8,128)S(1)}, u32[]{:S(2)}, u32[]{:S(2)}) %collective-permute-start.9) | collective-permute-done | bytes 131104 | tf_op jit(solution)/shard_map/ppermute | solution.py:412
  19.6 1.7 %collective-permute-start = (f32[2,256,128]{2,1,0:T(8,128)S(1)}, f32[2,256,128]{2,1,0:T(8,128)S(1)}, u32[]{:S(2)}, u32[]{:S(2)}) collective-permute-start(f32[2,256,128]{2,1,0:T(8,128)S(1)} %get-tuple-element.67), channel_id=1, source_target_pairs={{0,14},{2,12},{4,10},{6,8},{8,6},{10,4},{12,2},{14,0},{16,30},{18,... | collective-permute-start | bytes 786440 | tf_op jit(solution)/shard_map/ppermute | solution.py:408
  21.4 3.1 %leaf.3 = (f32[8,2304,128]{2,1,0:T(8,128)S(1)}, f32[64,128]{1,0:T(8,128)S(1)}) custom-call(f32[2,256,128]{2,1,0:T(8,128)S(1)} %get-tuple-element.72.refs_0_, f32[2,256,128]{2,1,0:T(8,128)S(1)} %collective-permute-done.5.refs_1_, f32[2,256,128]{2,1,0:T(8,128)S(1)} %collective-permute-done.6.refs_2_, f32[256,128]{1,0:T(8,128)S(1)} %collective-permute-done.7.refs_3_, ...), custom_call_target="tpu_custom_call" | custom-call | flops 1 | bytes 1 | tf_op jit(solution)/shard_map/leaf/pallas_call | solution.py:477
  24.4 3.1 %collective-permute-done.3.refs_2_ = f32[2,256,128]{2,1,0:T(8,128)S(1)} collective-permute-done((f32[2,256,128]{2,1,0:T(8,128)S(1)}, f32[2,256,128]{2,1,0:T(8,128)S(1)}, u32[]{:S(2)}, u32[]{:S(2)}) %collective-permute-start.3) | collective-permute-done | bytes 262176 | tf_op jit(solution)/shard_map/ppermute | solution.py:408
  27.6 0.6 collective-permute-start.11
  28.3 0.6 collective-permute-start.13
  29.8 5.4 %leaf.4 = (f32[8,2304,128]{2,1,0:T(8,128)S(1)}, f32[64,128]{1,0:T(8,128)S(1)}) custom-call(f32[2,256,128]{2,1,0:T(8,128)S(1)} %collective-permute-done.1.refs_0_, f32[2,256,128]{2,1,0:T(8,128)S(1)} %collective-permute-done.2.refs_1_, f32[2,256,128]{2,1,0:T(8,128)S(1)} %collective-permute-done.3.refs_2_, ...), custom_call_target="tpu_custom_call", output_to_operand_aliasing={{0}: (9, {})} | custom-call | flops 1 | bytes 1 | tf_op jit(solution)/shard_map/leaf/pallas_call | solution.py:477
  35.6 1.0 collective-permute-done.14.refs_1_
  36.6 2.2 %leaf.5 = (f32[8,2304,128]{2,1,0:T(8,128)S(1)}, f32[40,128]{1,0:T(8,128)S(1)}) custom-call(f32[2,256,128]{2,1,0:T(8,128)S(1)} %collective-permute-done.refs_0_, f32[256,128]{1,0:T(8,128)S(1)} %collective-permute-done.14.refs_1_, f32[64,128]{1,0:T(8,128)S(1)} %get-tuple-element.84.refs_2_, ...), custom_call_target="tpu_custom_call", output_to_operand_aliasing={{0}: (3, {})} | custom-call | flops 1 | bytes 1 | tf_op jit(solution)/shard_map/leaf/pallas_call | solution.py:477
  38.9 1.3 %collective-permute-start.15 = (f32[40,128]{1,0:T(8,128)S(1)}, f32[40,128]{1,0:T(8,128)S(1)}, u32[]{:S(2)}, u32[]{:S(2)}) collective-permute-start(f32[40,128]{1,0:T(8,128)S(1)} %get-tuple-element.86), channel_id=1, source_target_pairs={{0,2},{2,0},{4,6},{6,4},{8,10},{10,8},{12,14},{14,12},{16,18},{18,... | collective-permute-start | bytes 61448 | tf_op jit(solution)/shard_map/ppermute | solution.py:16
  40.2 2.5 %collective-permute-done.15 = f32[40,128]{1,0:T(8,128)S(1)} collective-permute-done((f32[40,128]{1,0:T(8,128)S(1)}, f32[40,128]{1,0:T(8,128)S(1)}, u32[]{:S(2)}, u32[]{:S(2)}) %collective-permute-start.15) | collective-permute-done | bytes 20512 | tf_op jit(solution)/shard_map/ppermute | solution.py:16
  42.8 1.3 %collective-permute-start.16 = (f32[40,128]{1,0:T(8,128)S(1)}, f32[40,128]{1,0:T(8,128)S(1)}, u32[]{:S(2)}, u32[]{:S(2)}) collective-permute-start(f32[40,128]{1,0:T(8,128)S(1)} %add.51), channel_id=1, source_target_pairs={{0,4},{2,6},{4,0},{6,2},{8,12},{10,14},{12,8},{14,10},{16,20},{18,... | collective-permute-start | bytes 61448 | tf_op jit(solution)/shard_map/ppermute | solution.py:16
  44.1 2.4 %collective-permute-done.16 = f32[40,128]{1,0:T(8,128)S(1)} collective-permute-done((f32[40,128]{1,0:T(8,128)S(1)}, f32[40,128]{1,0:T(8,128)S(1)}, u32[]{:S(2)}, u32[]{:S(2)}) %collective-permute-start.16) | collective-permute-done | bytes 20512 | tf_op jit(solution)/shard_map/ppermute | solution.py:16
  46.6 1.6 %collective-permute-start.17 = (f32[40,128]{1,0:T(8,128)S(1)}, f32[40,128]{1,0:T(8,128)S(1)}, u32[]{:S(2)}, u32[]{:S(2)}) collective-permute-start(f32[40,128]{1,0:T(8,128)S(1)} %add.52), channel_id=1, source_target_pairs={{0,8},{2,10},{4,12},{6,14},{8,0},{10,2},{12,4},{14,6},{16,24},{18,... | collective-permute-start | bytes 61448 | tf_op jit(solution)/shard_map/ppermute | solution.py:16
  48.1 2.2 %collective-permute-done.17 = f32[40,128]{1,0:T(8,128)S(1)} collective-permute-done((f32[40,128]{1,0:T(8,128)S(1)}, f32[40,128]{1,0:T(8,128)S(1)}, u32[]{:S(2)}, u32[]{:S(2)}) %collective-permute-start.17) | collective-permute-done | bytes 20512 | tf_op jit(solution)/shard_map/ppermute | solution.py:16
  50.3 1.2 %collective-permute-done.18 = f32[40,128]{1,0:T(8,128)S(1)} collective-permute-done((f32[40,128]{1,0:T(8,128)S(1)}, f32[40,128]{1,0:T(8,128)S(1)}, u32[]{:S(2)}, u32[]{:S(2)}) %collective-permute-start.18) | collective-permute-done | bytes 20512 | tf_op jit(solution)/shard_map/ppermute | solution.py:412
  51.5 1.5 %combine.1 = (f32[1152,128]{1,0:T(8,128)S(1)}, f32[1152,128]{1,0:T(8,128)S(1)}, f32[192,128]{1,0:T(8,128)S(1)}, f32[128,128]{1,0:T(8,128)S(1)}, f32[128,128]{1,0:T(8,128)S(1)}, /*index=5*/f32[128,128]{1,0:T(8,128)S(1)}) custom-call(f32[40,128]{1,0:T(8,128)S(1)} %add.54.gram_ref, f32[8,2304,128]{2,1,0:T(8,128)S(1)} %get-tuple-element.89.leaf_ref), custom_call_target="tpu_custom_call" | custom-call | flops 1 | bytes 1 | tf_op jit(solution)/shard_map/combine/pallas_call | solution.py:499
  53.1 2.7 %collective-permute-start.20 = (f32[1152,128]{1,0:T(8,128)S(1)}, f32[1152,128]{1,0:T(8,128)S(1)}, u32[]{:S(2)}, u32[]{:S(2)}) collective-permute-start(f32[1152,128]{1,0:T(8,128)S(1)} %get-tuple-element.90), channel_id=1, source_target_pairs={{0,16},{2,18},{4,20},{6,22},{8,24},{10,26},{12,28},{14,30},{16,0},... | collective-permute-start | bytes 1769480 | tf_op jit(solution)/shard_map/ppermute | solution.py:408
  55.7 1.3 %collective-permute-start.21 = (f32[192,128]{1,0:T(8,128)S(1)}, f32[192,128]{1,0:T(8,128)S(1)}, u32[]{:S(2)}, u32[]{:S(2)}) collective-permute-start(f32[192,128]{1,0:T(8,128)S(1)} %get-tuple-element.91), channel_id=1, source_target_pairs={{0,2},{2,0},{4,6},{6,4},{8,10},{10,8},{12,14},{14,12},{16,18},{18,... | collective-permute-start | bytes 294920 | tf_op jit(solution)/shard_map/ppermute | solution.py:408
  57.0 1.5 %collective-permute-start.22 = (f32[128,128]{1,0:T(8,128)S(1)}, f32[128,128]{1,0:T(8,128)S(1)}, u32[]{:S(2)}, u32[]{:S(2)}) collective-permute-start(f32[128,128]{1,0:T(8,128)S(1)} %get-tuple-element.92), channel_id=1, source_target_pairs={{0,6},{2,4},{4,2},{6,0},{8,14},{10,12},{12,10},{14,8},{16,22},{18,... | collective-permute-start | bytes 196616 | tf_op jit(solution)/shard_map/ppermute | solution.py:408
  58.5 1.6 %collective-permute-start.23 = (f32[128,128]{1,0:T(8,128)S(1)}, f32[128,128]{1,0:T(8,128)S(1)}, u32[]{:S(2)}, u32[]{:S(2)}) collective-permute-start(f32[128,128]{1,0:T(8,128)S(1)} %get-tuple-element.93), channel_id=1, source_target_pairs={{0,10},{2,8},{4,14},{6,12},{8,2},{10,0},{12,6},{14,4},{16,26},{18,... | collective-permute-start | bytes 196616 | tf_op jit(solution)/shard_map/ppermute | solution.py:408
  60.2 1.4 %collective-permute-start.24 = (f32[128,128]{1,0:T(8,128)S(1)}, f32[128,128]{1,0:T(8,128)S(1)}, u32[]{:S(2)}, u32[]{:S(2)}) collective-permute-start(f32[128,128]{1,0:T(8,128)S(1)} %get-tuple-element.94), channel_id=1, source_target_pairs={{0,14},{2,12},{4,10},{6,8},{8,6},{10,4},{12,2},{14,0},{16,30},{18,... | collective-permute-start | bytes 196616 | tf_op jit(solution)/shard_map/ppermute | solution.py:408
  61.6 12.6 %image.1 = (f32[256,256]{1,0:T(8,128)}, f32[256,512]{1,0:T(8,128)S(1)}, f32[256,512]{1,0:T(8,128)S(1)}) custom-call(f32[256,512]{1,0:T(8,128)S(1)} %get-tuple-element.95.mine_ref, f32[256,512]{1,0:T(8,128)S(1)} %collective-permute-done.19.theirs_ref, f32[256,256]{1,0:T(8,128)S(1)} %bitcast.25, f32[9,256,1024]{2,1,0:T(8,128)} %bitcast.28), custom_call_target="tpu_custom_call" | custom-call | flops 10000000000 | bytes 1 | tf_op jit(solution)/shard_map/image/pallas_call | solution.py:512
  74.3 7.8 %collective-permute-done.20.far_ref = f32[1152,128]{1,0:T(8,128)S(1)} collective-permute-done((f32[1152,128]{1,0:T(8,128)S(1)}, f32[1152,128]{1,0:T(8,128)S(1)}, u32[]{:S(2)}, u32[]{:S(2)}) %collective-permute-start.20) | collective-permute-done | bytes 589856 | tf_op jit(solution)/shard_map/ppermute | solution.py:408
  82.3 1.5 %collective-permute-start.25 = (f32[264,128]{1,0:T(8,128)S(1)}, f32[264,128]{1,0:T(8,128)S(1)}, u32[]{:S(2)}, u32[]{:S(2)}) collective-permute-start(f32[264,128]{1,0:T(8,128)S(1)} %get-tuple-element.102), channel_id=1, source_target_pairs={{0,12},{2,14},{4,8},{6,10},{8,4},{10,6},{12,0},{14,2},{16,28},{18,... | collective-permute-start | bytes 405512 | tf_op jit(solution)/shard_map/ppermute | solution.py:408
  83.8 0.7 collective-permute-start.26
  84.5 0.8 collective-permute-start.27
  85.4 2.0 %collective-permute-start.28 = (f32[136,128]{1,0:T(8,128)S(1)}, f32[136,128]{1,0:T(8,128)S(1)}, u32[]{:S(2)}, u32[]{:S(2)}) collective-permute-start(f32[136,128]{1,0:T(8,128)S(1)} %get-tuple-element.111), channel_id=1, source_target_pairs={{0,10},{2,8},{4,14},{6,12},{8,2},{10,0},{12,6},{14,4},{16,26},{18,... | collective-permute-start | bytes 208904 | tf_op jit(solution)/shard_map/ppermute | solution.py:408
  87.3 1.1 %collective-permute-done.25.refs_6_ = f32[264,128]{1,0:T(8,128)S(1)} collective-permute-done((f32[264,128]{1,0:T(8,128)S(1)}, f32[264,128]{1,0:T(8,128)S(1)}, u32[]{:S(2)}, u32[]{:S(2)}) %collective-permute-start.25) | collective-permute-done | bytes 135200 | tf_op jit(solution)/shard_map/ppermute | solution.py:408
  88.4 1.1 %collective-permute-start.29 = (f32[264,128]{1,0:T(8,128)S(1)}, f32[264,128]{1,0:T(8,128)S(1)}, u32[]{:S(2)}, u32[]{:S(2)}) collective-permute-start(f32[264,128]{1,0:T(8,128)S(1)} %get-tuple-element.114), channel_id=1, source_target_pairs={{0,8},{2,10},{4,12},{6,14},{8,0},{10,2},{12,4},{14,6},{16,24},{18,... | collective-permute-start | bytes 405512 | tf_op jit(solution)/shard_map/ppermute | solution.py:408
  89.5 2.2 %collective-permute-start.30 = (f32[136,128]{1,0:T(8,128)S(1)}, f32[136,128]{1,0:T(8,128)S(1)}, u32[]{:S(2)}, u32[]{:S(2)}) collective-permute-start(f32[136,128]{1,0:T(8,128)S(1)} %get-tuple-element.117), channel_id=1, source_target_pairs={{0,6},{2,4},{4,2},{6,0},{8,14},{10,12},{12,10},{14,8},{16,22},{18,... | collective-permute-start | bytes 208904 | tf_op jit(solution)/shard_map/ppermute | solution.py:408
  91.7 1.5 %collective-permute-start.31 = (f32[136,128]{1,0:T(8,128)S(1)}, f32[136,128]{1,0:T(8,128)S(1)}, u32[]{:S(2)}, u32[]{:S(2)}) collective-permute-start(f32[136,128]{1,0:T(8,128)S(1)} %get-tuple-element.120), channel_id=1, source_target_pairs={{0,14},{2,12},{4,10},{6,8},{8,6},{10,4},{12,2},{14,0},{16,30},{18,... | collective-permute-start | bytes 208904 | tf_op jit(solution)/shard_map/ppermute | solution.py:408
  93.4 1.3 %collective-permute-done.30.refs_3_ = f32[136,128]{1,0:T(8,128)S(1)} collective-permute-done((f32[136,128]{1,0:T(8,128)S(1)}, f32[136,128]{1,0:T(8,128)S(1)}, u32[]{:S(2)}, u32[]{:S(2)}) %collective-permute-start.30) | collective-permute-done | bytes 69664 | tf_op jit(solution)/shard_map/ppermute | solution.py:408
  94.7 3.1 %collective-permute-done.31.refs_7_ = f32[136,128]{1,0:T(8,128)S(1)} collective-permute-done((f32[136,128]{1,0:T(8,128)S(1)}, f32[136,128]{1,0:T(8,128)S(1)}, u32[]{:S(2)}, u32[]{:S(2)}) %collective-permute-start.31) | collective-permute-done | bytes 69664 | tf_op jit(solution)/shard_map/ppermute | solution.py:408
  97.8 1.2 %collective-permute-done.32 = f32[8,128]{1,0:T(8,128)S(1)} collective-permute-done((f32[8,128]{1,0:T(8,128)S(1)}, f32[8,128]{1,0:T(8,128)S(1)}, u32[]{:S(2)}, u32[]{:S(2)}) %collective-permute-start.32) | collective-permute-done | bytes 4128 | tf_op jit(solution)/shard_map/ppermute | solution.py:412
  99.0 2.4 %collective-permute-start.33 = (f32[8,128]{1,0:T(8,128)S(1)}, f32[8,128]{1,0:T(8,128)S(1)}, u32[]{:S(2)}, u32[]{:S(2)}) collective-permute-start(f32[8,128]{1,0:T(8,128)S(1)} %add.62), channel_id=1, source_target_pairs={{0,16},{2,18},{4,20},{6,22},{8,24},{10,26},{12,28},{14,30},{16,0},... | collective-permute-start | bytes 12296 | tf_op jit(solution)/shard_map/ppermute | solution.py:408
  101.3 1.0 fusion.4
  102.3 1.1 %collective-permute-done.33 = f32[8,128]{1,0:T(8,128)S(1)} collective-permute-done((f32[8,128]{1,0:T(8,128)S(1)}, f32[8,128]{1,0:T(8,128)S(1)}, u32[]{:S(2)}, u32[]{:S(2)}) %collective-permute-start.33) | collective-permute-done | bytes 4128 | tf_op jit(solution)/shard_map/ppermute | solution.py:408
  103.5 1.0 %finish.1 = f32[576,256]{1,0:T(8,128)} custom-call(f32[8,128]{1,0:T(8,128)S(1)} %add.63.moments_ref, f32[392,128]{1,0:T(8,128)S(1)} %get-tuple-element.101.refs_0_, f32[200,128]{1,0:T(8,128)S(1)} %collective-permute-done.26.refs_1_, f32[264,128]{1,0:T(8,128)S(1)} %collective-permute-done.27.refs_2_, f32[136,128]{1,0:T(8,128)S(1)} %collective-permute-done.30.refs_3_, ...), custom_call_target="tpu_custom_call" | custom-call | flops 1 | bytes 1 | tf_op jit(solution)/shard_map/finish/pallas_call | solution.py:554
  (61 shorter events, 2.8 us)
Async XLA Ops:
  0.6 1.0 copy-start
  1.7 0.9 copy-start.2
  3.0 9.3 %collective-permute-start.5 = (f32[2,256,128]{2,1,0:T(8,128)S(1)}, f32[2,256,128]{2,1,0:T(8,128)S(1)}, u32[]{:S(2)}, u32[]{:S(2)}) collective-permute-start(f32[2,256,128]{2,1,0:T(8,128)S(1)} %get-tuple-element.73), channel_id=1, source_target_pairs={{0,2},{2,0},{4,6},{6,4},{8,10},{10,8},{12,14},{14,12},{16,18},{18,... | collective-permute-start | bytes 786440 | tf_op jit(solution)/shard_map/ppermute | solution.py:408
  6.0 11.0 %collective-permute-start.6 = (f32[2,256,128]{2,1,0:T(8,128)S(1)}, f32[2,256,128]{2,1,0:T(8,128)S(1)}, u32[]{:S(2)}, u32[]{:S(2)}) collective-permute-start(f32[2,256,128]{2,1,0:T(8,128)S(1)} %get-tuple-element.74), channel_id=1, source_target_pairs={{0,12},{2,14},{4,8},{6,10},{8,4},{10,6},{12,0},{14,2},{16,28},{18,... | collective-permute-start | bytes 786440 | tf_op jit(solution)/shard_map/ppermute | solution.py:408
  8.5 5.6 %collective-permute-start.7 = (f32[256,128]{1,0:T(8,128)S(1)}, f32[256,128]{1,0:T(8,128)S(1)}, u32[]{:S(2)}, u32[]{:S(2)}) collective-permute-start(f32[256,128]{1,0:T(8,128)S(1)} %slice_bitcast_fusion.7), channel_id=1, source_target_pairs={{0,1},{1,0},{2,3},{3,2},{4,5},{5,4},{6,7},{7,6},{8,9},{9,8},{10,11... | collective-permute-start | bytes 393224 | tf_op jit(solution)/shard_map/ppermute | solution.py:412
  8.6 15.8 %collective-permute-start.1 = (f32[2,256,128]{2,1,0:T(8,128)S(1)}, f32[2,256,128]{2,1,0:T(8,128)S(1)}, u32[]{:S(2)}, u32[]{:S(2)}) collective-permute-start(f32[2,256,128]{2,1,0:T(8,128)S(1)} %get-tuple-element.68), channel_id=1, source_target_pairs={{0,4},{2,6},{4,0},{6,2},{8,12},{10,14},{12,8},{14,10},{16,20},{18,... | collective-permute-start | bytes 786440 | tf_op jit(solution)/shard_map/ppermute | solution.py:408
  9.2 15.3 %collective-permute-start.2 = (f32[2,256,128]{2,1,0:T(8,128)S(1)}, f32[2,256,128]{2,1,0:T(8,128)S(1)}, u32[]{:S(2)}, u32[]{:S(2)}) collective-permute-start(f32[2,256,128]{2,1,0:T(8,128)S(1)} %get-tuple-element.69), channel_id=1, source_target_pairs={{0,10},{2,8},{4,14},{6,12},{8,2},{10,0},{12,6},{14,4},{16,26},{18,... | collective-permute-start | bytes 786440 | tf_op jit(solution)/shard_map/ppermute | solution.py:408
  12.3 15.2 %collective-permute-start.3 = (f32[2,256,128]{2,1,0:T(8,128)S(1)}, f32[2,256,128]{2,1,0:T(8,128)S(1)}, u32[]{:S(2)}, u32[]{:S(2)}) collective-permute-start(f32[2,256,128]{2,1,0:T(8,128)S(1)} %get-tuple-element.70), channel_id=1, source_target_pairs={{0,8},{2,10},{4,12},{6,14},{8,0},{10,2},{12,4},{14,6},{16,24},{18,... | collective-permute-start | bytes 786440 | tf_op jit(solution)/shard_map/ppermute | solution.py:408
  14.1 13.4 %collective-permute-start.4 = (f32[2,256,128]{2,1,0:T(8,128)S(1)}, f32[2,256,128]{2,1,0:T(8,128)S(1)}, u32[]{:S(2)}, u32[]{:S(2)}) collective-permute-start(f32[2,256,128]{2,1,0:T(8,128)S(1)} %get-tuple-element.71), channel_id=1, source_target_pairs={{0,6},{2,4},{4,2},{6,0},{8,14},{10,12},{12,10},{14,8},{16,22},{18,... | collective-permute-start | bytes 786440 | tf_op jit(solution)/shard_map/ppermute | solution.py:408
  16.9 1.3 %collective-permute-start.8 = (f32[256,128]{1,0:T(8,128)S(1)}, f32[256,128]{1,0:T(8,128)S(1)}, u32[]{:S(2)}, u32[]{:S(2)}) collective-permute-start(f32[256,128]{1,0:T(8,128)S(1)} %slice_bitcast_fusion.1), channel_id=1, source_target_pairs={{0,1},{1,0},{2,3},{3,2},{4,5},{5,4},{6,7},{7,6},{8,9},{9,8},{10,11... | collective-permute-start | bytes 393224 | tf_op jit(solution)/shard_map/ppermute | solution.py:412
  18.3 1.3 %collective-permute-start.9 = (f32[256,128]{1,0:T(8,128)S(1)}, f32[256,128]{1,0:T(8,128)S(1)}, u32[]{:S(2)}, u32[]{:S(2)}) collective-permute-start(f32[256,128]{1,0:T(8,128)S(1)} %slice_bitcast_fusion), channel_id=1, source_target_pairs={{0,1},{1,0},{2,3},{3,2},{4,5},{5,4},{6,7},{7,6},{8,9},{9,8},{10,11... | collective-permute-start | bytes 393224 | tf_op jit(solution)/shard_map/ppermute | solution.py:412
  19.6 15.5 %collective-permute-start = (f32[2,256,128]{2,1,0:T(8,128)S(1)}, f32[2,256,128]{2,1,0:T(8,128)S(1)}, u32[]{:S(2)}, u32[]{:S(2)}) collective-permute-start(f32[2,256,128]{2,1,0:T(8,128)S(1)} %get-tuple-element.67), channel_id=1, source_target_pairs={{0,14},{2,12},{4,10},{6,8},{8,6},{10,4},{12,2},{14,0},{16,30},{18,... | collective-permute-start | bytes 786440 | tf_op jit(solution)/shard_map/ppermute | solution.py:408
  27.5 1.4 %collective-permute-start.10 = (f32[256,128]{1,0:T(8,128)S(1)}, f32[256,128]{1,0:T(8,128)S(1)}, u32[]{:S(2)}, u32[]{:S(2)}) collective-permute-start(f32[256,128]{1,0:T(8,128)S(1)} %slice_bitcast_fusion.6), channel_id=1, source_target_pairs={{0,1},{1,0},{2,3},{3,2},{4,5},{5,4},{6,7},{7,6},{8,9},{9,8},{10,11... | collective-permute-start | bytes 393224 | tf_op jit(solution)/shard_map/ppermute | solution.py:412
  27.6 1.5 %collective-permute-start.11 = (f32[256,128]{1,0:T(8,128)S(1)}, f32[256,128]{1,0:T(8,128)S(1)}, u32[]{:S(2)}, u32[]{:S(2)}) collective-permute-start(f32[256,128]{1,0:T(8,128)S(1)} %slice_bitcast_fusion.5), channel_id=1, source_target_pairs={{0,1},{1,0},{2,3},{3,2},{4,5},{5,4},{6,7},{7,6},{8,9},{9,8},{10,11... | collective-permute-start | bytes 393224 | tf_op jit(solution)/shard_map/ppermute | solution.py:412
  28.2 1.4 %collective-permute-start.12 = (f32[256,128]{1,0:T(8,128)S(1)}, f32[256,128]{1,0:T(8,128)S(1)}, u32[]{:S(2)}, u32[]{:S(2)}) collective-permute-start(f32[256,128]{1,0:T(8,128)S(1)} %slice_bitcast_fusion.4), channel_id=1, source_target_pairs={{0,1},{1,0},{2,3},{3,2},{4,5},{5,4},{6,7},{7,6},{8,9},{9,8},{10,11... | collective-permute-start | bytes 393224 | tf_op jit(solution)/shard_map/ppermute | solution.py:412
  28.3 1.5 %collective-permute-start.13 = (f32[256,128]{1,0:T(8,128)S(1)}, f32[256,128]{1,0:T(8,128)S(1)}, u32[]{:S(2)}, u32[]{:S(2)}) collective-permute-start(f32[256,128]{1,0:T(8,128)S(1)} %slice_bitcast_fusion.3), channel_id=1, source_target_pairs={{0,1},{1,0},{2,3},{3,2},{4,5},{5,4},{6,7},{7,6},{8,9},{9,8},{10,11... | collective-permute-start | bytes 393224 | tf_op jit(solution)/shard_map/ppermute | solution.py:412
  28.9 22.6 %collective-permute-start.19 = (f32[256,512]{1,0:T(8,128)S(1)}, f32[256,512]{1,0:T(8,128)S(1)}, u32[]{:S(2)}, u32[]{:S(2)}) collective-permute-start(f32[256,512]{1,0:T(8,128)S(1)} %get-tuple-element.95.mine_ref), channel_id=1, source_target_pairs={{0,1},{1,0},{2,3},{3,2},{4,5},{5,4},{6,7},{7,6},{8,9},{9,8},{10,11... | collective-permute-start | bytes 1572872 | tf_op jit(solution)/shard_map/ppermute | solution.py:412
  35.2 1.4 %collective-permute-start.14 = (f32[256,128]{1,0:T(8,128)S(1)}, f32[256,128]{1,0:T(8,128)S(1)}, u32[]{:S(2)}, u32[]{:S(2)}) collective-permute-start(f32[256,128]{1,0:T(8,128)S(1)} %slice_bitcast_fusion.2), channel_id=1, source_target_pairs={{0,1},{1,0},{2,3},{3,2},{4,5},{5,4},{6,7},{7,6},{8,9},{9,8},{10,11... | collective-permute-start | bytes 393224 | tf_op jit(solution)/shard_map/ppermute | solution.py:412
  36.6 25.0 %copy-start.3 = (f32[1,16,16,256]{3,2,1,0:T(8,128)S(1)}, f32[1,16,16,256]{3,2,1,0:T(8,128)}, u32[]{:S(2)}) copy-start(f32[1,16,16,256]{3,2,1,0:T(8,128)} %param.5) | copy-start | bytes 786436
  38.9 3.9 %collective-permute-start.15 = (f32[40,128]{1,0:T(8,128)S(1)}, f32[40,128]{1,0:T(8,128)S(1)}, u32[]{:S(2)}, u32[]{:S(2)}) collective-permute-start(f32[40,128]{1,0:T(8,128)S(1)} %get-tuple-element.86), channel_id=1, source_target_pairs={{0,2},{2,0},{4,6},{6,4},{8,10},{10,8},{12,14},{14,12},{16,18},{18,... | collective-permute-start | bytes 61448 | tf_op jit(solution)/shard_map/ppermute | solution.py:16
  42.8 3.8 %collective-permute-start.16 = (f32[40,128]{1,0:T(8,128)S(1)}, f32[40,128]{1,0:T(8,128)S(1)}, u32[]{:S(2)}, u32[]{:S(2)}) collective-permute-start(f32[40,128]{1,0:T(8,128)S(1)} %add.51), channel_id=1, source_target_pairs={{0,4},{2,6},{4,0},{6,2},{8,12},{10,14},{12,8},{14,10},{16,20},{18,... | collective-permute-start | bytes 61448 | tf_op jit(solution)/shard_map/ppermute | solution.py:16
  46.6 3.8 %collective-permute-start.17 = (f32[40,128]{1,0:T(8,128)S(1)}, f32[40,128]{1,0:T(8,128)S(1)}, u32[]{:S(2)}, u32[]{:S(2)}) collective-permute-start(f32[40,128]{1,0:T(8,128)S(1)} %add.52), channel_id=1, source_target_pairs={{0,8},{2,10},{4,12},{6,14},{8,0},{10,2},{12,4},{14,6},{16,24},{18,... | collective-permute-start | bytes 61448 | tf_op jit(solution)/shard_map/ppermute | solution.py:16
  50.3 1.2 %collective-permute-start.18 = (f32[40,128]{1,0:T(8,128)S(1)}, f32[40,128]{1,0:T(8,128)S(1)}, u32[]{:S(2)}, u32[]{:S(2)}) collective-permute-start(f32[40,128]{1,0:T(8,128)S(1)} %add.53), channel_id=1, source_target_pairs={{0,1},{1,0},{2,3},{3,2},{4,5},{5,4},{6,7},{7,6},{8,9},{9,8},{10,11... | collective-permute-start | bytes 61448 | tf_op jit(solution)/shard_map/ppermute | solution.py:412
  53.1 29.0 %collective-permute-start.20 = (f32[1152,128]{1,0:T(8,128)S(1)}, f32[1152,128]{1,0:T(8,128)S(1)}, u32[]{:S(2)}, u32[]{:S(2)}) collective-permute-start(f32[1152,128]{1,0:T(8,128)S(1)} %get-tuple-element.90), channel_id=1, source_target_pairs={{0,16},{2,18},{4,20},{6,22},{8,24},{10,26},{12,28},{14,30},{16,0},... | collective-permute-start | bytes 1769480 | tf_op jit(solution)/shard_map/ppermute | solution.py:408
  55.7 18.5 %collective-permute-start.21 = (f32[192,128]{1,0:T(8,128)S(1)}, f32[192,128]{1,0:T(8,128)S(1)}, u32[]{:S(2)}, u32[]{:S(2)}) collective-permute-start(f32[192,128]{1,0:T(8,128)S(1)} %get-tuple-element.91), channel_id=1, source_target_pairs={{0,2},{2,0},{4,6},{6,4},{8,10},{10,8},{12,14},{14,12},{16,18},{18,... | collective-permute-start | bytes 294920 | tf_op jit(solution)/shard_map/ppermute | solution.py:408
  57.0 17.2 %collective-permute-start.22 = (f32[128,128]{1,0:T(8,128)S(1)}, f32[128,128]{1,0:T(8,128)S(1)}, u32[]{:S(2)}, u32[]{:S(2)}) collective-permute-start(f32[128,128]{1,0:T(8,128)S(1)} %get-tuple-element.92), channel_id=1, source_target_pairs={{0,6},{2,4},{4,2},{6,0},{8,14},{10,12},{12,10},{14,8},{16,22},{18,... | collective-permute-start | bytes 196616 | tf_op jit(solution)/shard_map/ppermute | solution.py:408
  58.5 15.7 %collective-permute-start.23 = (f32[128,128]{1,0:T(8,128)S(1)}, f32[128,128]{1,0:T(8,128)S(1)}, u32[]{:S(2)}, u32[]{:S(2)}) collective-permute-start(f32[128,128]{1,0:T(8,128)S(1)} %get-tuple-element.93), channel_id=1, source_target_pairs={{0,10},{2,8},{4,14},{6,12},{8,2},{10,0},{12,6},{14,4},{16,26},{18,... | collective-permute-start | bytes 196616 | tf_op jit(solution)/shard_map/ppermute | solution.py:408
  60.2 14.1 %collective-permute-start.24 = (f32[128,128]{1,0:T(8,128)S(1)}, f32[128,128]{1,0:T(8,128)S(1)}, u32[]{:S(2)}, u32[]{:S(2)}) collective-permute-start(f32[128,128]{1,0:T(8,128)S(1)} %get-tuple-element.94), channel_id=1, source_target_pairs={{0,14},{2,12},{4,10},{6,8},{8,6},{10,4},{12,2},{14,0},{16,30},{18,... | collective-permute-start | bytes 196616 | tf_op jit(solution)/shard_map/ppermute | solution.py:408
  61.6 39.7 %copy-start.1 = (f32[1,16,16,512]{3,2,1,0:T(8,128)S(1)}, f32[1,16,16,512]{3,2,1,0:T(8,128)}, u32[]{:S(2)}) copy-start(f32[1,16,16,512]{3,2,1,0:T(8,128)} %param.3) | copy-start | bytes 1572868
  82.3 6.1 %collective-permute-start.25 = (f32[264,128]{1,0:T(8,128)S(1)}, f32[264,128]{1,0:T(8,128)S(1)}, u32[]{:S(2)}, u32[]{:S(2)}) collective-permute-start(f32[264,128]{1,0:T(8,128)S(1)} %get-tuple-element.102), channel_id=1, source_target_pairs={{0,12},{2,14},{4,8},{6,10},{8,4},{10,6},{12,0},{14,2},{16,28},{18,... | collective-permute-start | bytes 405512 | tf_op jit(solution)/shard_map/ppermute | solution.py:408
  83.8 17.5 %collective-permute-start.34 = (f32[256,512]{1,0:T(8,128)S(1)}, f32[256,512]{1,0:T(8,128)S(1)}, u32[]{:S(2)}, u32[]{:S(2)}) collective-permute-start(f32[256,512]{1,0:T(8,128)S(1)} %get-tuple-element.124), channel_id=1, source_target_pairs={{0,1},{1,0},{2,3},{3,2},{4,5},{5,4},{6,7},{7,6},{8,9},{9,8},{10,11... | collective-permute-start | bytes 1572872 | tf_op jit(solution)/shard_map/ppermute | solution.py:412
  83.8 5.7 %collective-permute-start.26 = (f32[200,128]{1,0:T(8,128)S(1)}, f32[200,128]{1,0:T(8,128)S(1)}, u32[]{:S(2)}, u32[]{:S(2)}) collective-permute-start(f32[200,128]{1,0:T(8,128)S(1)} %get-tuple-element.105), channel_id=1, source_target_pairs={{0,2},{2,0},{4,6},{6,4},{8,10},{10,8},{12,14},{14,12},{16,18},{18,... | collective-permute-start | bytes 307208 | tf_op jit(solution)/shard_map/ppermute | solution.py:408
  84.5 7.1 %collective-permute-start.27 = (f32[264,128]{1,0:T(8,128)S(1)}, f32[264,128]{1,0:T(8,128)S(1)}, u32[]{:S(2)}, u32[]{:S(2)}) collective-permute-start(f32[264,128]{1,0:T(8,128)S(1)} %get-tuple-element.108), channel_id=1, source_target_pairs={{0,4},{2,6},{4,0},{6,2},{8,12},{10,14},{12,8},{14,10},{16,20},{18,... | collective-permute-start | bytes 405512 | tf_op jit(solution)/shard_map/ppermute | solution.py:408
  85.4 7.8 %collective-permute-start.28 = (f32[136,128]{1,0:T(8,128)S(1)}, f32[136,128]{1,0:T(8,128)S(1)}, u32[]{:S(2)}, u32[]{:S(2)}) collective-permute-start(f32[136,128]{1,0:T(8,128)S(1)} %get-tuple-element.111), channel_id=1, source_target_pairs={{0,10},{2,8},{4,14},{6,12},{8,2},{10,0},{12,6},{14,4},{16,26},{18,... | collective-permute-start | bytes 208904 | tf_op jit(solution)/shard_map/ppermute | solution.py:408
  88.4 5.0 %collective-permute-start.29 = (f32[264,128]{1,0:T(8,128)S(1)}, f32[264,128]{1,0:T(8,128)S(1)}, u32[]{:S(2)}, u32[]{:S(2)}) collective-permute-start(f32[264,128]{1,0:T(8,128)S(1)} %get-tuple-element.114), channel_id=1, source_target_pairs={{0,8},{2,10},{4,12},{6,14},{8,0},{10,2},{12,4},{14,6},{16,24},{18,... | collective-permute-start | bytes 405512 | tf_op jit(solution)/shard_map/ppermute | solution.py:408
  89.5 5.2 %collective-permute-start.30 = (f32[136,128]{1,0:T(8,128)S(1)}, f32[136,128]{1,0:T(8,128)S(1)}, u32[]{:S(2)}, u32[]{:S(2)}) collective-permute-start(f32[136,128]{1,0:T(8,128)S(1)} %get-tuple-element.117), channel_id=1, source_target_pairs={{0,6},{2,4},{4,2},{6,0},{8,14},{10,12},{12,10},{14,8},{16,22},{18,... | collective-permute-start | bytes 208904 | tf_op jit(solution)/shard_map/ppermute | solution.py:408
  91.7 6.1 %collective-permute-start.31 = (f32[136,128]{1,0:T(8,128)S(1)}, f32[136,128]{1,0:T(8,128)S(1)}, u32[]{:S(2)}, u32[]{:S(2)}) collective-permute-start(f32[136,128]{1,0:T(8,128)S(1)} %get-tuple-element.120), channel_id=1, source_target_pairs={{0,14},{2,12},{4,10},{6,8},{8,6},{10,4},{12,2},{14,0},{16,30},{18,... | collective-permute-start | bytes 208904 | tf_op jit(solution)/shard_map/ppermute | solution.py:408
  97.8 1.2 %collective-permute-start.32 = (f32[8,128]{1,0:T(8,128)S(1)}, f32[8,128]{1,0:T(8,128)S(1)}, u32[]{:S(2)}, u32[]{:S(2)}) collective-permute-start(f32[8,128]{1,0:T(8,128)S(1)} %slice_add_fusion), channel_id=1, source_target_pairs={{0,1},{1,0},{2,3},{3,2},{4,5},{5,4},{6,7},{7,6},{8,9},{9,8},{10,11... | collective-permute-start | bytes 12296 | tf_op jit(solution)/shard_map/ppermute | solution.py:412
  99.0 4.5 %collective-permute-start.33 = (f32[8,128]{1,0:T(8,128)S(1)}, f32[8,128]{1,0:T(8,128)S(1)}, u32[]{:S(2)}, u32[]{:S(2)}) collective-permute-start(f32[8,128]{1,0:T(8,128)S(1)} %add.62), channel_id=1, source_target_pairs={{0,16},{2,18},{4,20},{6,22},{8,24},{10,26},{12,28},{14,30},{16,0},... | collective-permute-start | bytes 12296 | tf_op jit(solution)/shard_map/ppermute | solution.py:408

commit v4 on v3

--- a/solution.py
+++ b/solution.py
@@ -416,11 +416,11 @@
     return jax.ShapeDtypeStruct(shape, jnp.float32)
 
 
-ORDER = (1, 6, 2, 5, 4, 3, 7)
+ORDER = (1, 6, 2, 5, 3, 4, 7)
 EARLY = (1, 3, 5, 7)
 LAST = (6, 1, 2, 5, 4, 3, 7)
 COST = 10**10
-BATCHES = ((0, 1, 6), (2, 5, 4, 3), (7,))
+BATCHES = ((0, 1, 6), (2, 5), (3, 4), (7,))
 
 
 def spread(messages):
@@ -490,8 +490,8 @@
         )(*operands)
         known += batch
     gram = products
-    for bit in range(3):
-        gram = gram + from_partner(gram, "dp", bit)
+    gram = gram + exchange(gram, 1) + exchange(gram, 2) + exchange(gram, 3)
+    gram = gram + exchange(gram, 4)
     gram = gram + swap_cores(gram)
 
     theirs = swap_cores(activity)

time: 105 us -> 102 us (0.971)
  waiting for transfers between devices: 34.7 us -> 31.7 us
    ppermute x3 -> x0, waiting for transfers between devices: 7.18 us -> none  [from_partner(): lax.ppermute(x, axis, [(i, i ^ 1 << apart) for i in range(lax.axis_size(a...]
    ppermute x20 -> x24, waiting for transfers between devices: 20.8 us -> 27.1 us  [exchange(): return lax.ppermute(x, 'dp', [(i, i ^ other) for i in range(size)])]
    ppermute x3 -> x0, starting transfers between devices: 4.25 us -> none  [from_partner(): lax.ppermute(x, axis, [(i, i ^ 1 << apart) for i in range(lax.axis_size(a...]
    ppermute x20 -> x24, starting transfers between devices: 33.1 us -> 37.1 us  [exchange(): return lax.ppermute(x, 'dp', [(i, i ^ other) for i in range(size)])]
    ppermute x12, waiting for transfers between devices: 6.71 us -> 4.61 us  [swap_cores(): return lax.ppermute(x, 'mp', [(0, 1), (1, 0)])]
    pallas_call x3 -> x4, Pallas kernels: 10.7 us -> 11.2 us  [local_cube(): pl.pallas_call(functools.partial(leaf_kernel, extent, images, known, batc...]
  transfers between devices with their start and end apart: 35 -> 36, of which waited for: 20 -> 17; matrix products, arithmetic and copies ran while one was open for 1% -> 1% of each run, Pallas kernels for 22% -> 24%
where the time goes in v4:
time: 102 us; the launch traced here: 101 us
  starting transfers between devices  38.7 us (38%)
  waiting for transfers between devices  31.7 us (31%)
  Pallas kernels  27 us (26%)
  local copies, waits for them, and re-layouts  2.07 us (2%)
  other arithmetic  1.07 us (1%)
    ppermute x24, starting transfers between devices, exchange(): return lax.ppermute(x, 'dp', [(i, i ^ other) for i in range(size)])  37.1 us
    ppermute x24, waiting for transfers between devices, exchange(): return lax.ppermute(x, 'dp', [(i, i ^ other) for i in range(size)])  27.1 us
    pallas_call x1, Pallas kernels, local_cube(): pl.pallas_call(functools.partial(image_kernel, extent), grid=(taps,), in_...  12.6 us
    pallas_call x4, Pallas kernels, local_cube(): pl.pallas_call(functools.partial(leaf_kernel, extent, images, known, batc...  11.2 us
    ppermute x12, waiting for transfers between devices, swap_cores(): return lax.ppermute(x, 'mp', [(0, 1), (1, 0)])  4.61 us
  transfers between devices with their start and end apart: 36, of which 17 were waited for; matrix products, arithmetic and copies ran while one was open for 1% of the time, Pallas kernels for 24%

profile of v4, /device:TPU:0, one launch (start us, length us, event | category | flops | bytes accessed | tf_op | source)
XLA Modules:
  0.0 101.5 jit_solution(2094190697806849110)
XLA Ops:
  0.6 1.0 %copy-done = f32[1,16,16,512]{3,2,1,0:T(8,128)S(1)} copy-done((f32[1,16,16,512]{3,2,1,0:T(8,128)S(1)}, f32[1,16,16,512]{3,2,1,0:T(8,128)}, u32[]{:S(2)}) %copy-start) | copy-done | bytes 524312
  1.7 0.9 copy-done.2
  3.0 3.0 %collective-permute-start.5 = (f32[2,256,128]{2,1,0:T(8,128)S(1)}, f32[2,256,128]{2,1,0:T(8,128)S(1)}, u32[]{:S(2)}, u32[]{:S(2)}) collective-permute-start(f32[2,256,128]{2,1,0:T(8,128)S(1)} %get-tuple-element.76), channel_id=1, source_target_pairs={{0,2},{2,0},{4,6},{6,4},{8,10},{10,8},{12,14},{14,12},{16,18},{18,... | collective-permute-start | bytes 786440 | tf_op jit(solution)/shard_map/ppermute | solution.py:408
  6.0 2.5 %collective-permute-start.6 = (f32[2,256,128]{2,1,0:T(8,128)S(1)}, f32[2,256,128]{2,1,0:T(8,128)S(1)}, u32[]{:S(2)}, u32[]{:S(2)}) collective-permute-start(f32[2,256,128]{2,1,0:T(8,128)S(1)} %get-tuple-element.77), channel_id=1, source_target_pairs={{0,12},{2,14},{4,8},{6,10},{8,4},{10,6},{12,0},{14,2},{16,28},{18,... | collective-permute-start | bytes 786440 | tf_op jit(solution)/shard_map/ppermute | solution.py:408
  8.6 0.6 collective-permute-start.3
  9.2 3.1 %collective-permute-done.5.refs_1_ = f32[2,256,128]{2,1,0:T(8,128)S(1)} collective-permute-done((f32[2,256,128]{2,1,0:T(8,128)S(1)}, f32[2,256,128]{2,1,0:T(8,128)S(1)}, u32[]{:S(2)}, u32[]{:S(2)}) %collective-permute-start.5) | collective-permute-done | bytes 262176 | tf_op jit(solution)/shard_map/ppermute | solution.py:408
  12.4 3.7 %collective-permute-done.6.refs_2_ = f32[2,256,128]{2,1,0:T(8,128)S(1)} collective-permute-done((f32[2,256,128]{2,1,0:T(8,128)S(1)}, f32[2,256,128]{2,1,0:T(8,128)S(1)}, u32[]{:S(2)}, u32[]{:S(2)}) %collective-permute-start.6) | collective-permute-done | bytes 262176 | tf_op jit(solution)/shard_map/ppermute | solution.py:408
  16.2 1.6 %collective-permute-start.1 = (f32[2,256,128]{2,1,0:T(8,128)S(1)}, f32[2,256,128]{2,1,0:T(8,128)S(1)}, u32[]{:S(2)}, u32[]{:S(2)}) collective-permute-start(f32[2,256,128]{2,1,0:T(8,128)S(1)} %get-tuple-element.71), channel_id=1, source_target_pairs={{0,6},{2,4},{4,2},{6,0},{8,14},{10,12},{12,10},{14,8},{16,22},{18,... | collective-permute-start | bytes 786440 | tf_op jit(solution)/shard_map/ppermute | solution.py:408
  17.8 1.6 %collective-permute-start.2 = (f32[2,256,128]{2,1,0:T(8,128)S(1)}, f32[2,256,128]{2,1,0:T(8,128)S(1)}, u32[]{:S(2)}, u32[]{:S(2)}) collective-permute-start(f32[2,256,128]{2,1,0:T(8,128)S(1)} %get-tuple-element.72), channel_id=1, source_target_pairs={{0,8},{2,10},{4,12},{6,14},{8,0},{10,2},{12,4},{14,6},{16,24},{18,... | collective-permute-start | bytes 786440 | tf_op jit(solution)/shard_map/ppermute | solution.py:408
  19.4 3.1 %leaf.4 = (f32[8,2304,128]{2,1,0:T(8,128)S(1)}, f32[64,128]{1,0:T(8,128)S(1)}) custom-call(f32[2,256,128]{2,1,0:T(8,128)S(1)} %get-tuple-element.75.refs_0_, f32[2,256,128]{2,1,0:T(8,128)S(1)} %collective-permute-done.5.refs_1_, f32[2,256,128]{2,1,0:T(8,128)S(1)} %collective-permute-done.6.refs_2_, f32[256,128]{1,0:T(8,128)S(1)} %collective-permute-done.7.refs_3_, ...), custom_call_target="tpu_custom_call" | custom-call | flops 1 | bytes 1 | tf_op jit(solution)/shard_map/leaf/pallas_call | solution.py:477
  22.6 0.6 collective-permute-start.11
  23.2 1.3 %collective-permute-start = (f32[2,256,128]{2,1,0:T(8,128)S(1)}, f32[2,256,128]{2,1,0:T(8,128)S(1)}, u32[]{:S(2)}, u32[]{:S(2)}) collective-permute-start(f32[2,256,128]{2,1,0:T(8,128)S(1)} %get-tuple-element.70), channel_id=1, source_target_pairs={{0,14},{2,12},{4,10},{6,8},{8,6},{10,4},{12,2},{14,0},{16,30},{18,... | collective-permute-start | bytes 786440 | tf_op jit(solution)/shard_map/ppermute | solution.py:408
  24.4 2.7 %leaf.5 = (f32[8,2304,128]{2,1,0:T(8,128)S(1)}, f32[64,128]{1,0:T(8,128)S(1)}) custom-call(f32[2,256,128]{2,1,0:T(8,128)S(1)} %collective-permute-done.3.refs_0_, f32[2,256,128]{2,1,0:T(8,128)S(1)} %collective-permute-done.4.refs_1_, f32[256,128]{1,0:T(8,128)S(1)} %collective-permute-done.10.refs_2_, ...), custom_call_target="tpu_custom_call", output_to_operand_aliasing={{0}: (5, {})} | custom-call | flops 1 | bytes 1 | tf_op jit(solution)/shard_map/leaf/pallas_call | solution.py:477
  27.9 0.7 collective-permute-done.12.refs_2_
  28.8 3.2 %leaf.6 = (f32[8,2304,128]{2,1,0:T(8,128)S(1)}, f32[64,128]{1,0:T(8,128)S(1)}) custom-call(f32[2,256,128]{2,1,0:T(8,128)S(1)} %collective-permute-done.1.refs_0_, f32[2,256,128]{2,1,0:T(8,128)S(1)} %collective-permute-done.2.refs_1_, f32[256,128]{1,0:T(8,128)S(1)} %collective-permute-done.12.refs_2_, ...), custom_call_target="tpu_custom_call", output_to_operand_aliasing={{0}: (5, {})} | custom-call | flops 1 | bytes 1 | tf_op jit(solution)/shard_map/leaf/pallas_call | solution.py:477
  32.1 1.2 %collective-permute-done.refs_0_ = f32[2,256,128]{2,1,0:T(8,128)S(1)} collective-permute-done((f32[2,256,128]{2,1,0:T(8,128)S(1)}, f32[2,256,128]{2,1,0:T(8,128)S(1)}, u32[]{:S(2)}, u32[]{:S(2)}) %collective-permute-start) | collective-permute-done | bytes 262176 | tf_op jit(solution)/shard_map/ppermute | solution.py:408
  33.3 1.3 %collective-permute-done.14.refs_1_ = f32[256,128]{1,0:T(8,128)S(1)} collective-permute-done((f32[256,128]{1,0:T(8,128)S(1)}, f32[256,128]{1,0:T(8,128)S(1)}, u32[]{:S(2)}, u32[]{:S(2)}) %collective-permute-start.14) | collective-permute-done | bytes 131104 | tf_op jit(solution)/shard_map/ppermute | solution.py:412
  34.7 2.3 %leaf.7 = (f32[8,2304,128]{2,1,0:T(8,128)S(1)}, f32[40,128]{1,0:T(8,128)S(1)}) custom-call(f32[2,256,128]{2,1,0:T(8,128)S(1)} %collective-permute-done.refs_0_, f32[256,128]{1,0:T(8,128)S(1)} %collective-permute-done.14.refs_1_, f32[64,128]{1,0:T(8,128)S(1)} %get-tuple-element.90.refs_2_, ...), custom_call_target="tpu_custom_call", output_to_operand_aliasing={{0}: (3, {})} | custom-call | flops 1 | bytes 1 | tf_op jit(solution)/shard_map/leaf/pallas_call | solution.py:477
  36.9 1.6 %collective-permute-start.15 = (f32[40,128]{1,0:T(8,128)S(1)}, f32[40,128]{1,0:T(8,128)S(1)}, u32[]{:S(2)}, u32[]{:S(2)}) collective-permute-start(f32[40,128]{1,0:T(8,128)S(1)} %get-tuple-element.92), channel_id=1, source_target_pairs={{0,2},{2,0},{4,6},{6,4},{8,10},{10,8},{12,14},{14,12},{16,18},{18,... | collective-permute-start | bytes 61448 | tf_op jit(solution)/shard_map/ppermute | solution.py:408
  39.0 1.5 %collective-permute-start.17 = (f32[40,128]{1,0:T(8,128)S(1)}, f32[40,128]{1,0:T(8,128)S(1)}, u32[]{:S(2)}, u32[]{:S(2)}) collective-permute-start(f32[40,128]{1,0:T(8,128)S(1)} %get-tuple-element.92), channel_id=1, source_target_pairs={{0,6},{2,4},{4,2},{6,0},{8,14},{10,12},{12,10},{14,8},{16,22},{18,... | collective-permute-start | bytes 61448 | tf_op jit(solution)/shard_map/ppermute | solution.py:408
  40.8 1.7 %collective-permute-done.16 = f32[40,128]{1,0:T(8,128)S(1)} collective-permute-done((f32[40,128]{1,0:T(8,128)S(1)}, f32[40,128]{1,0:T(8,128)S(1)}, u32[]{:S(2)}, u32[]{:S(2)}) %collective-permute-start.16) | collective-permute-done | bytes 20512 | tf_op jit(solution)/shard_map/ppermute | solution.py:408
  42.5 1.2 %collective-permute-done.17 = f32[40,128]{1,0:T(8,128)S(1)} collective-permute-done((f32[40,128]{1,0:T(8,128)S(1)}, f32[40,128]{1,0:T(8,128)S(1)}, u32[]{:S(2)}, u32[]{:S(2)}) %collective-permute-start.17) | collective-permute-done | bytes 20512 | tf_op jit(solution)/shard_map/ppermute | solution.py:408
  43.7 1.1 %collective-permute-start.18 = (f32[40,128]{1,0:T(8,128)S(1)}, f32[40,128]{1,0:T(8,128)S(1)}, u32[]{:S(2)}, u32[]{:S(2)}) collective-permute-start(f32[40,128]{1,0:T(8,128)S(1)} %add_add_fusion), channel_id=1, source_target_pairs={{0,8},{2,10},{4,12},{6,14},{8,0},{10,2},{12,4},{14,6},{16,24},{18,... | collective-permute-start | bytes 61448 | tf_op jit(solution)/shard_map/ppermute | solution.py:408
  44.8 2.7 %collective-permute-done.18 = f32[40,128]{1,0:T(8,128)S(1)} collective-permute-done((f32[40,128]{1,0:T(8,128)S(1)}, f32[40,128]{1,0:T(8,128)S(1)}, u32[]{:S(2)}, u32[]{:S(2)}) %collective-permute-start.18) | collective-permute-done | bytes 20512 | tf_op jit(solution)/shard_map/ppermute | solution.py:408
  47.5 1.2 %collective-permute-done.19 = f32[40,128]{1,0:T(8,128)S(1)} collective-permute-done((f32[40,128]{1,0:T(8,128)S(1)}, f32[40,128]{1,0:T(8,128)S(1)}, u32[]{:S(2)}, u32[]{:S(2)}) %collective-permute-start.19) | collective-permute-done | bytes 20512 | tf_op jit(solution)/shard_map/ppermute | solution.py:412
  48.7 1.5 %combine.1 = (f32[1152,128]{1,0:T(8,128)S(1)}, f32[1152,128]{1,0:T(8,128)S(1)}, f32[192,128]{1,0:T(8,128)S(1)}, f32[128,128]{1,0:T(8,128)S(1)}, f32[128,128]{1,0:T(8,128)S(1)}, /*index=5*/f32[128,128]{1,0:T(8,128)S(1)}) custom-call(f32[40,128]{1,0:T(8,128)S(1)} %add.58.gram_ref, f32[8,2304,128]{2,1,0:T(8,128)S(1)} %get-tuple-element.95.leaf_ref), custom_call_target="tpu_custom_call" | custom-call | flops 1 | bytes 1 | tf_op jit(solution)/shard_map/combine/pallas_call | solution.py:499
  50.3 2.7 %collective-permute-start.21 = (f32[1152,128]{1,0:T(8,128)S(1)}, f32[1152,128]{1,0:T(8,128)S(1)}, u32[]{:S(2)}, u32[]{:S(2)}) collective-permute-start(f32[1152,128]{1,0:T(8,128)S(1)} %get-tuple-element.96), channel_id=1, source_target_pairs={{0,16},{2,18},{4,20},{6,22},{8,24},{10,26},{12,28},{14,30},{16,0},... | collective-permute-start | bytes 1769480 | tf_op jit(solution)/shard_map/ppermute | solution.py:408
  52.9 1.0 collective-permute-start.22
  53.9 2.0 %collective-permute-start.23 = (f32[128,128]{1,0:T(8,128)S(1)}, f32[128,128]{1,0:T(8,128)S(1)}, u32[]{:S(2)}, u32[]{:S(2)}) collective-permute-start(f32[128,128]{1,0:T(8,128)S(1)} %get-tuple-element.98), channel_id=1, source_target_pairs={{0,6},{2,4},{4,2},{6,0},{8,14},{10,12},{12,10},{14,8},{16,22},{18,... | collective-permute-start | bytes 196616 | tf_op jit(solution)/shard_map/ppermute | solution.py:408
  55.9 1.0 collective-permute-start.24
  56.9 1.9 %collective-permute-start.25 = (f32[128,128]{1,0:T(8,128)S(1)}, f32[128,128]{1,0:T(8,128)S(1)}, u32[]{:S(2)}, u32[]{:S(2)}) collective-permute-start(f32[128,128]{1,0:T(8,128)S(1)} %get-tuple-element.100), channel_id=1, source_target_pairs={{0,14},{2,12},{4,10},{6,8},{8,6},{10,4},{12,2},{14,0},{16,30},{18,... | collective-permute-start | bytes 196616 | tf_op jit(solution)/shard_map/ppermute | solution.py:408
  58.8 12.6 %image.1 = (f32[256,256]{1,0:T(8,128)}, f32[256,512]{1,0:T(8,128)S(1)}, f32[256,512]{1,0:T(8,128)S(1)}) custom-call(f32[256,512]{1,0:T(8,128)S(1)} %get-tuple-element.101.mine_ref, f32[256,512]{1,0:T(8,128)S(1)} %collective-permute-done.20.theirs_ref, f32[256,256]{1,0:T(8,128)S(1)} %bitcast.25, f32[9,256,1024]{2,1,0:T(8,128)} %bitcast.28), custom_call_target="tpu_custom_call" | custom-call | flops 10000000000 | bytes 1 | tf_op jit(solution)/shard_map/image/pallas_call | solution.py:512
  71.5 7.8 %collective-permute-done.21.far_ref = f32[1152,128]{1,0:T(8,128)S(1)} collective-permute-done((f32[1152,128]{1,0:T(8,128)S(1)}, f32[1152,128]{1,0:T(8,128)S(1)}, u32[]{:S(2)}, u32[]{:S(2)}) %collective-permute-start.21) | collective-permute-done | bytes 589856 | tf_op jit(solution)/shard_map/ppermute | solution.py:408
  79.5 0.7 collective-permute-start.26
  80.2 1.1 %collective-permute-start.27 = (f32[200,128]{1,0:T(8,128)S(1)}, f32[200,128]{1,0:T(8,128)S(1)}, u32[]{:S(2)}, u32[]{:S(2)}) collective-permute-start(f32[200,128]{1,0:T(8,128)S(1)} %get-tuple-element.111), channel_id=1, source_target_pairs={{0,2},{2,0},{4,6},{6,4},{8,10},{10,8},{12,14},{14,12},{16,18},{18,... | collective-permute-start | bytes 307208 | tf_op jit(solution)/shard_map/ppermute | solution.py:408
  81.3 1.4 %collective-permute-start.28 = (f32[264,128]{1,0:T(8,128)S(1)}, f32[264,128]{1,0:T(8,128)S(1)}, u32[]{:S(2)}, u32[]{:S(2)}) collective-permute-start(f32[264,128]{1,0:T(8,128)S(1)} %get-tuple-element.114), channel_id=1, source_target_pairs={{0,4},{2,6},{4,0},{6,2},{8,12},{10,14},{12,8},{14,10},{16,20},{18,... | collective-permute-start | bytes 405512 | tf_op jit(solution)/shard_map/ppermute | solution.py:408
  82.7 1.8 %collective-permute-start.29 = (f32[136,128]{1,0:T(8,128)S(1)}, f32[136,128]{1,0:T(8,128)S(1)}, u32[]{:S(2)}, u32[]{:S(2)}) collective-permute-start(f32[136,128]{1,0:T(8,128)S(1)} %get-tuple-element.117), channel_id=1, source_target_pairs={{0,10},{2,8},{4,14},{6,12},{8,2},{10,0},{12,6},{14,4},{16,26},{18,... | collective-permute-start | bytes 208904 | tf_op jit(solution)/shard_map/ppermute | solution.py:408
  84.5 1.1 %collective-permute-done.26.refs_6_ = f32[264,128]{1,0:T(8,128)S(1)} collective-permute-done((f32[264,128]{1,0:T(8,128)S(1)}, f32[264,128]{1,0:T(8,128)S(1)}, u32[]{:S(2)}, u32[]{:S(2)}) %collective-permute-start.26) | collective-permute-done | bytes 135200 | tf_op jit(solution)/shard_map/ppermute | solution.py:408
  85.6 0.7 collective-permute-start.30
  86.3 2.3 %collective-permute-start.31 = (f32[136,128]{1,0:T(8,128)S(1)}, f32[136,128]{1,0:T(8,128)S(1)}, u32[]{:S(2)}, u32[]{:S(2)}) collective-permute-start(f32[136,128]{1,0:T(8,128)S(1)} %get-tuple-element.123), channel_id=1, source_target_pairs={{0,6},{2,4},{4,2},{6,0},{8,14},{10,12},{12,10},{14,8},{16,22},{18,... | collective-permute-start | bytes 208904 | tf_op jit(solution)/shard_map/ppermute | solution.py:408
  88.5 2.3 %collective-permute-start.32 = (f32[136,128]{1,0:T(8,128)S(1)}, f32[136,128]{1,0:T(8,128)S(1)}, u32[]{:S(2)}, u32[]{:S(2)}) collective-permute-start(f32[136,128]{1,0:T(8,128)S(1)} %get-tuple-element.126), channel_id=1, source_target_pairs={{0,14},{2,12},{4,10},{6,8},{8,6},{10,4},{12,2},{14,0},{16,30},{18,... | collective-permute-start | bytes 208904 | tf_op jit(solution)/shard_map/ppermute | solution.py:408
  90.9 0.6 collective-permute-done.31.refs_3_
  91.5 3.2 %collective-permute-done.32.refs_7_ = f32[136,128]{1,0:T(8,128)S(1)} collective-permute-done((f32[136,128]{1,0:T(8,128)S(1)}, f32[136,128]{1,0:T(8,128)S(1)}, u32[]{:S(2)}, u32[]{:S(2)}) %collective-permute-start.32) | collective-permute-done | bytes 69664 | tf_op jit(solution)/shard_map/ppermute | solution.py:408
  94.6 1.2 %collective-permute-done.33 = f32[8,128]{1,0:T(8,128)S(1)} collective-permute-done((f32[8,128]{1,0:T(8,128)S(1)}, f32[8,128]{1,0:T(8,128)S(1)}, u32[]{:S(2)}, u32[]{:S(2)}) %collective-permute-start.33) | collective-permute-done | bytes 4128 | tf_op jit(solution)/shard_map/ppermute | solution.py:412
  95.8 3.0 %collective-permute-start.34 = (f32[8,128]{1,0:T(8,128)S(1)}, f32[8,128]{1,0:T(8,128)S(1)}, u32[]{:S(2)}, u32[]{:S(2)}) collective-permute-start(f32[8,128]{1,0:T(8,128)S(1)} %add.66), channel_id=1, source_target_pairs={{0,16},{2,18},{4,20},{6,22},{8,24},{10,26},{12,28},{14,30},{16,0},... | collective-permute-start | bytes 12296 | tf_op jit(solution)/shard_map/ppermute | solution.py:408
  98.9 1.0 %fusion.4 = f32[256,512]{1,0:T(8,128)} fusion(f32[256,512]{1,0:T(8,128)S(1)} %get-tuple-element.129, f32[256,512]{1,0:T(8,128)S(1)} %collective-permute-done.35, f32[1,16,16,512]{3,2,1,0:T(8,128)S(1)} %copy-done.1), kind=kLoop, calls=%fused_computation.5 | loop fusion | flops 1310720 | bytes 2097152 | tf_op jit(solution)/shard_map/mul | solution.py:530
  99.9 0.6 collective-permute-done.34
  100.4 1.0 %finish.1 = f32[576,256]{1,0:T(8,128)} custom-call(f32[8,128]{1,0:T(8,128)S(1)} %add.67.moments_ref, f32[392,128]{1,0:T(8,128)S(1)} %get-tuple-element.107.refs_0_, f32[200,128]{1,0:T(8,128)S(1)} %collective-permute-done.27.refs_1_, f32[264,128]{1,0:T(8,128)S(1)} %collective-permute-done.28.refs_2_, f32[136,128]{1,0:T(8,128)S(1)} %collective-permute-done.31.refs_3_, ...), custom_call_target="tpu_custom_call" | custom-call | flops 1 | bytes 1 | tf_op jit(solution)/shard_map/finish/pallas_call | solution.py:554
  (63 shorter events, 2.9 us)
Async XLA Ops:
  0.6 1.0 %copy-start = (f32[1,16,16,512]{3,2,1,0:T(8,128)S(1)}, f32[1,16,16,512]{3,2,1,0:T(8,128)}, u32[]{:S(2)}) copy-start(f32[1,16,16,512]{3,2,1,0:T(8,128)} %param.3) | copy-start | bytes 1572868
  1.7 0.9 copy-start.2
  3.0 9.3 %collective-permute-start.5 = (f32[2,256,128]{2,1,0:T(8,128)S(1)}, f32[2,256,128]{2,1,0:T(8,128)S(1)}, u32[]{:S(2)}, u32[]{:S(2)}) collective-permute-start(f32[2,256,128]{2,1,0:T(8,128)S(1)} %get-tuple-element.76), channel_id=1, source_target_pairs={{0,2},{2,0},{4,6},{6,4},{8,10},{10,8},{12,14},{14,12},{16,18},{18,... | collective-permute-start | bytes 786440 | tf_op jit(solution)/shard_map/ppermute | solution.py:408
  6.0 10.1 %collective-permute-start.6 = (f32[2,256,128]{2,1,0:T(8,128)S(1)}, f32[2,256,128]{2,1,0:T(8,128)S(1)}, u32[]{:S(2)}, u32[]{:S(2)}) collective-permute-start(f32[2,256,128]{2,1,0:T(8,128)S(1)} %get-tuple-element.77), channel_id=1, source_target_pairs={{0,12},{2,14},{4,8},{6,10},{8,4},{10,6},{12,0},{14,2},{16,28},{18,... | collective-permute-start | bytes 786440 | tf_op jit(solution)/shard_map/ppermute | solution.py:408
  8.5 7.7 %collective-permute-start.7 = (f32[256,128]{1,0:T(8,128)S(1)}, f32[256,128]{1,0:T(8,128)S(1)}, u32[]{:S(2)}, u32[]{:S(2)}) collective-permute-start(f32[256,128]{1,0:T(8,128)S(1)} %slice_bitcast_fusion.7), channel_id=1, source_target_pairs={{0,1},{1,0},{2,3},{3,2},{4,5},{5,4},{6,7},{7,6},{8,9},{9,8},{10,11... | collective-permute-start | bytes 393224 | tf_op jit(solution)/shard_map/ppermute | solution.py:412
  8.6 13.9 %collective-permute-start.3 = (f32[2,256,128]{2,1,0:T(8,128)S(1)}, f32[2,256,128]{2,1,0:T(8,128)S(1)}, u32[]{:S(2)}, u32[]{:S(2)}) collective-permute-start(f32[2,256,128]{2,1,0:T(8,128)S(1)} %get-tuple-element.73), channel_id=1, source_target_pairs={{0,4},{2,6},{4,0},{6,2},{8,12},{10,14},{12,8},{14,10},{16,20},{18,... | collective-permute-start | bytes 786440 | tf_op jit(solution)/shard_map/ppermute | solution.py:408
  9.2 13.3 %collective-permute-start.4 = (f32[2,256,128]{2,1,0:T(8,128)S(1)}, f32[2,256,128]{2,1,0:T(8,128)S(1)}, u32[]{:S(2)}, u32[]{:S(2)}) collective-permute-start(f32[2,256,128]{2,1,0:T(8,128)S(1)} %get-tuple-element.74), channel_id=1, source_target_pairs={{0,10},{2,8},{4,14},{6,12},{8,2},{10,0},{12,6},{14,4},{16,26},{18,... | collective-permute-start | bytes 786440 | tf_op jit(solution)/shard_map/ppermute | solution.py:408
  12.3 5.5 %collective-permute-start.8 = (f32[256,128]{1,0:T(8,128)S(1)}, f32[256,128]{1,0:T(8,128)S(1)}, u32[]{:S(2)}, u32[]{:S(2)}) collective-permute-start(f32[256,128]{1,0:T(8,128)S(1)} %slice_bitcast_fusion.1), channel_id=1, source_target_pairs={{0,1},{1,0},{2,3},{3,2},{4,5},{5,4},{6,7},{7,6},{8,9},{9,8},{10,11... | collective-permute-start | bytes 393224 | tf_op jit(solution)/shard_map/ppermute | solution.py:412
  16.1 3.3 %collective-permute-start.9 = (f32[256,128]{1,0:T(8,128)S(1)}, f32[256,128]{1,0:T(8,128)S(1)}, u32[]{:S(2)}, u32[]{:S(2)}) collective-permute-start(f32[256,128]{1,0:T(8,128)S(1)} %slice_bitcast_fusion), channel_id=1, source_target_pairs={{0,1},{1,0},{2,3},{3,2},{4,5},{5,4},{6,7},{7,6},{8,9},{9,8},{10,11... | collective-permute-start | bytes 393224 | tf_op jit(solution)/shard_map/ppermute | solution.py:412
  16.2 10.9 %collective-permute-start.1 = (f32[2,256,128]{2,1,0:T(8,128)S(1)}, f32[2,256,128]{2,1,0:T(8,128)S(1)}, u32[]{:S(2)}, u32[]{:S(2)}) collective-permute-start(f32[2,256,128]{2,1,0:T(8,128)S(1)} %get-tuple-element.71), channel_id=1, source_target_pairs={{0,6},{2,4},{4,2},{6,0},{8,14},{10,12},{12,10},{14,8},{16,22},{18,... | collective-permute-start | bytes 786440 | tf_op jit(solution)/shard_map/ppermute | solution.py:408
  17.8 9.4 %collective-permute-start.2 = (f32[2,256,128]{2,1,0:T(8,128)S(1)}, f32[2,256,128]{2,1,0:T(8,128)S(1)}, u32[]{:S(2)}, u32[]{:S(2)}) collective-permute-start(f32[2,256,128]{2,1,0:T(8,128)S(1)} %get-tuple-element.72), channel_id=1, source_target_pairs={{0,8},{2,10},{4,12},{6,14},{8,0},{10,2},{12,4},{14,6},{16,24},{18,... | collective-permute-start | bytes 786440 | tf_op jit(solution)/shard_map/ppermute | solution.py:408
  22.5 1.9 %collective-permute-start.10 = (f32[256,128]{1,0:T(8,128)S(1)}, f32[256,128]{1,0:T(8,128)S(1)}, u32[]{:S(2)}, u32[]{:S(2)}) collective-permute-start(f32[256,128]{1,0:T(8,128)S(1)} %slice_bitcast_fusion.6), channel_id=1, source_target_pairs={{0,1},{1,0},{2,3},{3,2},{4,5},{5,4},{6,7},{7,6},{8,9},{9,8},{10,11... | collective-permute-start | bytes 393224 | tf_op jit(solution)/shard_map/ppermute | solution.py:412
  22.6 1.8 %collective-permute-start.11 = (f32[256,128]{1,0:T(8,128)S(1)}, f32[256,128]{1,0:T(8,128)S(1)}, u32[]{:S(2)}, u32[]{:S(2)}) collective-permute-start(f32[256,128]{1,0:T(8,128)S(1)} %slice_bitcast_fusion.5), channel_id=1, source_target_pairs={{0,1},{1,0},{2,3},{3,2},{4,5},{5,4},{6,7},{7,6},{8,9},{9,8},{10,11... | collective-permute-start | bytes 393224 | tf_op jit(solution)/shard_map/ppermute | solution.py:412
  23.2 10.1 %collective-permute-start = (f32[2,256,128]{2,1,0:T(8,128)S(1)}, f32[2,256,128]{2,1,0:T(8,128)S(1)}, u32[]{:S(2)}, u32[]{:S(2)}) collective-permute-start(f32[2,256,128]{2,1,0:T(8,128)S(1)} %get-tuple-element.70), channel_id=1, source_target_pairs={{0,14},{2,12},{4,10},{6,8},{8,6},{10,4},{12,2},{14,0},{16,30},{18,... | collective-permute-start | bytes 786440 | tf_op jit(solution)/shard_map/ppermute | solution.py:408
  27.2 1.4 %collective-permute-start.12 = (f32[256,128]{1,0:T(8,128)S(1)}, f32[256,128]{1,0:T(8,128)S(1)}, u32[]{:S(2)}, u32[]{:S(2)}) collective-permute-start(f32[256,128]{1,0:T(8,128)S(1)} %slice_bitcast_fusion.4), channel_id=1, source_target_pairs={{0,1},{1,0},{2,3},{3,2},{4,5},{5,4},{6,7},{7,6},{8,9},{9,8},{10,11... | collective-permute-start | bytes 393224 | tf_op jit(solution)/shard_map/ppermute | solution.py:412
  27.4 1.5 %collective-permute-start.13 = (f32[256,128]{1,0:T(8,128)S(1)}, f32[256,128]{1,0:T(8,128)S(1)}, u32[]{:S(2)}, u32[]{:S(2)}) collective-permute-start(f32[256,128]{1,0:T(8,128)S(1)} %slice_bitcast_fusion.3), channel_id=1, source_target_pairs={{0,1},{1,0},{2,3},{3,2},{4,5},{5,4},{6,7},{7,6},{8,9},{9,8},{10,11... | collective-permute-start | bytes 393224 | tf_op jit(solution)/shard_map/ppermute | solution.py:412
  27.9 20.9 %collective-permute-start.20 = (f32[256,512]{1,0:T(8,128)S(1)}, f32[256,512]{1,0:T(8,128)S(1)}, u32[]{:S(2)}, u32[]{:S(2)}) collective-permute-start(f32[256,512]{1,0:T(8,128)S(1)} %get-tuple-element.101.mine_ref), channel_id=1, source_target_pairs={{0,1},{1,0},{2,3},{3,2},{4,5},{5,4},{6,7},{7,6},{8,9},{9,8},{10,11... | collective-permute-start | bytes 1572872 | tf_op jit(solution)/shard_map/ppermute | solution.py:412
  33.3 1.4 %collective-permute-start.14 = (f32[256,128]{1,0:T(8,128)S(1)}, f32[256,128]{1,0:T(8,128)S(1)}, u32[]{:S(2)}, u32[]{:S(2)}) collective-permute-start(f32[256,128]{1,0:T(8,128)S(1)} %slice_bitcast_fusion.2), channel_id=1, source_target_pairs={{0,1},{1,0},{2,3},{3,2},{4,5},{5,4},{6,7},{7,6},{8,9},{9,8},{10,11... | collective-permute-start | bytes 393224 | tf_op jit(solution)/shard_map/ppermute | solution.py:412
  34.7 24.1 %copy-start.3 = (f32[1,16,16,256]{3,2,1,0:T(8,128)S(1)}, f32[1,16,16,256]{3,2,1,0:T(8,128)}, u32[]{:S(2)}) copy-start(f32[1,16,16,256]{3,2,1,0:T(8,128)} %param.5) | copy-start | bytes 786436
  36.9 3.8 %collective-permute-start.15 = (f32[40,128]{1,0:T(8,128)S(1)}, f32[40,128]{1,0:T(8,128)S(1)}, u32[]{:S(2)}, u32[]{:S(2)}) collective-permute-start(f32[40,128]{1,0:T(8,128)S(1)} %get-tuple-element.92), channel_id=1, source_target_pairs={{0,2},{2,0},{4,6},{6,4},{8,10},{10,8},{12,14},{14,12},{16,18},{18,... | collective-permute-start | bytes 61448 | tf_op jit(solution)/shard_map/ppermute | solution.py:408
  38.5 4.0 %collective-permute-start.16 = (f32[40,128]{1,0:T(8,128)S(1)}, f32[40,128]{1,0:T(8,128)S(1)}, u32[]{:S(2)}, u32[]{:S(2)}) collective-permute-start(f32[40,128]{1,0:T(8,128)S(1)} %get-tuple-element.92), channel_id=1, source_target_pairs={{0,4},{2,6},{4,0},{6,2},{8,12},{10,14},{12,8},{14,10},{16,20},{18,... | collective-permute-start | bytes 61448 | tf_op jit(solution)/shard_map/ppermute | solution.py:408
  39.0 4.7 %collective-permute-start.17 = (f32[40,128]{1,0:T(8,128)S(1)}, f32[40,128]{1,0:T(8,128)S(1)}, u32[]{:S(2)}, u32[]{:S(2)}) collective-permute-start(f32[40,128]{1,0:T(8,128)S(1)} %get-tuple-element.92), channel_id=1, source_target_pairs={{0,6},{2,4},{4,2},{6,0},{8,14},{10,12},{12,10},{14,8},{16,22},{18,... | collective-permute-start | bytes 61448 | tf_op jit(solution)/shard_map/ppermute | solution.py:408
  43.7 3.8 %collective-permute-start.18 = (f32[40,128]{1,0:T(8,128)S(1)}, f32[40,128]{1,0:T(8,128)S(1)}, u32[]{:S(2)}, u32[]{:S(2)}) collective-permute-start(f32[40,128]{1,0:T(8,128)S(1)} %add_add_fusion), channel_id=1, source_target_pairs={{0,8},{2,10},{4,12},{6,14},{8,0},{10,2},{12,4},{14,6},{16,24},{18,... | collective-permute-start | bytes 61448 | tf_op jit(solution)/shard_map/ppermute | solution.py:408
  47.5 1.2 %collective-permute-start.19 = (f32[40,128]{1,0:T(8,128)S(1)}, f32[40,128]{1,0:T(8,128)S(1)}, u32[]{:S(2)}, u32[]{:S(2)}) collective-permute-start(f32[40,128]{1,0:T(8,128)S(1)} %add.57), channel_id=1, source_target_pairs={{0,1},{1,0},{2,3},{3,2},{4,5},{5,4},{6,7},{7,6},{8,9},{9,8},{10,11... | collective-permute-start | bytes 61448 | tf_op jit(solution)/shard_map/ppermute | solution.py:412
  50.3 29.0 %collective-permute-start.21 = (f32[1152,128]{1,0:T(8,128)S(1)}, f32[1152,128]{1,0:T(8,128)S(1)}, u32[]{:S(2)}, u32[]{:S(2)}) collective-permute-start(f32[1152,128]{1,0:T(8,128)S(1)} %get-tuple-element.96), channel_id=1, source_target_pairs={{0,16},{2,18},{4,20},{6,22},{8,24},{10,26},{12,28},{14,30},{16,0},... | collective-permute-start | bytes 1769480 | tf_op jit(solution)/shard_map/ppermute | solution.py:408
  52.9 18.5 %collective-permute-start.22 = (f32[192,128]{1,0:T(8,128)S(1)}, f32[192,128]{1,0:T(8,128)S(1)}, u32[]{:S(2)}, u32[]{:S(2)}) collective-permute-start(f32[192,128]{1,0:T(8,128)S(1)} %get-tuple-element.97), channel_id=1, source_target_pairs={{0,2},{2,0},{4,6},{6,4},{8,10},{10,8},{12,14},{14,12},{16,18},{18,... | collective-permute-start | bytes 294920 | tf_op jit(solution)/shard_map/ppermute | solution.py:408
  53.9 17.5 %collective-permute-start.23 = (f32[128,128]{1,0:T(8,128)S(1)}, f32[128,128]{1,0:T(8,128)S(1)}, u32[]{:S(2)}, u32[]{:S(2)}) collective-permute-start(f32[128,128]{1,0:T(8,128)S(1)} %get-tuple-element.98), channel_id=1, source_target_pairs={{0,6},{2,4},{4,2},{6,0},{8,14},{10,12},{12,10},{14,8},{16,22},{18,... | collective-permute-start | bytes 196616 | tf_op jit(solution)/shard_map/ppermute | solution.py:408
  55.9 15.5 %collective-permute-start.24 = (f32[128,128]{1,0:T(8,128)S(1)}, f32[128,128]{1,0:T(8,128)S(1)}, u32[]{:S(2)}, u32[]{:S(2)}) collective-permute-start(f32[128,128]{1,0:T(8,128)S(1)} %get-tuple-element.99), channel_id=1, source_target_pairs={{0,10},{2,8},{4,14},{6,12},{8,2},{10,0},{12,6},{14,4},{16,26},{18,... | collective-permute-start | bytes 196616 | tf_op jit(solution)/shard_map/ppermute | solution.py:408
  56.9 14.5 %collective-permute-start.25 = (f32[128,128]{1,0:T(8,128)S(1)}, f32[128,128]{1,0:T(8,128)S(1)}, u32[]{:S(2)}, u32[]{:S(2)}) collective-permute-start(f32[128,128]{1,0:T(8,128)S(1)} %get-tuple-element.100), channel_id=1, source_target_pairs={{0,14},{2,12},{4,10},{6,8},{8,6},{10,4},{12,2},{14,0},{16,30},{18,... | collective-permute-start | bytes 196616 | tf_op jit(solution)/shard_map/ppermute | solution.py:408
  58.8 40.1 %copy-start.1 = (f32[1,16,16,512]{3,2,1,0:T(8,128)S(1)}, f32[1,16,16,512]{3,2,1,0:T(8,128)}, u32[]{:S(2)}) copy-start(f32[1,16,16,512]{3,2,1,0:T(8,128)} %param.3) | copy-start | bytes 1572868
  79.5 6.1 %collective-permute-start.26 = (f32[264,128]{1,0:T(8,128)S(1)}, f32[264,128]{1,0:T(8,128)S(1)}, u32[]{:S(2)}, u32[]{:S(2)}) collective-permute-start(f32[264,128]{1,0:T(8,128)S(1)} %get-tuple-element.108), channel_id=1, source_target_pairs={{0,12},{2,14},{4,8},{6,10},{8,4},{10,6},{12,0},{14,2},{16,28},{18,... | collective-permute-start | bytes 405512 | tf_op jit(solution)/shard_map/ppermute | solution.py:408
  80.2 18.7 %collective-permute-start.35 = (f32[256,512]{1,0:T(8,128)S(1)}, f32[256,512]{1,0:T(8,128)S(1)}, u32[]{:S(2)}, u32[]{:S(2)}) collective-permute-start(f32[256,512]{1,0:T(8,128)S(1)} %get-tuple-element.130), channel_id=1, source_target_pairs={{0,1},{1,0},{2,3},{3,2},{4,5},{5,4},{6,7},{7,6},{8,9},{9,8},{10,11... | collective-permute-start | bytes 1572872 | tf_op jit(solution)/shard_map/ppermute | solution.py:412
  80.2 6.1 %collective-permute-start.27 = (f32[200,128]{1,0:T(8,128)S(1)}, f32[200,128]{1,0:T(8,128)S(1)}, u32[]{:S(2)}, u32[]{:S(2)}) collective-permute-start(f32[200,128]{1,0:T(8,128)S(1)} %get-tuple-element.111), channel_id=1, source_target_pairs={{0,2},{2,0},{4,6},{6,4},{8,10},{10,8},{12,14},{14,12},{16,18},{18,... | collective-permute-start | bytes 307208 | tf_op jit(solution)/shard_map/ppermute | solution.py:408
  81.3 7.3 %collective-permute-start.28 = (f32[264,128]{1,0:T(8,128)S(1)}, f32[264,128]{1,0:T(8,128)S(1)}, u32[]{:S(2)}, u32[]{:S(2)}) collective-permute-start(f32[264,128]{1,0:T(8,128)S(1)} %get-tuple-element.114), channel_id=1, source_target_pairs={{0,4},{2,6},{4,0},{6,2},{8,12},{10,14},{12,8},{14,10},{16,20},{18,... | collective-permute-start | bytes 405512 | tf_op jit(solution)/shard_map/ppermute | solution.py:408
  82.7 8.2 %collective-permute-start.29 = (f32[136,128]{1,0:T(8,128)S(1)}, f32[136,128]{1,0:T(8,128)S(1)}, u32[]{:S(2)}, u32[]{:S(2)}) collective-permute-start(f32[136,128]{1,0:T(8,128)S(1)} %get-tuple-element.117), channel_id=1, source_target_pairs={{0,10},{2,8},{4,14},{6,12},{8,2},{10,0},{12,6},{14,4},{16,26},{18,... | collective-permute-start | bytes 208904 | tf_op jit(solution)/shard_map/ppermute | solution.py:408
  85.6 5.3 %collective-permute-start.30 = (f32[264,128]{1,0:T(8,128)S(1)}, f32[264,128]{1,0:T(8,128)S(1)}, u32[]{:S(2)}, u32[]{:S(2)}) collective-permute-start(f32[264,128]{1,0:T(8,128)S(1)} %get-tuple-element.120), channel_id=1, source_target_pairs={{0,8},{2,10},{4,12},{6,14},{8,0},{10,2},{12,4},{14,6},{16,24},{18,... | collective-permute-start | bytes 405512 | tf_op jit(solution)/shard_map/ppermute | solution.py:408
  86.3 5.2 %collective-permute-start.31 = (f32[136,128]{1,0:T(8,128)S(1)}, f32[136,128]{1,0:T(8,128)S(1)}, u32[]{:S(2)}, u32[]{:S(2)}) collective-permute-start(f32[136,128]{1,0:T(8,128)S(1)} %get-tuple-element.123), channel_id=1, source_target_pairs={{0,6},{2,4},{4,2},{6,0},{8,14},{10,12},{12,10},{14,8},{16,22},{18,... | collective-permute-start | bytes 208904 | tf_op jit(solution)/shard_map/ppermute | solution.py:408
  88.5 6.1 %collective-permute-start.32 = (f32[136,128]{1,0:T(8,128)S(1)}, f32[136,128]{1,0:T(8,128)S(1)}, u32[]{:S(2)}, u32[]{:S(2)}) collective-permute-start(f32[136,128]{1,0:T(8,128)S(1)} %get-tuple-element.126), channel_id=1, source_target_pairs={{0,14},{2,12},{4,10},{6,8},{8,6},{10,4},{12,2},{14,0},{16,30},{18,... | collective-permute-start | bytes 208904 | tf_op jit(solution)/shard_map/ppermute | solution.py:408
  94.6 1.2 %collective-permute-start.33 = (f32[8,128]{1,0:T(8,128)S(1)}, f32[8,128]{1,0:T(8,128)S(1)}, u32[]{:S(2)}, u32[]{:S(2)}) collective-permute-start(f32[8,128]{1,0:T(8,128)S(1)} %slice_add_fusion), channel_id=1, source_target_pairs={{0,1},{1,0},{2,3},{3,2},{4,5},{5,4},{6,7},{7,6},{8,9},{9,8},{10,11... | collective-permute-start | bytes 12296 | tf_op jit(solution)/shard_map/ppermute | solution.py:412
  95.8 4.6 %collective-permute-start.34 = (f32[8,128]{1,0:T(8,128)S(1)}, f32[8,128]{1,0:T(8,128)S(1)}, u32[]{:S(2)}, u32[]{:S(2)}) collective-permute-start(f32[8,128]{1,0:T(8,128)S(1)} %add.66), channel_id=1, source_target_pairs={{0,16},{2,18},{4,20},{6,22},{8,24},{10,26},{12,28},{14,30},{16,0},... | collective-permute-start | bytes 12296 | tf_op jit(solution)/shard_map/ppermute | solution.py:408

commit v5 on v4

--- a/solution.py
+++ b/solution.py
@@ -417,8 +417,8 @@
 
 
 ORDER = (1, 6, 2, 5, 3, 4, 7)
-EARLY = (1, 3, 5, 7)
-LAST = (6, 1, 2, 5, 4, 3, 7)
+EARLY = (1, 3, 5, 6)
+LAST = (2, 4, 1, 7, 6, 5, 3)
 COST = 10**10
 BATCHES = ((0, 1, 6), (2, 5), (3, 4), (7,))
 

time: 102 us -> 101 us (level)
  starting transfers between devices: 38.7 us -> 34.8 us
  waiting for transfers between devices: 31.7 us -> 34.8 us
    ppermute x24, starting transfers between devices: 37.1 us -> 33.2 us  [exchange(): return lax.ppermute(x, 'dp', [(i, i ^ other) for i in range(size)])]
    ppermute x24, waiting for transfers between devices: 27.1 us -> 30.2 us  [exchange(): return lax.ppermute(x, 'dp', [(i, i ^ other) for i in range(size)])]
  transfers between devices with their start and end apart: 36 -> 36, of which waited for: 17 -> 20; matrix products, arithmetic and copies ran while one was open for 1% -> 1% of each run, Pallas kernels for 24% -> 24%
where the time goes in v5:
time: 101 us
  starting transfers between devices  34.8 us (34%)
  waiting for transfers between devices  34.8 us (34%)
  Pallas kernels  27 us (27%)
  local copies, waits for them, and re-layouts  2.07 us (2%)
  other arithmetic  1.07 us (1%)
    ppermute x24, starting transfers between devices, exchange(): return lax.ppermute(x, 'dp', [(i, i ^ other) for i in range(size)])  33.2 us
    ppermute x24, waiting for transfers between devices, exchange(): return lax.ppermute(x, 'dp', [(i, i ^ other) for i in range(size)])  30.2 us
    pallas_call x1, Pallas kernels, local_cube(): pl.pallas_call(functools.partial(image_kernel, extent), grid=(taps,), in_...  12.7 us
    pallas_call x4, Pallas kernels, local_cube(): pl.pallas_call(functools.partial(leaf_kernel, extent, images, known, batc...  11.2 us
    ppermute x12, waiting for transfers between devices, swap_cores(): return lax.ppermute(x, 'mp', [(0, 1), (1, 0)])  4.61 us
  transfers between devices with their start and end apart: 36, of which 20 were waited for; matrix products, arithmetic and copies ran while one was open for 1% of the time, Pallas kernels for 24%

profile of v5, /device:TPU:0, one launch (start us, length us, event | category | flops | bytes accessed | tf_op | source)
XLA Modules:
  0.0 100.7 jit_solution(9088755269055607555)
XLA Ops:
  0.6 1.0 %copy-done = f32[1,16,16,512]{3,2,1,0:T(8,128)S(1)} copy-done((f32[1,16,16,512]{3,2,1,0:T(8,128)S(1)}, f32[1,16,16,512]{3,2,1,0:T(8,128)}, u32[]{:S(2)}) %copy-start) | copy-done | bytes 524312
  1.7 0.9 copy-done.2
  3.0 3.0 %collective-permute-start.5 = (f32[2,256,128]{2,1,0:T(8,128)S(1)}, f32[2,256,128]{2,1,0:T(8,128)S(1)}, u32[]{:S(2)}, u32[]{:S(2)}) collective-permute-start(f32[2,256,128]{2,1,0:T(8,128)S(1)} %get-tuple-element.76), channel_id=1, source_target_pairs={{0,2},{2,0},{4,6},{6,4},{8,10},{10,8},{12,14},{14,12},{16,18},{18,... | collective-permute-start | bytes 786440 | tf_op jit(solution)/shard_map/ppermute | solution.py:408
  6.0 2.5 %collective-permute-start.6 = (f32[2,256,128]{2,1,0:T(8,128)S(1)}, f32[2,256,128]{2,1,0:T(8,128)S(1)}, u32[]{:S(2)}, u32[]{:S(2)}) collective-permute-start(f32[2,256,128]{2,1,0:T(8,128)S(1)} %get-tuple-element.77), channel_id=1, source_target_pairs={{0,12},{2,14},{4,8},{6,10},{8,4},{10,6},{12,0},{14,2},{16,28},{18,... | collective-permute-start | bytes 786440 | tf_op jit(solution)/shard_map/ppermute | solution.py:408
  8.6 0.6 collective-permute-start.3
  9.2 3.1 %collective-permute-done.5.refs_1_ = f32[2,256,128]{2,1,0:T(8,128)S(1)} collective-permute-done((f32[2,256,128]{2,1,0:T(8,128)S(1)}, f32[2,256,128]{2,1,0:T(8,128)S(1)}, u32[]{:S(2)}, u32[]{:S(2)}) %collective-permute-start.5) | collective-permute-done | bytes 262176 | tf_op jit(solution)/shard_map/ppermute | solution.py:408
  12.4 3.7 %collective-permute-done.6.refs_2_ = f32[2,256,128]{2,1,0:T(8,128)S(1)} collective-permute-done((f32[2,256,128]{2,1,0:T(8,128)S(1)}, f32[2,256,128]{2,1,0:T(8,128)S(1)}, u32[]{:S(2)}, u32[]{:S(2)}) %collective-permute-start.6) | collective-permute-done | bytes 262176 | tf_op jit(solution)/shard_map/ppermute | solution.py:408
  16.2 1.6 %collective-permute-start.1 = (f32[2,256,128]{2,1,0:T(8,128)S(1)}, f32[2,256,128]{2,1,0:T(8,128)S(1)}, u32[]{:S(2)}, u32[]{:S(2)}) collective-permute-start(f32[2,256,128]{2,1,0:T(8,128)S(1)} %get-tuple-element.71), channel_id=1, source_target_pairs={{0,6},{2,4},{4,2},{6,0},{8,14},{10,12},{12,10},{14,8},{16,22},{18,... | collective-permute-start | bytes 786440 | tf_op jit(solution)/shard_map/ppermute | solution.py:408
  17.8 1.6 %collective-permute-start.2 = (f32[2,256,128]{2,1,0:T(8,128)S(1)}, f32[2,256,128]{2,1,0:T(8,128)S(1)}, u32[]{:S(2)}, u32[]{:S(2)}) collective-permute-start(f32[2,256,128]{2,1,0:T(8,128)S(1)} %get-tuple-element.72), channel_id=1, source_target_pairs={{0,8},{2,10},{4,12},{6,14},{8,0},{10,2},{12,4},{14,6},{16,24},{18,... | collective-permute-start | bytes 786440 | tf_op jit(solution)/shard_map/ppermute | solution.py:408
  19.4 3.1 %leaf.4 = (f32[8,2304,128]{2,1,0:T(8,128)S(1)}, f32[64,128]{1,0:T(8,128)S(1)}) custom-call(f32[2,256,128]{2,1,0:T(8,128)S(1)} %get-tuple-element.75.refs_0_, f32[2,256,128]{2,1,0:T(8,128)S(1)} %collective-permute-done.5.refs_1_, f32[2,256,128]{2,1,0:T(8,128)S(1)} %collective-permute-done.6.refs_2_, f32[256,128]{1,0:T(8,128)S(1)} %collective-permute-done.7.refs_3_, ...), custom_call_target="tpu_custom_call" | custom-call | flops 1 | bytes 1 | tf_op jit(solution)/shard_map/leaf/pallas_call | solution.py:477
  22.6 0.6 collective-permute-start.11
  23.2 1.3 %collective-permute-start = (f32[2,256,128]{2,1,0:T(8,128)S(1)}, f32[2,256,128]{2,1,0:T(8,128)S(1)}, u32[]{:S(2)}, u32[]{:S(2)}) collective-permute-start(f32[2,256,128]{2,1,0:T(8,128)S(1)} %get-tuple-element.70), channel_id=1, source_target_pairs={{0,14},{2,12},{4,10},{6,8},{8,6},{10,4},{12,2},{14,0},{16,30},{18,... | collective-permute-start | bytes 786440 | tf_op jit(solution)/shard_map/ppermute | solution.py:408
  24.4 2.7 %leaf.5 = (f32[8,2304,128]{2,1,0:T(8,128)S(1)}, f32[64,128]{1,0:T(8,128)S(1)}) custom-call(f32[2,256,128]{2,1,0:T(8,128)S(1)} %collective-permute-done.3.refs_0_, f32[2,256,128]{2,1,0:T(8,128)S(1)} %collective-permute-done.4.refs_1_, f32[256,128]{1,0:T(8,128)S(1)} %collective-permute-done.10.refs_2_, ...), custom_call_target="tpu_custom_call", output_to_operand_aliasing={{0}: (5, {})} | custom-call | flops 1 | bytes 1 | tf_op jit(solution)/shard_map/leaf/pallas_call | solution.py:477
  27.9 0.7 collective-permute-done.12.refs_2_
  28.8 3.2 %leaf.6 = (f32[8,2304,128]{2,1,0:T(8,128)S(1)}, f32[64,128]{1,0:T(8,128)S(1)}) custom-call(f32[2,256,128]{2,1,0:T(8,128)S(1)} %collective-permute-done.1.refs_0_, f32[2,256,128]{2,1,0:T(8,128)S(1)} %collective-permute-done.2.refs_1_, f32[256,128]{1,0:T(8,128)S(1)} %collective-permute-done.12.refs_2_, ...), custom_call_target="tpu_custom_call", output_to_operand_aliasing={{0}: (5, {})} | custom-call | flops 1 | bytes 1 | tf_op jit(solution)/shard_map/leaf/pallas_call | solution.py:477
  32.1 1.2 %collective-permute-done.refs_0_ = f32[2,256,128]{2,1,0:T(8,128)S(1)} collective-permute-done((f32[2,256,128]{2,1,0:T(8,128)S(1)}, f32[2,256,128]{2,1,0:T(8,128)S(1)}, u32[]{:S(2)}, u32[]{:S(2)}) %collective-permute-start) | collective-permute-done | bytes 262176 | tf_op jit(solution)/shard_map/ppermute | solution.py:408
  33.3 1.3 %collective-permute-done.14.refs_1_ = f32[256,128]{1,0:T(8,128)S(1)} collective-permute-done((f32[256,128]{1,0:T(8,128)S(1)}, f32[256,128]{1,0:T(8,128)S(1)}, u32[]{:S(2)}, u32[]{:S(2)}) %collective-permute-start.14) | collective-permute-done | bytes 131104 | tf_op jit(solution)/shard_map/ppermute | solution.py:412
  34.7 2.3 %leaf.7 = (f32[8,2304,128]{2,1,0:T(8,128)S(1)}, f32[40,128]{1,0:T(8,128)S(1)}) custom-call(f32[2,256,128]{2,1,0:T(8,128)S(1)} %collective-permute-done.refs_0_, f32[256,128]{1,0:T(8,128)S(1)} %collective-permute-done.14.refs_1_, f32[64,128]{1,0:T(8,128)S(1)} %get-tuple-element.90.refs_2_, ...), custom_call_target="tpu_custom_call", output_to_operand_aliasing={{0}: (3, {})} | custom-call | flops 1 | bytes 1 | tf_op jit(solution)/shard_map/leaf/pallas_call | solution.py:477
  36.9 1.6 %collective-permute-start.15 = (f32[40,128]{1,0:T(8,128)S(1)}, f32[40,128]{1,0:T(8,128)S(1)}, u32[]{:S(2)}, u32[]{:S(2)}) collective-permute-start(f32[40,128]{1,0:T(8,128)S(1)} %get-tuple-element.92), channel_id=1, source_target_pairs={{0,2},{2,0},{4,6},{6,4},{8,10},{10,8},{12,14},{14,12},{16,18},{18,... | collective-permute-start | bytes 61448 | tf_op jit(solution)/shard_map/ppermute | solution.py:408
  39.0 1.5 %collective-permute-start.17 = (f32[40,128]{1,0:T(8,128)S(1)}, f32[40,128]{1,0:T(8,128)S(1)}, u32[]{:S(2)}, u32[]{:S(2)}) collective-permute-start(f32[40,128]{1,0:T(8,128)S(1)} %get-tuple-element.92), channel_id=1, source_target_pairs={{0,6},{2,4},{4,2},{6,0},{8,14},{10,12},{12,10},{14,8},{16,22},{18,... | collective-permute-start | bytes 61448 | tf_op jit(solution)/shard_map/ppermute | solution.py:408
  40.8 1.7 %collective-permute-done.16 = f32[40,128]{1,0:T(8,128)S(1)} collective-permute-done((f32[40,128]{1,0:T(8,128)S(1)}, f32[40,128]{1,0:T(8,128)S(1)}, u32[]{:S(2)}, u32[]{:S(2)}) %collective-permute-start.16) | collective-permute-done | bytes 20512 | tf_op jit(solution)/shard_map/ppermute | solution.py:408
  42.5 1.2 %collective-permute-done.17 = f32[40,128]{1,0:T(8,128)S(1)} collective-permute-done((f32[40,128]{1,0:T(8,128)S(1)}, f32[40,128]{1,0:T(8,128)S(1)}, u32[]{:S(2)}, u32[]{:S(2)}) %collective-permute-start.17) | collective-permute-done | bytes 20512 | tf_op jit(solution)/shard_map/ppermute | solution.py:408
  43.7 1.1 %collective-permute-start.18 = (f32[40,128]{1,0:T(8,128)S(1)}, f32[40,128]{1,0:T(8,128)S(1)}, u32[]{:S(2)}, u32[]{:S(2)}) collective-permute-start(f32[40,128]{1,0:T(8,128)S(1)} %add_add_fusion), channel_id=1, source_target_pairs={{0,8},{2,10},{4,12},{6,14},{8,0},{10,2},{12,4},{14,6},{16,24},{18,... | collective-permute-start | bytes 61448 | tf_op jit(solution)/shard_map/ppermute | solution.py:408
  44.8 2.7 %collective-permute-done.18 = f32[40,128]{1,0:T(8,128)S(1)} collective-permute-done((f32[40,128]{1,0:T(8,128)S(1)}, f32[40,128]{1,0:T(8,128)S(1)}, u32[]{:S(2)}, u32[]{:S(2)}) %collective-permute-start.18) | collective-permute-done | bytes 20512 | tf_op jit(solution)/shard_map/ppermute | solution.py:408
  47.5 1.2 %collective-permute-done.19 = f32[40,128]{1,0:T(8,128)S(1)} collective-permute-done((f32[40,128]{1,0:T(8,128)S(1)}, f32[40,128]{1,0:T(8,128)S(1)}, u32[]{:S(2)}, u32[]{:S(2)}) %collective-permute-start.19) | collective-permute-done | bytes 20512 | tf_op jit(solution)/shard_map/ppermute | solution.py:412
  48.7 1.5 %combine.1 = (f32[1152,128]{1,0:T(8,128)S(1)}, f32[1152,128]{1,0:T(8,128)S(1)}, f32[192,128]{1,0:T(8,128)S(1)}, f32[128,128]{1,0:T(8,128)S(1)}, f32[128,128]{1,0:T(8,128)S(1)}, /*index=5*/f32[128,128]{1,0:T(8,128)S(1)}) custom-call(f32[40,128]{1,0:T(8,128)S(1)} %add.58.gram_ref, f32[8,2304,128]{2,1,0:T(8,128)S(1)} %get-tuple-element.95.leaf_ref), custom_call_target="tpu_custom_call" | custom-call | flops 1 | bytes 1 | tf_op jit(solution)/shard_map/combine/pallas_call | solution.py:499
  50.3 2.7 %collective-permute-start.21 = (f32[1152,128]{1,0:T(8,128)S(1)}, f32[1152,128]{1,0:T(8,128)S(1)}, u32[]{:S(2)}, u32[]{:S(2)}) collective-permute-start(f32[1152,128]{1,0:T(8,128)S(1)} %get-tuple-element.96), channel_id=1, source_target_pairs={{0,16},{2,18},{4,20},{6,22},{8,24},{10,26},{12,28},{14,30},{16,0},... | collective-permute-start | bytes 1769480 | tf_op jit(solution)/shard_map/ppermute | solution.py:408
  52.9 1.0 collective-permute-start.22
  53.9 2.0 %collective-permute-start.23 = (f32[128,128]{1,0:T(8,128)S(1)}, f32[128,128]{1,0:T(8,128)S(1)}, u32[]{:S(2)}, u32[]{:S(2)}) collective-permute-start(f32[128,128]{1,0:T(8,128)S(1)} %get-tuple-element.98), channel_id=1, source_target_pairs={{0,6},{2,4},{4,2},{6,0},{8,14},{10,12},{12,10},{14,8},{16,22},{18,... | collective-permute-start | bytes 196616 | tf_op jit(solution)/shard_map/ppermute | solution.py:408
  55.9 1.0 collective-permute-start.24
  56.9 1.4 %collective-permute-start.25 = (f32[128,128]{1,0:T(8,128)S(1)}, f32[128,128]{1,0:T(8,128)S(1)}, u32[]{:S(2)}, u32[]{:S(2)}) collective-permute-start(f32[128,128]{1,0:T(8,128)S(1)} %get-tuple-element.100), channel_id=1, source_target_pairs={{0,12},{2,14},{4,8},{6,10},{8,4},{10,6},{12,0},{14,2},{16,28},{18,... | collective-permute-start | bytes 196616 | tf_op jit(solution)/shard_map/ppermute | solution.py:408
  58.3 12.7 %image.1 = (f32[256,256]{1,0:T(8,128)}, f32[256,512]{1,0:T(8,128)S(1)}, f32[256,512]{1,0:T(8,128)S(1)}) custom-call(f32[256,512]{1,0:T(8,128)S(1)} %get-tuple-element.101.mine_ref, f32[256,512]{1,0:T(8,128)S(1)} %collective-permute-done.20.theirs_ref, f32[256,256]{1,0:T(8,128)S(1)} %bitcast.25, f32[9,256,1024]{2,1,0:T(8,128)} %bitcast.28), custom_call_target="tpu_custom_call" | custom-call | flops 10000000000 | bytes 1 | tf_op jit(solution)/shard_map/image/pallas_call | solution.py:512
  71.0 8.3 %collective-permute-done.21.far_ref = f32[1152,128]{1,0:T(8,128)S(1)} collective-permute-done((f32[1152,128]{1,0:T(8,128)S(1)}, f32[1152,128]{1,0:T(8,128)S(1)}, u32[]{:S(2)}, u32[]{:S(2)}) %collective-permute-start.21) | collective-permute-done | bytes 589856 | tf_op jit(solution)/shard_map/ppermute | solution.py:408
  79.5 1.5 %collective-permute-start.26 = (f32[264,128]{1,0:T(8,128)S(1)}, f32[264,128]{1,0:T(8,128)S(1)}, u32[]{:S(2)}, u32[]{:S(2)}) collective-permute-start(f32[264,128]{1,0:T(8,128)S(1)} %get-tuple-element.108), channel_id=1, source_target_pairs={{0,4},{2,6},{4,0},{6,2},{8,12},{10,14},{12,8},{14,10},{16,20},{18,... | collective-permute-start | bytes 405512 | tf_op jit(solution)/shard_map/ppermute | solution.py:408
  81.0 0.9 collective-permute-start.28
  81.8 2.7 %collective-permute-start.29 = (f32[264,128]{1,0:T(8,128)S(1)}, f32[264,128]{1,0:T(8,128)S(1)}, u32[]{:S(2)}, u32[]{:S(2)}) collective-permute-start(f32[264,128]{1,0:T(8,128)S(1)} %get-tuple-element.117), channel_id=1, source_target_pairs={{0,14},{2,12},{4,10},{6,8},{8,6},{10,4},{12,2},{14,0},{16,30},{18,... | collective-permute-start | bytes 405512 | tf_op jit(solution)/shard_map/ppermute | solution.py:408
  84.8 0.7 collective-permute-start.30
  85.4 1.9 %collective-permute-done.27.refs_4_ = f32[264,128]{1,0:T(8,128)S(1)} collective-permute-done((f32[264,128]{1,0:T(8,128)S(1)}, f32[264,128]{1,0:T(8,128)S(1)}, u32[]{:S(2)}, u32[]{:S(2)}) %collective-permute-start.27) | collective-permute-done | bytes 135200 | tf_op jit(solution)/shard_map/ppermute | solution.py:408
  87.6 1.6 %collective-permute-start.32 = (f32[136,128]{1,0:T(8,128)S(1)}, f32[136,128]{1,0:T(8,128)S(1)}, u32[]{:S(2)}, u32[]{:S(2)}) collective-permute-start(f32[136,128]{1,0:T(8,128)S(1)} %get-tuple-element.126), channel_id=1, source_target_pairs={{0,6},{2,4},{4,2},{6,0},{8,14},{10,12},{12,10},{14,8},{16,22},{18,... | collective-permute-start | bytes 208904 | tf_op jit(solution)/shard_map/ppermute | solution.py:408
  89.2 2.2 %collective-permute-done.29.refs_7_ = f32[264,128]{1,0:T(8,128)S(1)} collective-permute-done((f32[264,128]{1,0:T(8,128)S(1)}, f32[264,128]{1,0:T(8,128)S(1)}, u32[]{:S(2)}, u32[]{:S(2)}) %collective-permute-start.29) | collective-permute-done | bytes 135200 | tf_op jit(solution)/shard_map/ppermute | solution.py:408
  91.3 1.2 %collective-permute-done.30.refs_6_ = f32[136,128]{1,0:T(8,128)S(1)} collective-permute-done((f32[136,128]{1,0:T(8,128)S(1)}, f32[136,128]{1,0:T(8,128)S(1)}, u32[]{:S(2)}, u32[]{:S(2)}) %collective-permute-start.30) | collective-permute-done | bytes 69664 | tf_op jit(solution)/shard_map/ppermute | solution.py:408
  92.6 0.5 collective-permute-done.31.refs_5_
  93.1 0.9 collective-permute-done.32.refs_3_
  94.0 1.2 %collective-permute-done.33 = f32[8,128]{1,0:T(8,128)S(1)} collective-permute-done((f32[8,128]{1,0:T(8,128)S(1)}, f32[8,128]{1,0:T(8,128)S(1)}, u32[]{:S(2)}, u32[]{:S(2)}) %collective-permute-start.33) | collective-permute-done | bytes 4128 | tf_op jit(solution)/shard_map/ppermute | solution.py:412
  95.2 2.4 %collective-permute-start.34 = (f32[8,128]{1,0:T(8,128)S(1)}, f32[8,128]{1,0:T(8,128)S(1)}, u32[]{:S(2)}, u32[]{:S(2)}) collective-permute-start(f32[8,128]{1,0:T(8,128)S(1)} %add.66), channel_id=1, source_target_pairs={{0,16},{2,18},{4,20},{6,22},{8,24},{10,26},{12,28},{14,30},{16,0},... | collective-permute-start | bytes 12296 | tf_op jit(solution)/shard_map/ppermute | solution.py:408
  97.6 1.0 %fusion.4 = f32[256,512]{1,0:T(8,128)} fusion(f32[256,512]{1,0:T(8,128)S(1)} %get-tuple-element.129, f32[256,512]{1,0:T(8,128)S(1)} %collective-permute-done.35, f32[1,16,16,512]{3,2,1,0:T(8,128)S(1)} %copy-done.1), kind=kLoop, calls=%fused_computation.5 | loop fusion | flops 1310720 | bytes 2097152 | tf_op jit(solution)/shard_map/mul | solution.py:530
  98.6 1.1 %collective-permute-done.34 = f32[8,128]{1,0:T(8,128)S(1)} collective-permute-done((f32[8,128]{1,0:T(8,128)S(1)}, f32[8,128]{1,0:T(8,128)S(1)}, u32[]{:S(2)}, u32[]{:S(2)}) %collective-permute-start.34) | collective-permute-done | bytes 4128 | tf_op jit(solution)/shard_map/ppermute | solution.py:408
  99.7 1.0 %finish.1 = f32[576,256]{1,0:T(8,128)} custom-call(f32[8,128]{1,0:T(8,128)S(1)} %add.67.moments_ref, f32[392,128]{1,0:T(8,128)S(1)} %get-tuple-element.107.refs_0_, f32[200,128]{1,0:T(8,128)S(1)} %collective-permute-done.28.refs_1_, f32[264,128]{1,0:T(8,128)S(1)} %collective-permute-done.26.refs_2_, f32[136,128]{1,0:T(8,128)S(1)} %collective-permute-done.32.refs_3_, ...), custom_call_target="tpu_custom_call" | custom-call | flops 1 | bytes 1 | tf_op jit(solution)/shard_map/finish/pallas_call | solution.py:554
  (63 shorter events, 3.4 us)
Async XLA Ops:
  0.6 1.0 %copy-start = (f32[1,16,16,512]{3,2,1,0:T(8,128)S(1)}, f32[1,16,16,512]{3,2,1,0:T(8,128)}, u32[]{:S(2)}) copy-start(f32[1,16,16,512]{3,2,1,0:T(8,128)} %param.3) | copy-start | bytes 1572868
  1.7 0.9 copy-start.2
  3.0 9.3 %collective-permute-start.5 = (f32[2,256,128]{2,1,0:T(8,128)S(1)}, f32[2,256,128]{2,1,0:T(8,128)S(1)}, u32[]{:S(2)}, u32[]{:S(2)}) collective-permute-start(f32[2,256,128]{2,1,0:T(8,128)S(1)} %get-tuple-element.76), channel_id=1, source_target_pairs={{0,2},{2,0},{4,6},{6,4},{8,10},{10,8},{12,14},{14,12},{16,18},{18,... | collective-permute-start | bytes 786440 | tf_op jit(solution)/shard_map/ppermute | solution.py:408
  6.0 10.1 %collective-permute-start.6 = (f32[2,256,128]{2,1,0:T(8,128)S(1)}, f32[2,256,128]{2,1,0:T(8,128)S(1)}, u32[]{:S(2)}, u32[]{:S(2)}) collective-permute-start(f32[2,256,128]{2,1,0:T(8,128)S(1)} %get-tuple-element.77), channel_id=1, source_target_pairs={{0,12},{2,14},{4,8},{6,10},{8,4},{10,6},{12,0},{14,2},{16,28},{18,... | collective-permute-start | bytes 786440 | tf_op jit(solution)/shard_map/ppermute | solution.py:408
  8.5 7.7 %collective-permute-start.7 = (f32[256,128]{1,0:T(8,128)S(1)}, f32[256,128]{1,0:T(8,128)S(1)}, u32[]{:S(2)}, u32[]{:S(2)}) collective-permute-start(f32[256,128]{1,0:T(8,128)S(1)} %slice_bitcast_fusion.7), channel_id=1, source_target_pairs={{0,1},{1,0},{2,3},{3,2},{4,5},{5,4},{6,7},{7,6},{8,9},{9,8},{10,11... | collective-permute-start | bytes 393224 | tf_op jit(solution)/shard_map/ppermute | solution.py:412
  8.6 13.9 %collective-permute-start.3 = (f32[2,256,128]{2,1,0:T(8,128)S(1)}, f32[2,256,128]{2,1,0:T(8,128)S(1)}, u32[]{:S(2)}, u32[]{:S(2)}) collective-permute-start(f32[2,256,128]{2,1,0:T(8,128)S(1)} %get-tuple-element.73), channel_id=1, source_target_pairs={{0,4},{2,6},{4,0},{6,2},{8,12},{10,14},{12,8},{14,10},{16,20},{18,... | collective-permute-start | bytes 786440 | tf_op jit(solution)/shard_map/ppermute | solution.py:408
  9.2 13.3 %collective-permute-start.4 = (f32[2,256,128]{2,1,0:T(8,128)S(1)}, f32[2,256,128]{2,1,0:T(8,128)S(1)}, u32[]{:S(2)}, u32[]{:S(2)}) collective-permute-start(f32[2,256,128]{2,1,0:T(8,128)S(1)} %get-tuple-element.74), channel_id=1, source_target_pairs={{0,10},{2,8},{4,14},{6,12},{8,2},{10,0},{12,6},{14,4},{16,26},{18,... | collective-permute-start | bytes 786440 | tf_op jit(solution)/shard_map/ppermute | solution.py:408
  12.3 5.5 %collective-permute-start.8 = (f32[256,128]{1,0:T(8,128)S(1)}, f32[256,128]{1,0:T(8,128)S(1)}, u32[]{:S(2)}, u32[]{:S(2)}) collective-permute-start(f32[256,128]{1,0:T(8,128)S(1)} %slice_bitcast_fusion.1), channel_id=1, source_target_pairs={{0,1},{1,0},{2,3},{3,2},{4,5},{5,4},{6,7},{7,6},{8,9},{9,8},{10,11... | collective-permute-start | bytes 393224 | tf_op jit(solution)/shard_map/ppermute | solution.py:412
  16.1 3.3 %collective-permute-start.9 = (f32[256,128]{1,0:T(8,128)S(1)}, f32[256,128]{1,0:T(8,128)S(1)}, u32[]{:S(2)}, u32[]{:S(2)}) collective-permute-start(f32[256,128]{1,0:T(8,128)S(1)} %slice_bitcast_fusion), channel_id=1, source_target_pairs={{0,1},{1,0},{2,3},{3,2},{4,5},{5,4},{6,7},{7,6},{8,9},{9,8},{10,11... | collective-permute-start | bytes 393224 | tf_op jit(solution)/shard_map/ppermute | solution.py:412
  16.2 10.9 %collective-permute-start.1 = (f32[2,256,128]{2,1,0:T(8,128)S(1)}, f32[2,256,128]{2,1,0:T(8,128)S(1)}, u32[]{:S(2)}, u32[]{:S(2)}) collective-permute-start(f32[2,256,128]{2,1,0:T(8,128)S(1)} %get-tuple-element.71), channel_id=1, source_target_pairs={{0,6},{2,4},{4,2},{6,0},{8,14},{10,12},{12,10},{14,8},{16,22},{18,... | collective-permute-start | bytes 786440 | tf_op jit(solution)/shard_map/ppermute | solution.py:408
  17.8 9.4 %collective-permute-start.2 = (f32[2,256,128]{2,1,0:T(8,128)S(1)}, f32[2,256,128]{2,1,0:T(8,128)S(1)}, u32[]{:S(2)}, u32[]{:S(2)}) collective-permute-start(f32[2,256,128]{2,1,0:T(8,128)S(1)} %get-tuple-element.72), channel_id=1, source_target_pairs={{0,8},{2,10},{4,12},{6,14},{8,0},{10,2},{12,4},{14,6},{16,24},{18,... | collective-permute-start | bytes 786440 | tf_op jit(solution)/shard_map/ppermute | solution.py:408
  22.5 1.9 %collective-permute-start.10 = (f32[256,128]{1,0:T(8,128)S(1)}, f32[256,128]{1,0:T(8,128)S(1)}, u32[]{:S(2)}, u32[]{:S(2)}) collective-permute-start(f32[256,128]{1,0:T(8,128)S(1)} %slice_bitcast_fusion.6), channel_id=1, source_target_pairs={{0,1},{1,0},{2,3},{3,2},{4,5},{5,4},{6,7},{7,6},{8,9},{9,8},{10,11... | collective-permute-start | bytes 393224 | tf_op jit(solution)/shard_map/ppermute | solution.py:412
  22.6 1.8 %collective-permute-start.11 = (f32[256,128]{1,0:T(8,128)S(1)}, f32[256,128]{1,0:T(8,128)S(1)}, u32[]{:S(2)}, u32[]{:S(2)}) collective-permute-start(f32[256,128]{1,0:T(8,128)S(1)} %slice_bitcast_fusion.5), channel_id=1, source_target_pairs={{0,1},{1,0},{2,3},{3,2},{4,5},{5,4},{6,7},{7,6},{8,9},{9,8},{10,11... | collective-permute-start | bytes 393224 | tf_op jit(solution)/shard_map/ppermute | solution.py:412
  23.2 10.1 %collective-permute-start = (f32[2,256,128]{2,1,0:T(8,128)S(1)}, f32[2,256,128]{2,1,0:T(8,128)S(1)}, u32[]{:S(2)}, u32[]{:S(2)}) collective-permute-start(f32[2,256,128]{2,1,0:T(8,128)S(1)} %get-tuple-element.70), channel_id=1, source_target_pairs={{0,14},{2,12},{4,10},{6,8},{8,6},{10,4},{12,2},{14,0},{16,30},{18,... | collective-permute-start | bytes 786440 | tf_op jit(solution)/shard_map/ppermute | solution.py:408
  27.2 1.4 %collective-permute-start.12 = (f32[256,128]{1,0:T(8,128)S(1)}, f32[256,128]{1,0:T(8,128)S(1)}, u32[]{:S(2)}, u32[]{:S(2)}) collective-permute-start(f32[256,128]{1,0:T(8,128)S(1)} %slice_bitcast_fusion.4), channel_id=1, source_target_pairs={{0,1},{1,0},{2,3},{3,2},{4,5},{5,4},{6,7},{7,6},{8,9},{9,8},{10,11... | collective-permute-start | bytes 393224 | tf_op jit(solution)/shard_map/ppermute | solution.py:412
  27.4 1.5 %collective-permute-start.13 = (f32[256,128]{1,0:T(8,128)S(1)}, f32[256,128]{1,0:T(8,128)S(1)}, u32[]{:S(2)}, u32[]{:S(2)}) collective-permute-start(f32[256,128]{1,0:T(8,128)S(1)} %slice_bitcast_fusion.3), channel_id=1, source_target_pairs={{0,1},{1,0},{2,3},{3,2},{4,5},{5,4},{6,7},{7,6},{8,9},{9,8},{10,11... | collective-permute-start | bytes 393224 | tf_op jit(solution)/shard_map/ppermute | solution.py:412
  27.9 20.9 %collective-permute-start.20 = (f32[256,512]{1,0:T(8,128)S(1)}, f32[256,512]{1,0:T(8,128)S(1)}, u32[]{:S(2)}, u32[]{:S(2)}) collective-permute-start(f32[256,512]{1,0:T(8,128)S(1)} %get-tuple-element.101.mine_ref), channel_id=1, source_target_pairs={{0,1},{1,0},{2,3},{3,2},{4,5},{5,4},{6,7},{7,6},{8,9},{9,8},{10,11... | collective-permute-start | bytes 1572872 | tf_op jit(solution)/shard_map/ppermute | solution.py:412
  33.3 1.4 %collective-permute-start.14 = (f32[256,128]{1,0:T(8,128)S(1)}, f32[256,128]{1,0:T(8,128)S(1)}, u32[]{:S(2)}, u32[]{:S(2)}) collective-permute-start(f32[256,128]{1,0:T(8,128)S(1)} %slice_bitcast_fusion.2), channel_id=1, source_target_pairs={{0,1},{1,0},{2,3},{3,2},{4,5},{5,4},{6,7},{7,6},{8,9},{9,8},{10,11... | collective-permute-start | bytes 393224 | tf_op jit(solution)/shard_map/ppermute | solution.py:412
  34.7 23.6 %copy-start.3 = (f32[1,16,16,256]{3,2,1,0:T(8,128)S(1)}, f32[1,16,16,256]{3,2,1,0:T(8,128)}, u32[]{:S(2)}) copy-start(f32[1,16,16,256]{3,2,1,0:T(8,128)} %param.5) | copy-start | bytes 786436
  36.9 3.8 %collective-permute-start.15 = (f32[40,128]{1,0:T(8,128)S(1)}, f32[40,128]{1,0:T(8,128)S(1)}, u32[]{:S(2)}, u32[]{:S(2)}) collective-permute-start(f32[40,128]{1,0:T(8,128)S(1)} %get-tuple-element.92), channel_id=1, source_target_pairs={{0,2},{2,0},{4,6},{6,4},{8,10},{10,8},{12,14},{14,12},{16,18},{18,... | collective-permute-start | bytes 61448 | tf_op jit(solution)/shard_map/ppermute | solution.py:408
  38.5 4.0 %collective-permute-start.16 = (f32[40,128]{1,0:T(8,128)S(1)}, f32[40,128]{1,0:T(8,128)S(1)}, u32[]{:S(2)}, u32[]{:S(2)}) collective-permute-start(f32[40,128]{1,0:T(8,128)S(1)} %get-tuple-element.92), channel_id=1, source_target_pairs={{0,4},{2,6},{4,0},{6,2},{8,12},{10,14},{12,8},{14,10},{16,20},{18,... | collective-permute-start | bytes 61448 | tf_op jit(solution)/shard_map/ppermute | solution.py:408
  39.0 4.7 %collective-permute-start.17 = (f32[40,128]{1,0:T(8,128)S(1)}, f32[40,128]{1,0:T(8,128)S(1)}, u32[]{:S(2)}, u32[]{:S(2)}) collective-permute-start(f32[40,128]{1,0:T(8,128)S(1)} %get-tuple-element.92), channel_id=1, source_target_pairs={{0,6},{2,4},{4,2},{6,0},{8,14},{10,12},{12,10},{14,8},{16,22},{18,... | collective-permute-start | bytes 61448 | tf_op jit(solution)/shard_map/ppermute | solution.py:408
  43.7 3.8 %collective-permute-start.18 = (f32[40,128]{1,0:T(8,128)S(1)}, f32[40,128]{1,0:T(8,128)S(1)}, u32[]{:S(2)}, u32[]{:S(2)}) collective-permute-start(f32[40,128]{1,0:T(8,128)S(1)} %add_add_fusion), channel_id=1, source_target_pairs={{0,8},{2,10},{4,12},{6,14},{8,0},{10,2},{12,4},{14,6},{16,24},{18,... | collective-permute-start | bytes 61448 | tf_op jit(solution)/shard_map/ppermute | solution.py:408
  47.5 1.2 %collective-permute-start.19 = (f32[40,128]{1,0:T(8,128)S(1)}, f32[40,128]{1,0:T(8,128)S(1)}, u32[]{:S(2)}, u32[]{:S(2)}) collective-permute-start(f32[40,128]{1,0:T(8,128)S(1)} %add.57), channel_id=1, source_target_pairs={{0,1},{1,0},{2,3},{3,2},{4,5},{5,4},{6,7},{7,6},{8,9},{9,8},{10,11... | collective-permute-start | bytes 61448 | tf_op jit(solution)/shard_map/ppermute | solution.py:412
  50.3 29.0 %collective-permute-start.21 = (f32[1152,128]{1,0:T(8,128)S(1)}, f32[1152,128]{1,0:T(8,128)S(1)}, u32[]{:S(2)}, u32[]{:S(2)}) collective-permute-start(f32[1152,128]{1,0:T(8,128)S(1)} %get-tuple-element.96), channel_id=1, source_target_pairs={{0,16},{2,18},{4,20},{6,22},{8,24},{10,26},{12,28},{14,30},{16,0},... | collective-permute-start | bytes 1769480 | tf_op jit(solution)/shard_map/ppermute | solution.py:408
  52.9 18.1 %collective-permute-start.22 = (f32[192,128]{1,0:T(8,128)S(1)}, f32[192,128]{1,0:T(8,128)S(1)}, u32[]{:S(2)}, u32[]{:S(2)}) collective-permute-start(f32[192,128]{1,0:T(8,128)S(1)} %get-tuple-element.97), channel_id=1, source_target_pairs={{0,2},{2,0},{4,6},{6,4},{8,10},{10,8},{12,14},{14,12},{16,18},{18,... | collective-permute-start | bytes 294920 | tf_op jit(solution)/shard_map/ppermute | solution.py:408
  53.9 17.0 %collective-permute-start.23 = (f32[128,128]{1,0:T(8,128)S(1)}, f32[128,128]{1,0:T(8,128)S(1)}, u32[]{:S(2)}, u32[]{:S(2)}) collective-permute-start(f32[128,128]{1,0:T(8,128)S(1)} %get-tuple-element.98), channel_id=1, source_target_pairs={{0,6},{2,4},{4,2},{6,0},{8,14},{10,12},{12,10},{14,8},{16,22},{18,... | collective-permute-start | bytes 196616 | tf_op jit(solution)/shard_map/ppermute | solution.py:408
  55.9 15.1 %collective-permute-start.24 = (f32[128,128]{1,0:T(8,128)S(1)}, f32[128,128]{1,0:T(8,128)S(1)}, u32[]{:S(2)}, u32[]{:S(2)}) collective-permute-start(f32[128,128]{1,0:T(8,128)S(1)} %get-tuple-element.99), channel_id=1, source_target_pairs={{0,10},{2,8},{4,14},{6,12},{8,2},{10,0},{12,6},{14,4},{16,26},{18,... | collective-permute-start | bytes 196616 | tf_op jit(solution)/shard_map/ppermute | solution.py:408
  56.9 14.1 %collective-permute-start.25 = (f32[128,128]{1,0:T(8,128)S(1)}, f32[128,128]{1,0:T(8,128)S(1)}, u32[]{:S(2)}, u32[]{:S(2)}) collective-permute-start(f32[128,128]{1,0:T(8,128)S(1)} %get-tuple-element.100), channel_id=1, source_target_pairs={{0,12},{2,14},{4,8},{6,10},{8,4},{10,6},{12,0},{14,2},{16,28},{18,... | collective-permute-start | bytes 196616 | tf_op jit(solution)/shard_map/ppermute | solution.py:408
  58.3 39.3 %copy-start.1 = (f32[1,16,16,512]{3,2,1,0:T(8,128)S(1)}, f32[1,16,16,512]{3,2,1,0:T(8,128)}, u32[]{:S(2)}) copy-start(f32[1,16,16,512]{3,2,1,0:T(8,128)} %param.3) | copy-start | bytes 1572868
  79.5 5.3 %collective-permute-start.26 = (f32[264,128]{1,0:T(8,128)S(1)}, f32[264,128]{1,0:T(8,128)S(1)}, u32[]{:S(2)}, u32[]{:S(2)}) collective-permute-start(f32[264,128]{1,0:T(8,128)S(1)} %get-tuple-element.108), channel_id=1, source_target_pairs={{0,4},{2,6},{4,0},{6,2},{8,12},{10,14},{12,8},{14,10},{16,20},{18,... | collective-permute-start | bytes 405512 | tf_op jit(solution)/shard_map/ppermute | solution.py:408
  81.0 16.6 %collective-permute-start.35 = (f32[256,512]{1,0:T(8,128)S(1)}, f32[256,512]{1,0:T(8,128)S(1)}, u32[]{:S(2)}, u32[]{:S(2)}) collective-permute-start(f32[256,512]{1,0:T(8,128)S(1)} %get-tuple-element.130), channel_id=1, source_target_pairs={{0,1},{1,0},{2,3},{3,2},{4,5},{5,4},{6,7},{7,6},{8,9},{9,8},{10,11... | collective-permute-start | bytes 1572872 | tf_op jit(solution)/shard_map/ppermute | solution.py:412
  81.0 6.4 %collective-permute-start.27 = (f32[264,128]{1,0:T(8,128)S(1)}, f32[264,128]{1,0:T(8,128)S(1)}, u32[]{:S(2)}, u32[]{:S(2)}) collective-permute-start(f32[264,128]{1,0:T(8,128)S(1)} %get-tuple-element.111), channel_id=1, source_target_pairs={{0,8},{2,10},{4,12},{6,14},{8,0},{10,2},{12,4},{14,6},{16,24},{18,... | collective-permute-start | bytes 405512 | tf_op jit(solution)/shard_map/ppermute | solution.py:408
  81.0 6.6 %collective-permute-start.28 = (f32[200,128]{1,0:T(8,128)S(1)}, f32[200,128]{1,0:T(8,128)S(1)}, u32[]{:S(2)}, u32[]{:S(2)}) collective-permute-start(f32[200,128]{1,0:T(8,128)S(1)} %get-tuple-element.114), channel_id=1, source_target_pairs={{0,2},{2,0},{4,6},{6,4},{8,10},{10,8},{12,14},{14,12},{16,18},{18,... | collective-permute-start | bytes 307208 | tf_op jit(solution)/shard_map/ppermute | solution.py:408
  81.8 9.5 %collective-permute-start.29 = (f32[264,128]{1,0:T(8,128)S(1)}, f32[264,128]{1,0:T(8,128)S(1)}, u32[]{:S(2)}, u32[]{:S(2)}) collective-permute-start(f32[264,128]{1,0:T(8,128)S(1)} %get-tuple-element.117), channel_id=1, source_target_pairs={{0,14},{2,12},{4,10},{6,8},{8,6},{10,4},{12,2},{14,0},{16,30},{18,... | collective-permute-start | bytes 405512 | tf_op jit(solution)/shard_map/ppermute | solution.py:408
  84.8 7.8 %collective-permute-start.30 = (f32[136,128]{1,0:T(8,128)S(1)}, f32[136,128]{1,0:T(8,128)S(1)}, u32[]{:S(2)}, u32[]{:S(2)}) collective-permute-start(f32[136,128]{1,0:T(8,128)S(1)} %get-tuple-element.120), channel_id=1, source_target_pairs={{0,12},{2,14},{4,8},{6,10},{8,4},{10,6},{12,0},{14,2},{16,28},{18,... | collective-permute-start | bytes 208904 | tf_op jit(solution)/shard_map/ppermute | solution.py:408
  87.4 5.8 %collective-permute-start.31 = (f32[136,128]{1,0:T(8,128)S(1)}, f32[136,128]{1,0:T(8,128)S(1)}, u32[]{:S(2)}, u32[]{:S(2)}) collective-permute-start(f32[136,128]{1,0:T(8,128)S(1)} %get-tuple-element.123), channel_id=1, source_target_pairs={{0,10},{2,8},{4,14},{6,12},{8,2},{10,0},{12,6},{14,4},{16,26},{18,... | collective-permute-start | bytes 208904 | tf_op jit(solution)/shard_map/ppermute | solution.py:408
  87.6 6.4 %collective-permute-start.32 = (f32[136,128]{1,0:T(8,128)S(1)}, f32[136,128]{1,0:T(8,128)S(1)}, u32[]{:S(2)}, u32[]{:S(2)}) collective-permute-start(f32[136,128]{1,0:T(8,128)S(1)} %get-tuple-element.126), channel_id=1, source_target_pairs={{0,6},{2,4},{4,2},{6,0},{8,14},{10,12},{12,10},{14,8},{16,22},{18,... | collective-permute-start | bytes 208904 | tf_op jit(solution)/shard_map/ppermute | solution.py:408
  94.0 1.2 %collective-permute-start.33 = (f32[8,128]{1,0:T(8,128)S(1)}, f32[8,128]{1,0:T(8,128)S(1)}, u32[]{:S(2)}, u32[]{:S(2)}) collective-permute-start(f32[8,128]{1,0:T(8,128)S(1)} %slice_add_fusion), channel_id=1, source_target_pairs={{0,1},{1,0},{2,3},{3,2},{4,5},{5,4},{6,7},{7,6},{8,9},{9,8},{10,11... | collective-permute-start | bytes 12296 | tf_op jit(solution)/shard_map/ppermute | solution.py:412
  95.2 4.5 %collective-permute-start.34 = (f32[8,128]{1,0:T(8,128)S(1)}, f32[8,128]{1,0:T(8,128)S(1)}, u32[]{:S(2)}, u32[]{:S(2)}) collective-permute-start(f32[8,128]{1,0:T(8,128)S(1)} %add.66), channel_id=1, source_target_pairs={{0,16},{2,18},{4,20},{6,22},{8,24},{10,26},{12,28},{14,30},{16,0},... | collective-permute-start | bytes 12296 | tf_op jit(solution)/shard_map/ppermute | solution.py:408

commit v6 on v5

--- a/solution.py
+++ b/solution.py
@@ -377,8 +377,8 @@
 
 
 def finish_kernel(unit, images, moments_ref, *refs):
-    far, own = refs[:images], refs[images:-2]
-    out_ref, placed = refs[-2:]
+    far, own = refs[:images], refs[images:-4]
+    out_ref, placed, joined, sems = refs[-4:]
     member, cube, _ = place()
     lower = cube == 0
     moments = jnp.sum(moments_ref[...], 1, keepdims=True)
@@ -390,6 +390,7 @@
         rows = units(other) * unit
         own_rows = own[EARLY.index(other)][...] if other in EARLY else far[other][8 + rows :, :]
         placed[member ^ other, 0:rows, :] = own_factor * own_rows + far_factor * far[other][8 : 8 + rows, :]
+    copies = []
     for slot in range(images + 1):
         kind = (member + slot) & (images - 1)
         part = kind >> 1
@@ -397,10 +398,15 @@
             part == member >> 1, 0 if slot == 0 else 2 if slot == images else 1, kind & 1
         )
         rows = pl.ds(pl.multiple_of(at * unit, unit), unit)
+        mine = slice(slot * unit, (slot + 1) * unit)
         for half in range(2):
-            out_ref[slot * unit : (slot + 1) * unit, half * filters : (half + 1) * filters] = placed[
-                2 * part + half, rows, :
-            ]
+            joined[mine, half * filters : (half + 1) * filters] = placed[2 * part + half, rows, :]
+        if slot % 3 == 2:
+            mine = slice((slot - 2) * unit, (slot + 1) * unit)
+            copies.append(pltpu.make_async_copy(joined.at[mine], out_ref.at[mine], sems.at[slot // 3]))
+            copies[-1].start()
+    for copy in copies:
+        copy.wait()
 
 
 def exchange(x, other):
@@ -554,9 +560,13 @@
     weight_grad = pl.pallas_call(
         functools.partial(finish_kernel, unit, images),
         in_specs=[VMEM] * (1 + images + len(EARLY)),
-        out_specs=VMEM,
+        out_specs=pl.BlockSpec(memory_space=pl.ANY),
         out_shape=f32(taps * unit, filters),
-        scratch_shapes=[pltpu.VMEM((images, 3 * unit, lanes), jnp.float32)],
+        scratch_shapes=[
+            pltpu.VMEM((images, 3 * unit, lanes), jnp.float32),
+            pltpu.VMEM((taps * unit, filters), jnp.float32),
+            pltpu.SemaphoreType.DMA((3,)),
+        ],
         compiler_params=params(24),
         cost_estimate=small,
         name="finish",

time: 101 us -> 101 us (level)
  no operation moved by 1% of the time
where the time goes in v6:
time: 101 us
  starting transfers between devices  34.8 us (34%)
  waiting for transfers between devices  34.8 us (34%)
  Pallas kernels  27 us (27%)
  local copies, waits for them, and re-layouts  2.07 us (2%)
  other arithmetic  1.07 us (1%)
    ppermute x24, starting transfers between devices, exchange(): return lax.ppermute(x, 'dp', [(i, i ^ other) for i in range(size)])  33.2 us
    ppermute x24, waiting for transfers between devices, exchange(): return lax.ppermute(x, 'dp', [(i, i ^ other) for i in range(size)])  30.2 us
    pallas_call x1, Pallas kernels, local_cube(): pl.pallas_call(functools.partial(image_kernel, extent), grid=(taps,), in_...  12.7 us
    pallas_call x4, Pallas kernels, local_cube(): pl.pallas_call(functools.partial(leaf_kernel, extent, images, known, batc...  11.2 us
    ppermute x12, waiting for transfers between devices, swap_cores(): return lax.ppermute(x, 'mp', [(0, 1), (1, 0)])  4.61 us
  transfers between devices with their start and end apart: 36, of which 20 were waited for; matrix products, arithmetic and copies ran while one was open for 1% of the time, Pallas kernels for 24%

profile of v6, /device:TPU:0, one launch (start us, length us, event | category | flops | bytes accessed | tf_op | source)
XLA Modules:
  0.0 100.7 jit_solution(11497075051750596927)
XLA Ops:
  0.6 1.0 %copy-done = f32[1,16,16,512]{3,2,1,0:T(8,128)S(1)} copy-done((f32[1,16,16,512]{3,2,1,0:T(8,128)S(1)}, f32[1,16,16,512]{3,2,1,0:T(8,128)}, u32[]{:S(2)}) %copy-start) | copy-done | bytes 524312
  1.7 0.9 copy-done.2
  3.0 3.0 %collective-permute-start.5 = (f32[2,256,128]{2,1,0:T(8,128)S(1)}, f32[2,256,128]{2,1,0:T(8,128)S(1)}, u32[]{:S(2)}, u32[]{:S(2)}) collective-permute-start(f32[2,256,128]{2,1,0:T(8,128)S(1)} %get-tuple-element.76), channel_id=1, source_target_pairs={{0,2},{2,0},{4,6},{6,4},{8,10},{10,8},{12,14},{14,12},{16,18},{18,... | collective-permute-start | bytes 786440 | tf_op jit(solution)/shard_map/ppermute | solution.py:414
  6.0 2.5 %collective-permute-start.6 = (f32[2,256,128]{2,1,0:T(8,128)S(1)}, f32[2,256,128]{2,1,0:T(8,128)S(1)}, u32[]{:S(2)}, u32[]{:S(2)}) collective-permute-start(f32[2,256,128]{2,1,0:T(8,128)S(1)} %get-tuple-element.77), channel_id=1, source_target_pairs={{0,12},{2,14},{4,8},{6,10},{8,4},{10,6},{12,0},{14,2},{16,28},{18,... | collective-permute-start | bytes 786440 | tf_op jit(solution)/shard_map/ppermute | solution.py:414
  8.6 0.6 collective-permute-start.3
  9.2 3.1 %collective-permute-done.5.refs_1_ = f32[2,256,128]{2,1,0:T(8,128)S(1)} collective-permute-done((f32[2,256,128]{2,1,0:T(8,128)S(1)}, f32[2,256,128]{2,1,0:T(8,128)S(1)}, u32[]{:S(2)}, u32[]{:S(2)}) %collective-permute-start.5) | collective-permute-done | bytes 262176 | tf_op jit(solution)/shard_map/ppermute | solution.py:414
  12.4 3.7 %collective-permute-done.6.refs_2_ = f32[2,256,128]{2,1,0:T(8,128)S(1)} collective-permute-done((f32[2,256,128]{2,1,0:T(8,128)S(1)}, f32[2,256,128]{2,1,0:T(8,128)S(1)}, u32[]{:S(2)}, u32[]{:S(2)}) %collective-permute-start.6) | collective-permute-done | bytes 262176 | tf_op jit(solution)/shard_map/ppermute | solution.py:414
  16.2 1.6 %collective-permute-start.1 = (f32[2,256,128]{2,1,0:T(8,128)S(1)}, f32[2,256,128]{2,1,0:T(8,128)S(1)}, u32[]{:S(2)}, u32[]{:S(2)}) collective-permute-start(f32[2,256,128]{2,1,0:T(8,128)S(1)} %get-tuple-element.71), channel_id=1, source_target_pairs={{0,6},{2,4},{4,2},{6,0},{8,14},{10,12},{12,10},{14,8},{16,22},{18,... | collective-permute-start | bytes 786440 | tf_op jit(solution)/shard_map/ppermute | solution.py:414
  17.8 1.6 %collective-permute-start.2 = (f32[2,256,128]{2,1,0:T(8,128)S(1)}, f32[2,256,128]{2,1,0:T(8,128)S(1)}, u32[]{:S(2)}, u32[]{:S(2)}) collective-permute-start(f32[2,256,128]{2,1,0:T(8,128)S(1)} %get-tuple-element.72), channel_id=1, source_target_pairs={{0,8},{2,10},{4,12},{6,14},{8,0},{10,2},{12,4},{14,6},{16,24},{18,... | collective-permute-start | bytes 786440 | tf_op jit(solution)/shard_map/ppermute | solution.py:414
  19.4 3.1 %leaf.4 = (f32[8,2304,128]{2,1,0:T(8,128)S(1)}, f32[64,128]{1,0:T(8,128)S(1)}) custom-call(f32[2,256,128]{2,1,0:T(8,128)S(1)} %get-tuple-element.75.refs_0_, f32[2,256,128]{2,1,0:T(8,128)S(1)} %collective-permute-done.5.refs_1_, f32[2,256,128]{2,1,0:T(8,128)S(1)} %collective-permute-done.6.refs_2_, f32[256,128]{1,0:T(8,128)S(1)} %collective-permute-done.7.refs_3_, ...), custom_call_target="tpu_custom_call" | custom-call | flops 1 | bytes 1 | tf_op jit(solution)/shard_map/leaf/pallas_call | solution.py:483
  22.6 0.6 collective-permute-start.11
  23.2 1.3 %collective-permute-start = (f32[2,256,128]{2,1,0:T(8,128)S(1)}, f32[2,256,128]{2,1,0:T(8,128)S(1)}, u32[]{:S(2)}, u32[]{:S(2)}) collective-permute-start(f32[2,256,128]{2,1,0:T(8,128)S(1)} %get-tuple-element.70), channel_id=1, source_target_pairs={{0,14},{2,12},{4,10},{6,8},{8,6},{10,4},{12,2},{14,0},{16,30},{18,... | collective-permute-start | bytes 786440 | tf_op jit(solution)/shard_map/ppermute | solution.py:414
  24.4 2.7 %leaf.5 = (f32[8,2304,128]{2,1,0:T(8,128)S(1)}, f32[64,128]{1,0:T(8,128)S(1)}) custom-call(f32[2,256,128]{2,1,0:T(8,128)S(1)} %collective-permute-done.3.refs_0_, f32[2,256,128]{2,1,0:T(8,128)S(1)} %collective-permute-done.4.refs_1_, f32[256,128]{1,0:T(8,128)S(1)} %collective-permute-done.10.refs_2_, ...), custom_call_target="tpu_custom_call", output_to_operand_aliasing={{0}: (5, {})} | custom-call | flops 1 | bytes 1 | tf_op jit(solution)/shard_map/leaf/pallas_call | solution.py:483
  27.9 0.7 collective-permute-done.12.refs_2_
  28.8 3.2 %leaf.6 = (f32[8,2304,128]{2,1,0:T(8,128)S(1)}, f32[64,128]{1,0:T(8,128)S(1)}) custom-call(f32[2,256,128]{2,1,0:T(8,128)S(1)} %collective-permute-done.1.refs_0_, f32[2,256,128]{2,1,0:T(8,128)S(1)} %collective-permute-done.2.refs_1_, f32[256,128]{1,0:T(8,128)S(1)} %collective-permute-done.12.refs_2_, ...), custom_call_target="tpu_custom_call", output_to_operand_aliasing={{0}: (5, {})} | custom-call | flops 1 | bytes 1 | tf_op jit(solution)/shard_map/leaf/pallas_call | solution.py:483
  32.1 1.2 %collective-permute-done.refs_0_ = f32[2,256,128]{2,1,0:T(8,128)S(1)} collective-permute-done((f32[2,256,128]{2,1,0:T(8,128)S(1)}, f32[2,256,128]{2,1,0:T(8,128)S(1)}, u32[]{:S(2)}, u32[]{:S(2)}) %collective-permute-start) | collective-permute-done | bytes 262176 | tf_op jit(solution)/shard_map/ppermute | solution.py:414
  33.3 1.3 %collective-permute-done.14.refs_1_ = f32[256,128]{1,0:T(8,128)S(1)} collective-permute-done((f32[256,128]{1,0:T(8,128)S(1)}, f32[256,128]{1,0:T(8,128)S(1)}, u32[]{:S(2)}, u32[]{:S(2)}) %collective-permute-start.14) | collective-permute-done | bytes 131104 | tf_op jit(solution)/shard_map/ppermute | solution.py:418
  34.7 2.3 %leaf.7 = (f32[8,2304,128]{2,1,0:T(8,128)S(1)}, f32[40,128]{1,0:T(8,128)S(1)}) custom-call(f32[2,256,128]{2,1,0:T(8,128)S(1)} %collective-permute-done.refs_0_, f32[256,128]{1,0:T(8,128)S(1)} %collective-permute-done.14.refs_1_, f32[64,128]{1,0:T(8,128)S(1)} %get-tuple-element.90.refs_2_, ...), custom_call_target="tpu_custom_call", output_to_operand_aliasing={{0}: (3, {})} | custom-call | flops 1 | bytes 1 | tf_op jit(solution)/shard_map/leaf/pallas_call | solution.py:483
  36.9 1.6 %collective-permute-start.15 = (f32[40,128]{1,0:T(8,128)S(1)}, f32[40,128]{1,0:T(8,128)S(1)}, u32[]{:S(2)}, u32[]{:S(2)}) collective-permute-start(f32[40,128]{1,0:T(8,128)S(1)} %get-tuple-element.92), channel_id=1, source_target_pairs={{0,2},{2,0},{4,6},{6,4},{8,10},{10,8},{12,14},{14,12},{16,18},{18,... | collective-permute-start | bytes 61448 | tf_op jit(solution)/shard_map/ppermute | solution.py:414
  39.0 1.5 %collective-permute-start.17 = (f32[40,128]{1,0:T(8,128)S(1)}, f32[40,128]{1,0:T(8,128)S(1)}, u32[]{:S(2)}, u32[]{:S(2)}) collective-permute-start(f32[40,128]{1,0:T(8,128)S(1)} %get-tuple-element.92), channel_id=1, source_target_pairs={{0,6},{2,4},{4,2},{6,0},{8,14},{10,12},{12,10},{14,8},{16,22},{18,... | collective-permute-start | bytes 61448 | tf_op jit(solution)/shard_map/ppermute | solution.py:414
  40.8 1.7 %collective-permute-done.16 = f32[40,128]{1,0:T(8,128)S(1)} collective-permute-done((f32[40,128]{1,0:T(8,128)S(1)}, f32[40,128]{1,0:T(8,128)S(1)}, u32[]{:S(2)}, u32[]{:S(2)}) %collective-permute-start.16) | collective-permute-done | bytes 20512 | tf_op jit(solution)/shard_map/ppermute | solution.py:414
  42.5 1.2 %collective-permute-done.17 = f32[40,128]{1,0:T(8,128)S(1)} collective-permute-done((f32[40,128]{1,0:T(8,128)S(1)}, f32[40,128]{1,0:T(8,128)S(1)}, u32[]{:S(2)}, u32[]{:S(2)}) %collective-permute-start.17) | collective-permute-done | bytes 20512 | tf_op jit(solution)/shard_map/ppermute | solution.py:414
  43.7 1.1 %collective-permute-start.18 = (f32[40,128]{1,0:T(8,128)S(1)}, f32[40,128]{1,0:T(8,128)S(1)}, u32[]{:S(2)}, u32[]{:S(2)}) collective-permute-start(f32[40,128]{1,0:T(8,128)S(1)} %add_add_fusion), channel_id=1, source_target_pairs={{0,8},{2,10},{4,12},{6,14},{8,0},{10,2},{12,4},{14,6},{16,24},{18,... | collective-permute-start | bytes 61448 | tf_op jit(solution)/shard_map/ppermute | solution.py:414
  44.8 2.7 %collective-permute-done.18 = f32[40,128]{1,0:T(8,128)S(1)} collective-permute-done((f32[40,128]{1,0:T(8,128)S(1)}, f32[40,128]{1,0:T(8,128)S(1)}, u32[]{:S(2)}, u32[]{:S(2)}) %collective-permute-start.18) | collective-permute-done | bytes 20512 | tf_op jit(solution)/shard_map/ppermute | solution.py:414
  47.5 1.2 %collective-permute-done.19 = f32[40,128]{1,0:T(8,128)S(1)} collective-permute-done((f32[40,128]{1,0:T(8,128)S(1)}, f32[40,128]{1,0:T(8,128)S(1)}, u32[]{:S(2)}, u32[]{:S(2)}) %collective-permute-start.19) | collective-permute-done | bytes 20512 | tf_op jit(solution)/shard_map/ppermute | solution.py:418
  48.7 1.5 %combine.1 = (f32[1152,128]{1,0:T(8,128)S(1)}, f32[1152,128]{1,0:T(8,128)S(1)}, f32[192,128]{1,0:T(8,128)S(1)}, f32[128,128]{1,0:T(8,128)S(1)}, f32[128,128]{1,0:T(8,128)S(1)}, /*index=5*/f32[128,128]{1,0:T(8,128)S(1)}) custom-call(f32[40,128]{1,0:T(8,128)S(1)} %add.58.gram_ref, f32[8,2304,128]{2,1,0:T(8,128)S(1)} %get-tuple-element.95.leaf_ref), custom_call_target="tpu_custom_call" | custom-call | flops 1 | bytes 1 | tf_op jit(solution)/shard_map/combine/pallas_call | solution.py:505
  50.3 2.7 %collective-permute-start.21 = (f32[1152,128]{1,0:T(8,128)S(1)}, f32[1152,128]{1,0:T(8,128)S(1)}, u32[]{:S(2)}, u32[]{:S(2)}) collective-permute-start(f32[1152,128]{1,0:T(8,128)S(1)} %get-tuple-element.96), channel_id=1, source_target_pairs={{0,16},{2,18},{4,20},{6,22},{8,24},{10,26},{12,28},{14,30},{16,0},... | collective-permute-start | bytes 1769480 | tf_op jit(solution)/shard_map/ppermute | solution.py:414
  52.9 1.0 collective-permute-start.22
  53.9 2.0 %collective-permute-start.23 = (f32[128,128]{1,0:T(8,128)S(1)}, f32[128,128]{1,0:T(8,128)S(1)}, u32[]{:S(2)}, u32[]{:S(2)}) collective-permute-start(f32[128,128]{1,0:T(8,128)S(1)} %get-tuple-element.98), channel_id=1, source_target_pairs={{0,6},{2,4},{4,2},{6,0},{8,14},{10,12},{12,10},{14,8},{16,22},{18,... | collective-permute-start | bytes 196616 | tf_op jit(solution)/shard_map/ppermute | solution.py:414
  55.9 1.0 collective-permute-start.24
  56.9 1.4 %collective-permute-start.25 = (f32[128,128]{1,0:T(8,128)S(1)}, f32[128,128]{1,0:T(8,128)S(1)}, u32[]{:S(2)}, u32[]{:S(2)}) collective-permute-start(f32[128,128]{1,0:T(8,128)S(1)} %get-tuple-element.100), channel_id=1, source_target_pairs={{0,12},{2,14},{4,8},{6,10},{8,4},{10,6},{12,0},{14,2},{16,28},{18,... | collective-permute-start | bytes 196616 | tf_op jit(solution)/shard_map/ppermute | solution.py:414
  58.3 12.7 %image.1 = (f32[256,256]{1,0:T(8,128)}, f32[256,512]{1,0:T(8,128)S(1)}, f32[256,512]{1,0:T(8,128)S(1)}) custom-call(f32[256,512]{1,0:T(8,128)S(1)} %get-tuple-element.101.mine_ref, f32[256,512]{1,0:T(8,128)S(1)} %collective-permute-done.20.theirs_ref, f32[256,256]{1,0:T(8,128)S(1)} %bitcast.25, f32[9,256,1024]{2,1,0:T(8,128)} %bitcast.28), custom_call_target="tpu_custom_call" | custom-call | flops 10000000000 | bytes 1 | tf_op jit(solution)/shard_map/image/pallas_call | solution.py:518
  71.0 8.3 %collective-permute-done.21.far_ref = f32[1152,128]{1,0:T(8,128)S(1)} collective-permute-done((f32[1152,128]{1,0:T(8,128)S(1)}, f32[1152,128]{1,0:T(8,128)S(1)}, u32[]{:S(2)}, u32[]{:S(2)}) %collective-permute-start.21) | collective-permute-done | bytes 589856 | tf_op jit(solution)/shard_map/ppermute | solution.py:414
  79.5 1.5 %collective-permute-start.26 = (f32[264,128]{1,0:T(8,128)S(1)}, f32[264,128]{1,0:T(8,128)S(1)}, u32[]{:S(2)}, u32[]{:S(2)}) collective-permute-start(f32[264,128]{1,0:T(8,128)S(1)} %get-tuple-element.108), channel_id=1, source_target_pairs={{0,4},{2,6},{4,0},{6,2},{8,12},{10,14},{12,8},{14,10},{16,20},{18,... | collective-permute-start | bytes 405512 | tf_op jit(solution)/shard_map/ppermute | solution.py:414
  81.0 0.9 collective-permute-start.28
  81.8 2.7 %collective-permute-start.29 = (f32[264,128]{1,0:T(8,128)S(1)}, f32[264,128]{1,0:T(8,128)S(1)}, u32[]{:S(2)}, u32[]{:S(2)}) collective-permute-start(f32[264,128]{1,0:T(8,128)S(1)} %get-tuple-element.117), channel_id=1, source_target_pairs={{0,14},{2,12},{4,10},{6,8},{8,6},{10,4},{12,2},{14,0},{16,30},{18,... | collective-permute-start | bytes 405512 | tf_op jit(solution)/shard_map/ppermute | solution.py:414
  84.8 0.7 collective-permute-start.30
  85.4 1.9 %collective-permute-done.27.refs_4_ = f32[264,128]{1,0:T(8,128)S(1)} collective-permute-done((f32[264,128]{1,0:T(8,128)S(1)}, f32[264,128]{1,0:T(8,128)S(1)}, u32[]{:S(2)}, u32[]{:S(2)}) %collective-permute-start.27) | collective-permute-done | bytes 135200 | tf_op jit(solution)/shard_map/ppermute | solution.py:414
  87.6 1.6 %collective-permute-start.32 = (f32[136,128]{1,0:T(8,128)S(1)}, f32[136,128]{1,0:T(8,128)S(1)}, u32[]{:S(2)}, u32[]{:S(2)}) collective-permute-start(f32[136,128]{1,0:T(8,128)S(1)} %get-tuple-element.126), channel_id=1, source_target_pairs={{0,6},{2,4},{4,2},{6,0},{8,14},{10,12},{12,10},{14,8},{16,22},{18,... | collective-permute-start | bytes 208904 | tf_op jit(solution)/shard_map/ppermute | solution.py:414
  89.2 2.2 %collective-permute-done.29.refs_7_ = f32[264,128]{1,0:T(8,128)S(1)} collective-permute-done((f32[264,128]{1,0:T(8,128)S(1)}, f32[264,128]{1,0:T(8,128)S(1)}, u32[]{:S(2)}, u32[]{:S(2)}) %collective-permute-start.29) | collective-permute-done | bytes 135200 | tf_op jit(solution)/shard_map/ppermute | solution.py:414
  91.3 1.2 %collective-permute-done.30.refs_6_ = f32[136,128]{1,0:T(8,128)S(1)} collective-permute-done((f32[136,128]{1,0:T(8,128)S(1)}, f32[136,128]{1,0:T(8,128)S(1)}, u32[]{:S(2)}, u32[]{:S(2)}) %collective-permute-start.30) | collective-permute-done | bytes 69664 | tf_op jit(solution)/shard_map/ppermute | solution.py:414
  92.6 0.5 collective-permute-done.31.refs_5_
  93.1 0.9 collective-permute-done.32.refs_3_
  94.0 1.2 %collective-permute-done.33 = f32[8,128]{1,0:T(8,128)S(1)} collective-permute-done((f32[8,128]{1,0:T(8,128)S(1)}, f32[8,128]{1,0:T(8,128)S(1)}, u32[]{:S(2)}, u32[]{:S(2)}) %collective-permute-start.33) | collective-permute-done | bytes 4128 | tf_op jit(solution)/shard_map/ppermute | solution.py:418
  95.2 2.4 %collective-permute-start.34 = (f32[8,128]{1,0:T(8,128)S(1)}, f32[8,128]{1,0:T(8,128)S(1)}, u32[]{:S(2)}, u32[]{:S(2)}) collective-permute-start(f32[8,128]{1,0:T(8,128)S(1)} %add.66), channel_id=1, source_target_pairs={{0,16},{2,18},{4,20},{6,22},{8,24},{10,26},{12,28},{14,30},{16,0},... | collective-permute-start | bytes 12296 | tf_op jit(solution)/shard_map/ppermute | solution.py:414
  97.6 1.0 %fusion.4 = f32[256,512]{1,0:T(8,128)} fusion(f32[256,512]{1,0:T(8,128)S(1)} %get-tuple-element.129, f32[256,512]{1,0:T(8,128)S(1)} %collective-permute-done.35, f32[1,16,16,512]{3,2,1,0:T(8,128)S(1)} %copy-done.1), kind=kLoop, calls=%fused_computation.5 | loop fusion | flops 1310720 | bytes 2097152 | tf_op jit(solution)/shard_map/mul | solution.py:536
  98.6 1.1 %collective-permute-done.34 = f32[8,128]{1,0:T(8,128)S(1)} collective-permute-done((f32[8,128]{1,0:T(8,128)S(1)}, f32[8,128]{1,0:T(8,128)S(1)}, u32[]{:S(2)}, u32[]{:S(2)}) %collective-permute-start.34) | collective-permute-done | bytes 4128 | tf_op jit(solution)/shard_map/ppermute | solution.py:414
  99.7 1.0 %finish.1 = f32[576,256]{1,0:T(8,128)} custom-call(f32[8,128]{1,0:T(8,128)S(1)} %add.67.moments_ref, f32[392,128]{1,0:T(8,128)S(1)} %get-tuple-element.107.refs_0_, f32[200,128]{1,0:T(8,128)S(1)} %collective-permute-done.28.refs_1_, f32[264,128]{1,0:T(8,128)S(1)} %collective-permute-done.26.refs_2_, f32[136,128]{1,0:T(8,128)S(1)} %collective-permute-done.32.refs_3_, ...), custom_call_target="tpu_custom_call" | custom-call | flops 1 | bytes 1 | tf_op jit(solution)/shard_map/finish/pallas_call | solution.py:560
  (63 shorter events, 3.4 us)
Async XLA Ops:
  0.6 1.0 %copy-start = (f32[1,16,16,512]{3,2,1,0:T(8,128)S(1)}, f32[1,16,16,512]{3,2,1,0:T(8,128)}, u32[]{:S(2)}) copy-start(f32[1,16,16,512]{3,2,1,0:T(8,128)} %param.3) | copy-start | bytes 1572868
  1.7 0.9 copy-start.2
  3.0 9.3 %collective-permute-start.5 = (f32[2,256,128]{2,1,0:T(8,128)S(1)}, f32[2,256,128]{2,1,0:T(8,128)S(1)}, u32[]{:S(2)}, u32[]{:S(2)}) collective-permute-start(f32[2,256,128]{2,1,0:T(8,128)S(1)} %get-tuple-element.76), channel_id=1, source_target_pairs={{0,2},{2,0},{4,6},{6,4},{8,10},{10,8},{12,14},{14,12},{16,18},{18,... | collective-permute-start | bytes 786440 | tf_op jit(solution)/shard_map/ppermute | solution.py:414
  6.0 10.1 %collective-permute-start.6 = (f32[2,256,128]{2,1,0:T(8,128)S(1)}, f32[2,256,128]{2,1,0:T(8,128)S(1)}, u32[]{:S(2)}, u32[]{:S(2)}) collective-permute-start(f32[2,256,128]{2,1,0:T(8,128)S(1)} %get-tuple-element.77), channel_id=1, source_target_pairs={{0,12},{2,14},{4,8},{6,10},{8,4},{10,6},{12,0},{14,2},{16,28},{18,... | collective-permute-start | bytes 786440 | tf_op jit(solution)/shard_map/ppermute | solution.py:414
  8.5 7.7 %collective-permute-start.7 = (f32[256,128]{1,0:T(8,128)S(1)}, f32[256,128]{1,0:T(8,128)S(1)}, u32[]{:S(2)}, u32[]{:S(2)}) collective-permute-start(f32[256,128]{1,0:T(8,128)S(1)} %slice_bitcast_fusion.7), channel_id=1, source_target_pairs={{0,1},{1,0},{2,3},{3,2},{4,5},{5,4},{6,7},{7,6},{8,9},{9,8},{10,11... | collective-permute-start | bytes 393224 | tf_op jit(solution)/shard_map/ppermute | solution.py:418
  8.6 13.9 %collective-permute-start.3 = (f32[2,256,128]{2,1,0:T(8,128)S(1)}, f32[2,256,128]{2,1,0:T(8,128)S(1)}, u32[]{:S(2)}, u32[]{:S(2)}) collective-permute-start(f32[2,256,128]{2,1,0:T(8,128)S(1)} %get-tuple-element.73), channel_id=1, source_target_pairs={{0,4},{2,6},{4,0},{6,2},{8,12},{10,14},{12,8},{14,10},{16,20},{18,... | collective-permute-start | bytes 786440 | tf_op jit(solution)/shard_map/ppermute | solution.py:414
  9.2 13.3 %collective-permute-start.4 = (f32[2,256,128]{2,1,0:T(8,128)S(1)}, f32[2,256,128]{2,1,0:T(8,128)S(1)}, u32[]{:S(2)}, u32[]{:S(2)}) collective-permute-start(f32[2,256,128]{2,1,0:T(8,128)S(1)} %get-tuple-element.74), channel_id=1, source_target_pairs={{0,10},{2,8},{4,14},{6,12},{8,2},{10,0},{12,6},{14,4},{16,26},{18,... | collective-permute-start | bytes 786440 | tf_op jit(solution)/shard_map/ppermute | solution.py:414
  12.3 5.5 %collective-permute-start.8 = (f32[256,128]{1,0:T(8,128)S(1)}, f32[256,128]{1,0:T(8,128)S(1)}, u32[]{:S(2)}, u32[]{:S(2)}) collective-permute-start(f32[256,128]{1,0:T(8,128)S(1)} %slice_bitcast_fusion.1), channel_id=1, source_target_pairs={{0,1},{1,0},{2,3},{3,2},{4,5},{5,4},{6,7},{7,6},{8,9},{9,8},{10,11... | collective-permute-start | bytes 393224 | tf_op jit(solution)/shard_map/ppermute | solution.py:418
  16.1 3.3 %collective-permute-start.9 = (f32[256,128]{1,0:T(8,128)S(1)}, f32[256,128]{1,0:T(8,128)S(1)}, u32[]{:S(2)}, u32[]{:S(2)}) collective-permute-start(f32[256,128]{1,0:T(8,128)S(1)} %slice_bitcast_fusion), channel_id=1, source_target_pairs={{0,1},{1,0},{2,3},{3,2},{4,5},{5,4},{6,7},{7,6},{8,9},{9,8},{10,11... | collective-permute-start | bytes 393224 | tf_op jit(solution)/shard_map/ppermute | solution.py:418
  16.2 10.9 %collective-permute-start.1 = (f32[2,256,128]{2,1,0:T(8,128)S(1)}, f32[2,256,128]{2,1,0:T(8,128)S(1)}, u32[]{:S(2)}, u32[]{:S(2)}) collective-permute-start(f32[2,256,128]{2,1,0:T(8,128)S(1)} %get-tuple-element.71), channel_id=1, source_target_pairs={{0,6},{2,4},{4,2},{6,0},{8,14},{10,12},{12,10},{14,8},{16,22},{18,... | collective-permute-start | bytes 786440 | tf_op jit(solution)/shard_map/ppermute | solution.py:414
  17.8 9.4 %collective-permute-start.2 = (f32[2,256,128]{2,1,0:T(8,128)S(1)}, f32[2,256,128]{2,1,0:T(8,128)S(1)}, u32[]{:S(2)}, u32[]{:S(2)}) collective-permute-start(f32[2,256,128]{2,1,0:T(8,128)S(1)} %get-tuple-element.72), channel_id=1, source_target_pairs={{0,8},{2,10},{4,12},{6,14},{8,0},{10,2},{12,4},{14,6},{16,24},{18,... | collective-permute-start | bytes 786440 | tf_op jit(solution)/shard_map/ppermute | solution.py:414
  22.5 1.9 %collective-permute-start.10 = (f32[256,128]{1,0:T(8,128)S(1)}, f32[256,128]{1,0:T(8,128)S(1)}, u32[]{:S(2)}, u32[]{:S(2)}) collective-permute-start(f32[256,128]{1,0:T(8,128)S(1)} %slice_bitcast_fusion.6), channel_id=1, source_target_pairs={{0,1},{1,0},{2,3},{3,2},{4,5},{5,4},{6,7},{7,6},{8,9},{9,8},{10,11... | collective-permute-start | bytes 393224 | tf_op jit(solution)/shard_map/ppermute | solution.py:418
  22.6 1.8 %collective-permute-start.11 = (f32[256,128]{1,0:T(8,128)S(1)}, f32[256,128]{1,0:T(8,128)S(1)}, u32[]{:S(2)}, u32[]{:S(2)}) collective-permute-start(f32[256,128]{1,0:T(8,128)S(1)} %slice_bitcast_fusion.5), channel_id=1, source_target_pairs={{0,1},{1,0},{2,3},{3,2},{4,5},{5,4},{6,7},{7,6},{8,9},{9,8},{10,11... | collective-permute-start | bytes 393224 | tf_op jit(solution)/shard_map/ppermute | solution.py:418
  23.2 10.1 %collective-permute-start = (f32[2,256,128]{2,1,0:T(8,128)S(1)}, f32[2,256,128]{2,1,0:T(8,128)S(1)}, u32[]{:S(2)}, u32[]{:S(2)}) collective-permute-start(f32[2,256,128]{2,1,0:T(8,128)S(1)} %get-tuple-element.70), channel_id=1, source_target_pairs={{0,14},{2,12},{4,10},{6,8},{8,6},{10,4},{12,2},{14,0},{16,30},{18,... | collective-permute-start | bytes 786440 | tf_op jit(solution)/shard_map/ppermute | solution.py:414
  27.2 1.4 %collective-permute-start.12 = (f32[256,128]{1,0:T(8,128)S(1)}, f32[256,128]{1,0:T(8,128)S(1)}, u32[]{:S(2)}, u32[]{:S(2)}) collective-permute-start(f32[256,128]{1,0:T(8,128)S(1)} %slice_bitcast_fusion.4), channel_id=1, source_target_pairs={{0,1},{1,0},{2,3},{3,2},{4,5},{5,4},{6,7},{7,6},{8,9},{9,8},{10,11... | collective-permute-start | bytes 393224 | tf_op jit(solution)/shard_map/ppermute | solution.py:418
  27.4 1.5 %collective-permute-start.13 = (f32[256,128]{1,0:T(8,128)S(1)}, f32[256,128]{1,0:T(8,128)S(1)}, u32[]{:S(2)}, u32[]{:S(2)}) collective-permute-start(f32[256,128]{1,0:T(8,128)S(1)} %slice_bitcast_fusion.3), channel_id=1, source_target_pairs={{0,1},{1,0},{2,3},{3,2},{4,5},{5,4},{6,7},{7,6},{8,9},{9,8},{10,11... | collective-permute-start | bytes 393224 | tf_op jit(solution)/shard_map/ppermute | solution.py:418
  27.9 20.9 %collective-permute-start.20 = (f32[256,512]{1,0:T(8,128)S(1)}, f32[256,512]{1,0:T(8,128)S(1)}, u32[]{:S(2)}, u32[]{:S(2)}) collective-permute-start(f32[256,512]{1,0:T(8,128)S(1)} %get-tuple-element.101.mine_ref), channel_id=1, source_target_pairs={{0,1},{1,0},{2,3},{3,2},{4,5},{5,4},{6,7},{7,6},{8,9},{9,8},{10,11... | collective-permute-start | bytes 1572872 | tf_op jit(solution)/shard_map/ppermute | solution.py:418
  33.3 1.4 %collective-permute-start.14 = (f32[256,128]{1,0:T(8,128)S(1)}, f32[256,128]{1,0:T(8,128)S(1)}, u32[]{:S(2)}, u32[]{:S(2)}) collective-permute-start(f32[256,128]{1,0:T(8,128)S(1)} %slice_bitcast_fusion.2), channel_id=1, source_target_pairs={{0,1},{1,0},{2,3},{3,2},{4,5},{5,4},{6,7},{7,6},{8,9},{9,8},{10,11... | collective-permute-start | bytes 393224 | tf_op jit(solution)/shard_map/ppermute | solution.py:418
  34.7 23.6 %copy-start.3 = (f32[1,16,16,256]{3,2,1,0:T(8,128)S(1)}, f32[1,16,16,256]{3,2,1,0:T(8,128)}, u32[]{:S(2)}) copy-start(f32[1,16,16,256]{3,2,1,0:T(8,128)} %param.5) | copy-start | bytes 786436
  36.9 3.8 %collective-permute-start.15 = (f32[40,128]{1,0:T(8,128)S(1)}, f32[40,128]{1,0:T(8,128)S(1)}, u32[]{:S(2)}, u32[]{:S(2)}) collective-permute-start(f32[40,128]{1,0:T(8,128)S(1)} %get-tuple-element.92), channel_id=1, source_target_pairs={{0,2},{2,0},{4,6},{6,4},{8,10},{10,8},{12,14},{14,12},{16,18},{18,... | collective-permute-start | bytes 61448 | tf_op jit(solution)/shard_map/ppermute | solution.py:414
  38.5 4.0 %collective-permute-start.16 = (f32[40,128]{1,0:T(8,128)S(1)}, f32[40,128]{1,0:T(8,128)S(1)}, u32[]{:S(2)}, u32[]{:S(2)}) collective-permute-start(f32[40,128]{1,0:T(8,128)S(1)} %get-tuple-element.92), channel_id=1, source_target_pairs={{0,4},{2,6},{4,0},{6,2},{8,12},{10,14},{12,8},{14,10},{16,20},{18,... | collective-permute-start | bytes 61448 | tf_op jit(solution)/shard_map/ppermute | solution.py:414
  39.0 4.7 %collective-permute-start.17 = (f32[40,128]{1,0:T(8,128)S(1)}, f32[40,128]{1,0:T(8,128)S(1)}, u32[]{:S(2)}, u32[]{:S(2)}) collective-permute-start(f32[40,128]{1,0:T(8,128)S(1)} %get-tuple-element.92), channel_id=1, source_target_pairs={{0,6},{2,4},{4,2},{6,0},{8,14},{10,12},{12,10},{14,8},{16,22},{18,... | collective-permute-start | bytes 61448 | tf_op jit(solution)/shard_map/ppermute | solution.py:414
  43.7 3.8 %collective-permute-start.18 = (f32[40,128]{1,0:T(8,128)S(1)}, f32[40,128]{1,0:T(8,128)S(1)}, u32[]{:S(2)}, u32[]{:S(2)}) collective-permute-start(f32[40,128]{1,0:T(8,128)S(1)} %add_add_fusion), channel_id=1, source_target_pairs={{0,8},{2,10},{4,12},{6,14},{8,0},{10,2},{12,4},{14,6},{16,24},{18,... | collective-permute-start | bytes 61448 | tf_op jit(solution)/shard_map/ppermute | solution.py:414
  47.5 1.2 %collective-permute-start.19 = (f32[40,128]{1,0:T(8,128)S(1)}, f32[40,128]{1,0:T(8,128)S(1)}, u32[]{:S(2)}, u32[]{:S(2)}) collective-permute-start(f32[40,128]{1,0:T(8,128)S(1)} %add.57), channel_id=1, source_target_pairs={{0,1},{1,0},{2,3},{3,2},{4,5},{5,4},{6,7},{7,6},{8,9},{9,8},{10,11... | collective-permute-start | bytes 61448 | tf_op jit(solution)/shard_map/ppermute | solution.py:418
  50.3 29.0 %collective-permute-start.21 = (f32[1152,128]{1,0:T(8,128)S(1)}, f32[1152,128]{1,0:T(8,128)S(1)}, u32[]{:S(2)}, u32[]{:S(2)}) collective-permute-start(f32[1152,128]{1,0:T(8,128)S(1)} %get-tuple-element.96), channel_id=1, source_target_pairs={{0,16},{2,18},{4,20},{6,22},{8,24},{10,26},{12,28},{14,30},{16,0},... | collective-permute-start | bytes 1769480 | tf_op jit(solution)/shard_map/ppermute | solution.py:414
  52.9 18.1 %collective-permute-start.22 = (f32[192,128]{1,0:T(8,128)S(1)}, f32[192,128]{1,0:T(8,128)S(1)}, u32[]{:S(2)}, u32[]{:S(2)}) collective-permute-start(f32[192,128]{1,0:T(8,128)S(1)} %get-tuple-element.97), channel_id=1, source_target_pairs={{0,2},{2,0},{4,6},{6,4},{8,10},{10,8},{12,14},{14,12},{16,18},{18,... | collective-permute-start | bytes 294920 | tf_op jit(solution)/shard_map/ppermute | solution.py:414
  53.9 17.0 %collective-permute-start.23 = (f32[128,128]{1,0:T(8,128)S(1)}, f32[128,128]{1,0:T(8,128)S(1)}, u32[]{:S(2)}, u32[]{:S(2)}) collective-permute-start(f32[128,128]{1,0:T(8,128)S(1)} %get-tuple-element.98), channel_id=1, source_target_pairs={{0,6},{2,4},{4,2},{6,0},{8,14},{10,12},{12,10},{14,8},{16,22},{18,... | collective-permute-start | bytes 196616 | tf_op jit(solution)/shard_map/ppermute | solution.py:414
  55.9 15.1 %collective-permute-start.24 = (f32[128,128]{1,0:T(8,128)S(1)}, f32[128,128]{1,0:T(8,128)S(1)}, u32[]{:S(2)}, u32[]{:S(2)}) collective-permute-start(f32[128,128]{1,0:T(8,128)S(1)} %get-tuple-element.99), channel_id=1, source_target_pairs={{0,10},{2,8},{4,14},{6,12},{8,2},{10,0},{12,6},{14,4},{16,26},{18,... | collective-permute-start | bytes 196616 | tf_op jit(solution)/shard_map/ppermute | solution.py:414
  56.9 14.1 %collective-permute-start.25 = (f32[128,128]{1,0:T(8,128)S(1)}, f32[128,128]{1,0:T(8,128)S(1)}, u32[]{:S(2)}, u32[]{:S(2)}) collective-permute-start(f32[128,128]{1,0:T(8,128)S(1)} %get-tuple-element.100), channel_id=1, source_target_pairs={{0,12},{2,14},{4,8},{6,10},{8,4},{10,6},{12,0},{14,2},{16,28},{18,... | collective-permute-start | bytes 196616 | tf_op jit(solution)/shard_map/ppermute | solution.py:414
  58.3 39.3 %copy-start.1 = (f32[1,16,16,512]{3,2,1,0:T(8,128)S(1)}, f32[1,16,16,512]{3,2,1,0:T(8,128)}, u32[]{:S(2)}) copy-start(f32[1,16,16,512]{3,2,1,0:T(8,128)} %param.3) | copy-start | bytes 1572868
  79.5 5.3 %collective-permute-start.26 = (f32[264,128]{1,0:T(8,128)S(1)}, f32[264,128]{1,0:T(8,128)S(1)}, u32[]{:S(2)}, u32[]{:S(2)}) collective-permute-start(f32[264,128]{1,0:T(8,128)S(1)} %get-tuple-element.108), channel_id=1, source_target_pairs={{0,4},{2,6},{4,0},{6,2},{8,12},{10,14},{12,8},{14,10},{16,20},{18,... | collective-permute-start | bytes 405512 | tf_op jit(solution)/shard_map/ppermute | solution.py:414
  81.0 16.6 %collective-permute-start.35 = (f32[256,512]{1,0:T(8,128)S(1)}, f32[256,512]{1,0:T(8,128)S(1)}, u32[]{:S(2)}, u32[]{:S(2)}) collective-permute-start(f32[256,512]{1,0:T(8,128)S(1)} %get-tuple-element.130), channel_id=1, source_target_pairs={{0,1},{1,0},{2,3},{3,2},{4,5},{5,4},{6,7},{7,6},{8,9},{9,8},{10,11... | collective-permute-start | bytes 1572872 | tf_op jit(solution)/shard_map/ppermute | solution.py:418
  81.0 6.4 %collective-permute-start.27 = (f32[264,128]{1,0:T(8,128)S(1)}, f32[264,128]{1,0:T(8,128)S(1)}, u32[]{:S(2)}, u32[]{:S(2)}) collective-permute-start(f32[264,128]{1,0:T(8,128)S(1)} %get-tuple-element.111), channel_id=1, source_target_pairs={{0,8},{2,10},{4,12},{6,14},{8,0},{10,2},{12,4},{14,6},{16,24},{18,... | collective-permute-start | bytes 405512 | tf_op jit(solution)/shard_map/ppermute | solution.py:414
  81.0 6.6 %collective-permute-start.28 = (f32[200,128]{1,0:T(8,128)S(1)}, f32[200,128]{1,0:T(8,128)S(1)}, u32[]{:S(2)}, u32[]{:S(2)}) collective-permute-start(f32[200,128]{1,0:T(8,128)S(1)} %get-tuple-element.114), channel_id=1, source_target_pairs={{0,2},{2,0},{4,6},{6,4},{8,10},{10,8},{12,14},{14,12},{16,18},{18,... | collective-permute-start | bytes 307208 | tf_op jit(solution)/shard_map/ppermute | solution.py:414
  81.8 9.5 %collective-permute-start.29 = (f32[264,128]{1,0:T(8,128)S(1)}, f32[264,128]{1,0:T(8,128)S(1)}, u32[]{:S(2)}, u32[]{:S(2)}) collective-permute-start(f32[264,128]{1,0:T(8,128)S(1)} %get-tuple-element.117), channel_id=1, source_target_pairs={{0,14},{2,12},{4,10},{6,8},{8,6},{10,4},{12,2},{14,0},{16,30},{18,... | collective-permute-start | bytes 405512 | tf_op jit(solution)/shard_map/ppermute | solution.py:414
  84.8 7.8 %collective-permute-start.30 = (f32[136,128]{1,0:T(8,128)S(1)}, f32[136,128]{1,0:T(8,128)S(1)}, u32[]{:S(2)}, u32[]{:S(2)}) collective-permute-start(f32[136,128]{1,0:T(8,128)S(1)} %get-tuple-element.120), channel_id=1, source_target_pairs={{0,12},{2,14},{4,8},{6,10},{8,4},{10,6},{12,0},{14,2},{16,28},{18,... | collective-permute-start | bytes 208904 | tf_op jit(solution)/shard_map/ppermute | solution.py:414
  87.4 5.8 %collective-permute-start.31 = (f32[136,128]{1,0:T(8,128)S(1)}, f32[136,128]{1,0:T(8,128)S(1)}, u32[]{:S(2)}, u32[]{:S(2)}) collective-permute-start(f32[136,128]{1,0:T(8,128)S(1)} %get-tuple-element.123), channel_id=1, source_target_pairs={{0,10},{2,8},{4,14},{6,12},{8,2},{10,0},{12,6},{14,4},{16,26},{18,... | collective-permute-start | bytes 208904 | tf_op jit(solution)/shard_map/ppermute | solution.py:414
  87.6 6.4 %collective-permute-start.32 = (f32[136,128]{1,0:T(8,128)S(1)}, f32[136,128]{1,0:T(8,128)S(1)}, u32[]{:S(2)}, u32[]{:S(2)}) collective-permute-start(f32[136,128]{1,0:T(8,128)S(1)} %get-tuple-element.126), channel_id=1, source_target_pairs={{0,6},{2,4},{4,2},{6,0},{8,14},{10,12},{12,10},{14,8},{16,22},{18,... | collective-permute-start | bytes 208904 | tf_op jit(solution)/shard_map/ppermute | solution.py:414
  94.0 1.2 %collective-permute-start.33 = (f32[8,128]{1,0:T(8,128)S(1)}, f32[8,128]{1,0:T(8,128)S(1)}, u32[]{:S(2)}, u32[]{:S(2)}) collective-permute-start(f32[8,128]{1,0:T(8,128)S(1)} %slice_add_fusion), channel_id=1, source_target_pairs={{0,1},{1,0},{2,3},{3,2},{4,5},{5,4},{6,7},{7,6},{8,9},{9,8},{10,11... | collective-permute-start | bytes 12296 | tf_op jit(solution)/shard_map/ppermute | solution.py:418
  95.2 4.5 %collective-permute-start.34 = (f32[8,128]{1,0:T(8,128)S(1)}, f32[8,128]{1,0:T(8,128)S(1)}, u32[]{:S(2)}, u32[]{:S(2)}) collective-permute-start(f32[8,128]{1,0:T(8,128)S(1)} %add.66), channel_id=1, source_target_pairs={{0,16},{2,18},{4,20},{6,22},{8,24},{10,26},{12,28},{14,30},{16,0},... | collective-permute-start | bytes 12296 | tf_op jit(solution)/shard_map/ppermute | solution.py:414
